TPU v7x, 32 devices: a whole 2x2x4 slice. The times are simulated.
32 devices in a mesh: shard: 4 (over x, core), ctx: 2 (over y), tensor: 4 (over z).
Axes of the slice: x: 2, y: 2, z: 4, core: 2. Of those that a mesh axis runs over, the one named last changes fastest.
Arguments:
- image_rows: bfloat16 [4, 2048, 1536], P('shard', 'ctx'), may hold values from -6 to 6
- text_input_rows: bfloat16 [4, 154, 1536], P('shard', 'ctx'), may hold values from -6 to 6
- condition: float32 [2, 1536], replicated, may hold values from -6 to 6
- slot_table: int32 [4], P('shard'), may hold values from -1 to 1, as said below
- weights: float32 [2, 1536, 18, 1536], P(None, ('shard', 'ctx'), None, 'tensor'), may hold values from -4 to 4
- weight_mom_one: float32 [2, 1536, 18, 1536], P(None, ('shard', 'ctx'), None, 'tensor'), may hold values from -0.00030517578 to 0.00030517578
- weight_mom_two: float32 [2, 1536, 18, 1536], P(None, ('shard', 'ctx'), None, 'tensor'), may hold values from 5.3e-10 to 2.1e-09
- biases: float32 [2, 14, 1536], replicated, may hold values from -1.5 to 1.5
- bias_mom_one: float32 [2, 14, 1536], replicated, may hold values from -0.00030517578 to 0.00030517578
- bias_mom_two: float32 [2, 14, 1536], replicated, may hold values from 5.3e-10 to 2.1e-09
- image_output_cotangent: bfloat16 [4, 2048, 1536], P('shard', 'ctx'), may hold values from -6 to 6
- text_output_cotangent: bfloat16 [4, 154, 1536], P('shard', 'ctx'), may hold values from -6 to 6
Outputs:
- image_out: bfloat16 [4, 2048, 1536], P('shard', 'ctx')
- text_out: bfloat16 [4, 154, 1536], P('shard', 'ctx')
- image_grad: bfloat16 [4, 2048, 1536], P('shard', 'ctx')
- text_grad: bfloat16 [4, 154, 1536], P('shard', 'ctx')
- condition_grad: float32 [2, 1536], replicated
- weight_grad: float32 [2, 1536, 18, 1536], P(None, ('shard', 'ctx'), None, 'tensor')
- weight_new: float32 [2, 1536, 18, 1536], P(None, ('shard', 'ctx'), None, 'tensor')
- weight_mom_one_new: float32 [2, 1536, 18, 1536], P(None, ('shard', 'ctx'), None, 'tensor')
- weight_mom_two_new: float32 [2, 1536, 18, 1536], P(None, ('shard', 'ctx'), None, 'tensor')
- bias_grad: float32 [2, 14, 1536], replicated
- bias_new: float32 [2, 14, 1536], replicated
- bias_mom_one_new: float32 [2, 14, 1536], replicated
- bias_mom_two_new: float32 [2, 14, 1536], replicated
Inputs may be any that keep to these rules, and one draw needn't show every extreme that they name: `slot_table`: each of the 2 sequences stands in exactly one slot, the other slots hold -1. Slot n belongs to shard group n; slots 0 and 2 are always filled.
All inputs are finite; a program needn't handle non-finite values.
Results may differ from a plain program's by a relative error of at most 0.024.
Values may be sent and summed in bfloat16 or wider, within the bound.
No kernel may reach another device: no remote copies, remote signals or barrier semaphores. Data moves between devices by JAX's collectives and lax.ppermute only.
A program may use at most 640 MiB of HBM per device.

v0:
```python
import jax
import jax.numpy as jnp
from jax import lax
from jax.sharding import PartitionSpec as P

MODEL_WIDTH = 1536
DH = 64


beta_one = 0.9
beta_two = 0.95
learn_rate = 0.1
decay_rate = 0.1
adam_eps = 1e-08
adam_step = 10.0
norm_eps = 1e-06
gelu_coef = 0.044715
root_two_pi = 0.7978845608028654
clip_unit = 0.0001
clip_eps = 1e-12


def layer_norm(drawn_values):
    center = drawn_values - jnp.mean(drawn_values, axis=-1, keepdims=True)
    inverse = lax.rsqrt(jnp.mean(center * center, axis=-1, keepdims=True) + norm_eps)
    return (center * inverse, inverse)


def norm_back(normed, inverse, upstream):
    mean_grad = jnp.mean(upstream, axis=-1, keepdims=True)
    mean_dot = jnp.mean(upstream * normed, axis=-1, keepdims=True)
    return inverse * (upstream - mean_grad - normed * mean_dot)


def gelu_parts(preact):
    inner = root_two_pi * (preact + gelu_coef * preact * preact * preact)
    tanh_value = jnp.tanh(inner)
    value_out = 0.5 * preact * (1.0 + tanh_value)
    slope_out = 0.5 * (1.0 + tanh_value) + 0.5 * preact * (
        1.0 - tanh_value * tanh_value
    ) * root_two_pi * (1.0 + 3.0 * gelu_coef * preact * preact)
    return (value_out, slope_out)


def silu_slope(drawn_values):
    sigmoid_val = jax.nn.sigmoid(drawn_values)
    return sigmoid_val * (1.0 + drawn_values * (1.0 - sigmoid_val))


def adam_update(parameter, moment_one, moment_two, gradient, decay_factor):
    new_one = beta_one * moment_one + (1.0 - beta_one) * gradient
    new_two = beta_two * moment_two + (1.0 - beta_two) * gradient * gradient
    first_hat = new_one / (1.0 - beta_one**adam_step)
    second_hat = new_two / (1.0 - beta_two**adam_step)
    new_param = parameter - learn_rate * (
        first_hat / (jnp.sqrt(second_hat) + adam_eps) + decay_factor * parameter
    )
    return (new_param, new_one, new_two)


def heads_first(drawn_values):
    return jnp.moveaxis(drawn_values, 1, 0)


def heads_back(drawn_values):
    return jnp.moveaxis(drawn_values, 0, 1)


def fold_block(carry_state, queries, key_block, value_block, score_scale):
    accumulated, run_max, run_sum = carry_state

    def fold_one_head(packed):
        acc_h, max_h, sum_h, query_h, key_h, value_h = packed
        scores = jnp.dot(query_h, key_h.T, preferred_element_type=jnp.float32) * score_scale
        new_max = jnp.maximum(max_h, jnp.max(scores, axis=1))
        shifted = jnp.exp(scores - new_max[:, None])
        factor = jnp.exp(max_h - new_max)
        new_sum = sum_h * factor + jnp.sum(shifted, axis=1)
        added = jnp.dot(shifted.astype(jnp.bfloat16), value_h, preferred_element_type=jnp.float32)
        return (acc_h * factor[:, None] + added, new_max, new_sum)

    new_acc, new_max, new_sum = lax.map(
        fold_one_head,
        (
            heads_first(accumulated),
            run_max,
            run_sum,
            heads_first(queries),
            heads_first(key_block),
            heads_first(value_block),
        ),
    )
    return (heads_back(new_acc), new_max, new_sum)


def attend_back(queries, key_block, value_block, attn_heads, grad_heads, log_sum, score_scale):

    def attend_one_head(packed):
        query_h, key_h, value_h, attn_h, grad_h, lse_h = packed
        scores = jnp.dot(query_h, key_h.T, preferred_element_type=jnp.float32) * score_scale
        soft = jnp.exp(scores - lse_h[:, None])
        row_delta = jnp.sum(grad_h.astype(jnp.float32) * attn_h.astype(jnp.float32), axis=1)
        grad_value = jnp.dot(
            soft.astype(jnp.bfloat16).T, grad_h, preferred_element_type=jnp.float32
        )
        grad_soft = jnp.dot(grad_h, value_h.T, preferred_element_type=jnp.float32)
        grad_score = (soft * (grad_soft - row_delta[:, None]) * score_scale).astype(jnp.bfloat16)
        grad_query = jnp.dot(grad_score, key_h, preferred_element_type=jnp.float32)
        grad_key = jnp.dot(grad_score.T, query_h, preferred_element_type=jnp.float32)
        return (grad_query, grad_key, grad_value)

    grad_query, grad_key, grad_value = lax.map(
        attend_one_head,
        (
            heads_first(queries),
            heads_first(key_block),
            heads_first(value_block),
            heads_first(attn_heads),
            heads_first(grad_heads),
            log_sum,
        ),
    )
    return (heads_back(grad_query), heads_back(grad_key), heads_back(grad_value))


def shards(
    image_rows,
    text_input_rows,
    condition,
    slot_table,
    weights,
    weight_mom_one,
    weight_mom_two,
    biases,
    bias_mom_one,
    bias_mom_two,
    image_output_cotangent,
    text_output_cotangent,
):
    highest = lax.Precision.HIGHEST
    slot_count = image_rows.shape[0]
    image_local = image_rows.shape[1]
    col_width = weights.shape[3]
    heads_local = col_width // DH
    score_scale = DH ** (-0.5)
    col_start = lax.axis_index("tensor") * col_width
    gathered = lax.all_gather(weights.astype(jnp.bfloat16), ("shard", "ctx"), axis=1, tiled=True)
    live_mask = (slot_table >= 0).astype(jnp.float32)
    picker = (
        slot_table[:, None] == jnp.arange(condition.shape[0], dtype=jnp.int32)[None, :]
    ).astype(jnp.float32)
    chosen = jnp.dot(picker, condition, precision=highest)
    silu_bf = jax.nn.silu(chosen).astype(jnp.bfloat16)
    bias_cols = lax.dynamic_slice_in_dim(biases, col_start, col_width, 2)
    mod_image = (
        jnp.einsum(
            "ni,ije->nje", silu_bf, gathered[0, :, 0:6, :], preferred_element_type=jnp.float32
        )
        + bias_cols[0, 0:6][None]
    )
    mod_text = (
        jnp.einsum(
            "ni,ije->nje", silu_bf, gathered[1, :, 0:6, :], preferred_element_type=jnp.float32
        )
        + bias_cols[1, 0:6][None]
    )
    modulation = lax.all_gather(jnp.stack([mod_image, mod_text]), "tensor", axis=3, tiled=True)
    inputs_all = (image_rows, text_input_rows)
    cots_all = (image_output_cotangent, text_output_cotangent)
    normed_one, inverse_one, hidden_one = ([], [], [])
    query_parts, key_parts, value_parts = ([], [], [])
    for stream in range(2):
        stream_mod = modulation[stream]
        normed, inverse = layer_norm(inputs_all[stream].astype(jnp.float32))
        hidden = (
            normed * (1.0 + stream_mod[:, 1][:, None, :]) + stream_mod[:, 0][:, None, :]
        ).astype(jnp.bfloat16)
        projected = jnp.einsum(
            "nti,ije->ntje", hidden, gathered[stream, :, 6:9, :], preferred_element_type=jnp.float32
        )
        query_parts.append((projected[:, :, 0] + bias_cols[stream, 6]).astype(jnp.bfloat16))
        key_parts.append(projected[:, :, 1].astype(jnp.bfloat16))
        value_parts.append((projected[:, :, 2] + bias_cols[stream, 7]).astype(jnp.bfloat16))
        normed_one.append(normed)
        inverse_one.append(inverse)
        hidden_one.append(hidden)
    queries_all = jnp.concatenate(query_parts, axis=1)
    keys_all = jnp.concatenate(key_parts, axis=1)
    values_all = jnp.concatenate(value_parts, axis=1)
    local_len = queries_all.shape[1]

    def split_heads(block):
        return block.reshape(slot_count, block.shape[1], heads_local, DH)

    query_heads = split_heads(queries_all)
    start_state = (
        jnp.zeros(query_heads.shape, jnp.float32),
        jnp.full((slot_count, heads_local, local_len), -jnp.inf, jnp.float32),
        jnp.zeros((slot_count, heads_local, local_len), jnp.float32),
    )

    def fold_slot(packed):
        return fold_block(
            (packed[0], packed[1], packed[2]), packed[3], packed[4], packed[5], score_scale
        )

    accumulated, run_max, run_sum = lax.map(
        fold_slot,
        (
            start_state[0],
            start_state[1],
            start_state[2],
            query_heads,
            split_heads(lax.all_gather(keys_all, "ctx", axis=1, tiled=True)),
            split_heads(lax.all_gather(values_all, "ctx", axis=1, tiled=True)),
        ),
    )
    attended = accumulated / jnp.transpose(run_sum, (0, 2, 1))[:, :, :, None]
    log_sum = run_max + jnp.log(run_sum)
    attn_bf = attended.reshape(slot_count, local_len, col_width).astype(jnp.bfloat16)
    attn_split = (attn_bf[:, :image_local], attn_bf[:, image_local:])
    out_image_part = jnp.einsum(
        "nte,ie->nti", attn_split[0], gathered[0, :, 9, :], preferred_element_type=jnp.float32
    )
    out_text_part = jnp.einsum(
        "nte,ie->nti", attn_split[1], gathered[1, :, 9, :], preferred_element_type=jnp.float32
    )
    branch_sum = (
        lax.psum(out_image_part.astype(jnp.bfloat16), "tensor").astype(jnp.float32),
        lax.psum(out_text_part.astype(jnp.bfloat16), "tensor").astype(jnp.float32),
    )
    (
        attn_projs,
        residuals,
        normed_two,
        inverse_two,
        hidden_two,
        gelu_list,
        slope_list,
        down_parts,
    ) = ([], [], [], [], [], [], [], [])
    for stream in range(2):
        stream_mod = modulation[stream]
        attn_proj = branch_sum[stream] + biases[stream, 8]
        residual = inputs_all[stream].astype(jnp.float32) + stream_mod[:, 2][:, None, :] * attn_proj
        normed, inverse = layer_norm(residual)
        hidden = (
            normed * (1.0 + stream_mod[:, 4][:, None, :]) + stream_mod[:, 3][:, None, :]
        ).astype(jnp.bfloat16)
        preact = (
            jnp.einsum(
                "nti,ije->ntje",
                hidden,
                gathered[stream, :, 10:14, :],
                preferred_element_type=jnp.float32,
            )
            + bias_cols[stream, 9:13]
        )
        gelu_value, gelu_slope = gelu_parts(preact)
        gelu_bf = gelu_value.astype(jnp.bfloat16)
        down_parts.append(
            jnp.einsum(
                "ntje,ije->nti",
                gelu_bf,
                gathered[stream, :, 14:18, :],
                preferred_element_type=jnp.float32,
            )
        )
        attn_projs.append(attn_proj)
        residuals.append(residual)
        normed_two.append(normed)
        inverse_two.append(inverse)
        hidden_two.append(hidden)
        gelu_list.append(gelu_bf)
        slope_list.append(gelu_slope)
    mlp_sum = (
        lax.psum(down_parts[0].astype(jnp.bfloat16), "tensor").astype(jnp.float32),
        lax.psum(down_parts[1].astype(jnp.bfloat16), "tensor").astype(jnp.float32),
    )
    outputs_list, cot_list, grad_y_list, gate_m_list, up_grads, down_grads, back_two_parts = (
        [],
        [],
        [],
        [],
        [],
        [],
        [],
    )
    for stream in range(2):
        stream_mod = modulation[stream]
        mlp_proj = mlp_sum[stream] + biases[stream, 13]
        outputs_list.append(
            (
                (residuals[stream] + stream_mod[:, 5][:, None, :] * mlp_proj)
                * live_mask[:, None, None]
            ).astype(jnp.bfloat16)
        )
        cotangent = cots_all[stream].astype(jnp.float32) * live_mask[:, None, None]
        gate_m_list.append(jnp.sum(cotangent * mlp_proj, axis=1))
        grad_y = cotangent * stream_mod[:, 5][:, None, :]
        grad_y_bf = grad_y.astype(jnp.bfloat16)
        down_grads.append(
            jnp.einsum(
                "nti,ntje->ije", grad_y_bf, gelu_list[stream], preferred_element_type=jnp.float32
            )
        )
        grad_pre = (
            jnp.einsum(
                "nti,ije->ntje",
                grad_y_bf,
                gathered[stream, :, 14:18, :],
                preferred_element_type=jnp.float32,
            )
            * slope_list[stream]
        )
        grad_pre_bf = grad_pre.astype(jnp.bfloat16)
        up_grads.append(
            jnp.einsum(
                "nti,ntje->ije", hidden_two[stream], grad_pre_bf, preferred_element_type=jnp.float32
            )
        )
        back_two_parts.append(
            jnp.einsum(
                "ntje,ije->nti",
                grad_pre_bf,
                gathered[stream, :, 10:14, :],
                preferred_element_type=jnp.float32,
            )
        )
        cot_list.append(cotangent)
        grad_y_list.append((grad_y, jnp.sum(grad_pre, axis=(0, 1))))
    back_two = (
        lax.psum(back_two_parts[0].astype(jnp.bfloat16), "tensor").astype(jnp.float32),
        lax.psum(back_two_parts[1].astype(jnp.bfloat16), "tensor").astype(jnp.float32),
    )
    grad_resids, mod_partial, out_grads, grad_attn_parts, bias_outs = ([], [], [], [], [])
    for stream in range(2):
        stream_mod = modulation[stream]
        grad_shift_m = jnp.sum(back_two[stream], axis=1)
        grad_scale_m = jnp.sum(back_two[stream] * normed_two[stream], axis=1)
        grad_resid = cot_list[stream] + norm_back(
            normed_two[stream],
            inverse_two[stream],
            back_two[stream] * (1.0 + stream_mod[:, 4][:, None, :]),
        )
        grad_gate_a = jnp.sum(grad_resid * attn_projs[stream], axis=1)
        grad_branch = grad_resid * stream_mod[:, 2][:, None, :]
        grad_branch_bf = grad_branch.astype(jnp.bfloat16)
        out_grads.append(
            jnp.einsum(
                "nti,nte->ie",
                grad_branch_bf,
                attn_split[stream],
                preferred_element_type=jnp.float32,
            )
        )
        grad_attn_parts.append(
            jnp.einsum(
                "nti,ie->nte",
                grad_branch_bf,
                gathered[stream, :, 9, :],
                preferred_element_type=jnp.float32,
            ).astype(jnp.bfloat16)
        )
        bias_outs.append(jnp.sum(grad_branch, axis=(0, 1)))
        grad_resids.append(grad_resid)
        mod_partial.append((grad_gate_a, grad_shift_m, grad_scale_m))
    keys_back, values_back = (
        lax.all_gather(keys_all, "ctx", axis=1, tiled=True),
        lax.all_gather(values_all, "ctx", axis=1, tiled=True),
    )
    grad_heads = split_heads(jnp.concatenate(grad_attn_parts, axis=1))

    def back_slot(packed):
        return attend_back(
            packed[0], packed[1], packed[2], packed[3], packed[4], packed[5], score_scale
        )

    grad_query, grad_key_full, grad_value_full = lax.map(
        back_slot,
        (
            query_heads,
            split_heads(keys_back),
            split_heads(values_back),
            split_heads(attn_bf),
            grad_heads,
            log_sum,
        ),
    )
    grad_key, grad_value = (
        lax.psum_scatter(
            grad_key_full.reshape(slot_count, -1, col_width).astype(jnp.bfloat16),
            "ctx",
            scatter_dimension=1,
            tiled=True,
        ).astype(jnp.float32),
        lax.psum_scatter(
            grad_value_full.reshape(slot_count, -1, col_width).astype(jnp.bfloat16),
            "ctx",
            scatter_dimension=1,
            tiled=True,
        ).astype(jnp.float32),
    )
    grad_query = grad_query.reshape(slot_count, local_len, col_width)
    qkv_grads, back_one_parts, bias_qv = ([], [], [])
    for stream in range(2):
        if stream == 0:
            part_q, part_k, part_v = (
                grad_query[:, :image_local],
                grad_key[:, :image_local],
                grad_value[:, :image_local],
            )
        else:
            part_q, part_k, part_v = (
                grad_query[:, image_local:],
                grad_key[:, image_local:],
                grad_value[:, image_local:],
            )
        bias_qv.append((jnp.sum(part_q, axis=(0, 1)), jnp.sum(part_v, axis=(0, 1))))
        grad_stack = jnp.stack([part_q, part_k, part_v], axis=2).astype(jnp.bfloat16)
        qkv_grads.append(
            jnp.einsum(
                "nti,ntje->ije", hidden_one[stream], grad_stack, preferred_element_type=jnp.float32
            )
        )
        back_one_parts.append(
            jnp.einsum(
                "ntje,ije->nti",
                grad_stack,
                gathered[stream, :, 6:9, :],
                preferred_element_type=jnp.float32,
            )
        )
    back_one = (
        lax.psum(back_one_parts[0].astype(jnp.bfloat16), "tensor").astype(jnp.float32),
        lax.psum(back_one_parts[1].astype(jnp.bfloat16), "tensor").astype(jnp.float32),
    )
    grad_outputs, front_list, full_list, bias_list = ([], [], [], [])
    slot_cond = jnp.zeros(chosen.shape, jnp.float32)
    silu_wide = silu_bf.astype(jnp.float32)
    for stream in range(2):
        stream_mod = modulation[stream]
        grad_gate_a, grad_shift_m, grad_scale_m = mod_partial[stream]
        grad_shift_a = jnp.sum(back_one[stream], axis=1)
        grad_scale_a = jnp.sum(back_one[stream] * normed_one[stream], axis=1)
        grad_input = grad_resids[stream] + norm_back(
            normed_one[stream],
            inverse_one[stream],
            back_one[stream] * (1.0 + stream_mod[:, 1][:, None, :]),
        )
        grad_outputs.append(grad_input.astype(jnp.bfloat16))
        grad_mod = jnp.stack(
            [
                grad_shift_a,
                grad_scale_a,
                grad_gate_a,
                grad_shift_m,
                grad_scale_m,
                gate_m_list[stream],
            ],
            axis=1,
        )
        mod_cols = lax.dynamic_slice_in_dim(grad_mod, col_start, col_width, 2)
        mod_weight_grad = jnp.einsum("ni,nje->ije", silu_wide, mod_cols, precision=highest)
        slot_cond = slot_cond + jnp.einsum(
            "nje,ije->ni",
            mod_cols,
            gathered[stream, :, 0:6, :],
            precision=highest,
            preferred_element_type=jnp.float32,
        )
        front_part = jnp.concatenate(
            [mod_weight_grad, qkv_grads[stream], out_grads[stream][:, None, :]], axis=1
        )
        front_list.append(front_part)
        full_list.append(
            jnp.concatenate([front_part, up_grads[stream], down_grads[stream]], axis=1)
        )
        grad_y, bias_up = grad_y_list[stream]
        bias_out = lax.dynamic_slice_in_dim(bias_outs[stream], col_start, col_width, 0)
        bias_down = lax.dynamic_slice_in_dim(jnp.sum(grad_y, axis=(0, 1)), col_start, col_width, 0)
        bias_list.append(
            jnp.concatenate(
                [
                    jnp.sum(mod_cols, axis=0),
                    bias_qv[stream][0][None],
                    bias_qv[stream][1][None],
                    bias_out[None],
                    bias_up,
                    bias_down[None],
                ],
                axis=0,
            )
        )
    weight_grad = lax.psum_scatter(
        jnp.stack(full_list).astype(jnp.bfloat16), ("shard", "ctx"), scatter_dimension=1, tiled=True
    ).astype(jnp.float32)
    cond_local = jnp.dot(jnp.transpose(picker), slot_cond * silu_slope(chosen), precision=highest)
    bias_spread = lax.dynamic_update_slice_in_dim(
        jnp.zeros(biases.shape, jnp.float32), jnp.stack(bias_list), col_start, 2
    )
    local_squares = jnp.sum(weight_grad * weight_grad, axis=(1, 3))
    bias_grad, condition_grad, segment_squares = lax.psum(
        (bias_spread, cond_local, local_squares), ("shard", "ctx", "tensor")
    )
    weight_factor = jnp.minimum(1.0, clip_unit * MODEL_WIDTH / jnp.sqrt(segment_squares + clip_eps))
    weight_clipped = weight_grad * weight_factor[:, None, :, None]
    bias_squares = jnp.sum(bias_grad * bias_grad, axis=2)
    bias_factor = jnp.minimum(1.0, clip_unit * MODEL_WIDTH**0.5 / jnp.sqrt(bias_squares + clip_eps))
    bias_clipped = bias_grad * bias_factor[:, :, None]
    weight_new, weight_one_new, weight_two_new = adam_update(
        weights, weight_mom_one, weight_mom_two, weight_clipped, decay_rate
    )
    bias_new, bias_one_new, bias_two_new = adam_update(
        biases, bias_mom_one, bias_mom_two, bias_clipped, 0.0
    )
    return (
        outputs_list[0],
        outputs_list[1],
        grad_outputs[0],
        grad_outputs[1],
        condition_grad,
        weight_grad,
        weight_new,
        weight_one_new,
        weight_two_new,
        bias_grad,
        bias_new,
        bias_one_new,
        bias_two_new,
    )


def solution(mesh):
    placed = (
        P("shard", "ctx", None),
        P("shard", "ctx", None),
        P(),
        P("shard"),
        P(None, ("shard", "ctx"), None, "tensor"),
        P(None, ("shard", "ctx"), None, "tensor"),
        P(None, ("shard", "ctx"), None, "tensor"),
        P(),
        P(),
        P(),
        P("shard", "ctx", None),
        P("shard", "ctx", None),
    )
    return jax.shard_map(
        shards,
        mesh=mesh,
        in_specs=placed,
        out_specs=(
            P("shard", "ctx", None),
            P("shard", "ctx", None),
            P("shard", "ctx", None),
            P("shard", "ctx", None),
            P(),
            P(None, ("shard", "ctx"), None, "tensor"),
            P(None, ("shard", "ctx"), None, "tensor"),
            P(None, ("shard", "ctx"), None, "tensor"),
            P(None, ("shard", "ctx"), None, "tensor"),
            P(),
            P(),
            P(),
            P(),
        ),
        check_vma=False,
    )
```

profile of v0, /device:TPU:0, one launch (start us, length us, event | category | flops | bytes accessed | tf_op | source)
XLA Modules:
  0.0 1702.0 jit_solution(3748329595266909562)
XLA Ops:
  7.3 7.3 convert_element_type.306
  19.9 196.8 %all-gather.4.cloned.1.call-done = bf16[2,1536,18,384]{3,1,2,0:T(8,128)(2,1)} async-done(((bf16[2,192,18,384]{3,1,2,0:T(8,128)(2,1)}), bf16[2,1536,18,384]{3,1,2,0:T(8,128)(2,1)}) %all-gather.4.cloned.1.call-update) | async-done | bytes 42467344 | tf_op jit(solution)/shard_map/all_gather | solution.py:147
  216.7 4.0 fusion.97
  220.7 4.0 fusion.95
  224.8 13.4 all_gather.15
  243.1 6.6 fusion.133
  252.2 7.9 copy.117
  262.8 7.9 copy.115
  283.8 24.1 %all-gather.8.cloned.1.call-done = bf16[1,2202,384]{2,0,1:T(2,128)(2,1)} async-done(((bf16[1,1101,384]{2,0,1:T(2,128)(2,1)}), bf16[1,2202,384]{2,0,1:T(2,128)(2,1)}) %all-gather.8.cloned.1.call-update) | async-done | bytes 1691152 | tf_op jit(solution)/shard_map/all_gather | solution.py:215
  307.9 8.4 copy.118
  316.3 4.6 copy.121
  320.9 36.7 %all-gather.6.cloned.1.call-done = bf16[1,2202,384]{2,0,1:T(2,128)(2,1)} async-done(((bf16[1,1101,384]{2,0,1:T(2,128)(2,1)}), bf16[1,2202,384]{2,0,1:T(2,128)(2,1)}) %all-gather.6.cloned.1.call-update) | async-done | bytes 1691152 | tf_op jit(solution)/shard_map/all_gather | solution.py:214
  357.6 8.4 copy.116
  366.1 4.5 copy.120
  371.9 48.7 %while.51 = (s32[]{:T(128)}, f32[6,1101,64]{1,2,0:T(8,128)}, f32[6,1101]{1,0:T(8,128)S(1)}, f32[6,1101]{1,0:T(8,128)S(1)}, bf16[6,1101,64]{2,1,0:T(8,128)(2,1)},...) while((s32[]{:T(128)}, f32[6,1101,64]{1,2,0:T(8,128)}, ...), condition=%wide.region_7.8_spmd, body=%wide.region_4.7_spmd.sunk | while | flops 635267136 | bytes 30873476 | solution.py:82
  425.1 4.8 fusion.109
  433.3 126.3 %all-reduce.21.cloned.1.call-done = (bf16[1,1024,1536]{2,1,0:T(8,128)(2,1)}, bf16[1,77,1536]{2,1,0:T(8,128)(2,1)}) async-done(((bf16[1,1024,1536]{2,1,0:T(8,128)(2,1)}, bf16[1,77,1536]{2,1,0:T(8,128)(2,1)}), (bf16[1,1024,1536]{2,1,0:T(8,128)(2,1)}, bf16[1,77,1536]{2,1,0:T(8,128)(2,1)})) %all-reduce.21.cloned.1.call-update) | async-done | bytes 3382288 | tf_op jit(solution)/shard_map/psum | solution.py:229
  570.7 4.2 fusion.235
  574.9 4.7 fusion.132
  579.6 8.1 fusion.98
  587.7 11.7 fusion.236
  601.0 8.8 fusion.107
  619.5 10.3 fusion.106
  629.7 108.8 %all-reduce.19.cloned.1.call-done = (bf16[1,1024,1536]{2,1,0:T(8,128)(2,1)}, bf16[1,77,1536]{2,1,0:T(8,128)(2,1)}) async-done(((bf16[1,1024,1536]{2,1,0:T(8,128)(2,1)}, bf16[1,77,1536]{2,1,0:T(8,128)(2,1)}), (bf16[1,1024,1536]{2,1,0:T(8,128)(2,1)}, bf16[1,77,1536]{2,1,0:T(8,128)(2,1)})) %all-reduce.19.cloned.1.call-update) | async-done | bytes 3382288 | tf_op jit(solution)/shard_map/psum | solution.py:333
  740.6 7.0 fusion.89
  754.1 8.2 multiply_reduce_fusion.4
  775.3 100.9 %while.52 = (s32[]{:T(128)}, f32[6,1101,64]{1,2,0:T(8,128)}, bf16[6,2202,64]{1,2,0:T(8,128)(2,1)}, bf16[6,2202,64]{1,2,0:T(8,128)(2,1)}, bf16[6,1101,64]{2,1,0:T...) while((s32[]{:T(128)}, f32[6,1101,64]{1,2,0:T(8,128)}, ...), condition=%wide.region_24.25_spmd, body=%wide.region_22.24_spmd.sunk | while | flops 1568868992 | bytes 62255156 | solution.py:112
  883.9 43.7 %fusion = bf16[1104,384]{1,0:T(8,128)(2,1)} fusion(bf16[1,2202,384]{2,1,0:T(8,128)(2,1)} %copy.131), kind=kCustom, calls=%all-reduce-scatter | all-reduce-scatter fusion | flops 847873 | bytes 2539520
  930.6 5.0 fusion.131
  939.7 5.5 concatenate.52
  948.7 4.6 all-reduce.15.cloned.1.call-done
  956.4 3.9 fusion.130
  960.3 7.7 fusion.108
  985.3 222.9 %all-reduce.17.cloned.1.call-done = (bf16[1,1024,1536]{2,1,0:T(8,128)(2,1)}, bf16[1,77,1536]{2,1,0:T(8,128)(2,1)}, bf16[1,1024,1536]{2,1,0:T(8,128)(2,1)}, bf16[1,77,1536]{2,1,0:T(8,128)(2,1)}) async-done(((bf16[1,1024,1536]{2,1,0:T(8,128)(2,1)}, bf16[1,77,1536]{2,1,0:T(8,128)(2,1)}, bf16[1,1024,1536]{2,1,0:T(8,128)(2,1)}, bf16[1,77,1536]{2,1,0:T(8,128)(2,1)}), (bf16[1,1024,1536]{2,1,0:T(8,128)(2,1)}, ...) | async-done | bytes 6764560 | tf_op jit(solution)/shard_map/psum | solution.py:277
  1214.9 5.5 fusion.90
  1221.0 11.2 fusion.92
  1245.9 8.2 fusion.69
  1254.2 6.6 fusion.105
  1263.8 8.1 convert_dynamic-update-slice_fusion.3
  1272.0 8.1 convert_dynamic-update-slice_fusion.2
  1292.1 28.8 %pad_maximum_fusion = bf16[2,1536,18,384]{3,1,2,0:T(8,128)(2,1)} fusion(bf16[1,1536,18,384]{3,1,2,0:T(8,128)(2,1)} %bitcast.109, bf16[1,1536,18,384]{3,1,2,0:T(8,128)(2,1)} %bitcast.416), kind=kLoop, calls=%fused_computation.56 | loop fusion | flops 21233664 | bytes 84934656 | tf_op jit(solution)/shard_map/stack | solution.py:496
  1321.6 8.0 fusion.144
  1329.6 7.7 fusion.145
  1337.4 29.3 %all-reduce.13.cloned.1.call-done = f32[2,14,1536]{2,0,1:T(2,128)} async-done(((f32[2,14,1536]{2,0,1:T(2,128)}), f32[2,14,1536]{2,0,1:T(2,128)}) %all-reduce.13.cloned.1.call-update) | async-done | bytes 172048 | tf_op jit(solution)/shard_map/psum | solution.py:503
  1370.1 249.3 %reduce-scatter.6.cloned.1.call-done = bf16[2,192,18,384]{3,1,2,0:T(8,128)(2,1)} async-done(((bf16[2,1536,18,384]{3,1,2,0:T(8,128)(2,1)}), bf16[2,192,18,384]{3,1,2,0:T(8,128)(2,1)}) %reduce-scatter.6.cloned.1.call-update) | async-done | bytes 5308432 | tf_op jit(solution)/shard_map/reduce_scatter | solution.py:495
  1619.5 7.7 multiply_reduce_fusion
  1627.2 39.5 %all-reduce.3 = (f32[2,1536]{1,0:T(2,128)}, f32[2,18]{1,0:T(2,128)S(1)}) all-reduce(f32[2,1536]{1,0:T(2,128)S(1)} %broadcast_multiply_fusion, f32[2,18]{1,0:T(2,128)S(1)} %get-tuple-element.359), channel_id=1, replica_groups=mesh['shard'=4,'ctx'=2,'tensor'=4] {'shard','ctx','tensor'}, use_global_device_ids=true, to_apply=%region_45.46 | all-reduce | flops 3108 | bytes 24864 | tf_op jit(solution)/shard_map/psum | solution.py:503
  1666.6 27.9 %multiply_subtract_fusion = (f32[2,192,18,384]{3,1,2,0:T(8,128)}, f32[2,192,18,384]{3,1,2,0:T(8,128)}, f32[2,192,18,384]{3,1,2,0:T(8,128)}) fusion(f32[2,192,18,384]{3,1,2,0:T(8,128)} %param.20, f32[2,192,18,384]{3,1,2,0:T(8,128)} %get-tuple-element.568, f32[2,18]{1,0:T(2,128)S(1)} %multiply_minimum_fusion.1, f32[2,192,18,384]{3,1,2,0:T(8,128)} %param.21, ...), kind=kLoop, calls=%fused_computation.61 | loop fusion | flops 42467328 | bytes 74317968 | tf_op jit(solution)/shard_map/sub | solution.py:55
  (477 shorter events, 307.2 us)
Async XLA Ops:
  7.2 10.8 copy-start.7
  7.2 209.5 %all-gather.4.cloned.1.call-start = ((), (), s32[]{:S(2)}) async-start(), calls=%async_computation.1 | async-start | bytes 47775744 | tf_op jit(solution)/shard_map/all_gather | solution.py:147
  14.5 293.3 %all-gather.8.cloned.1.call-start = ((), (), s32[]{:S(2)}) async-start(), calls=%async_computation.3 | async-start | bytes 5073408 | tf_op jit(solution)/shard_map/all_gather | solution.py:215
  18.1 221.4 %copy-start.83 = (f32[77]{0:T(128)}, f32[77]{0:T(128)S(1)}, u32[]{:S(2)}) copy-start(f32[77]{0:T(128)S(1)} %broadcast_multiply_fusion.12) | copy-start | bytes 928
  18.4 221.1 %copy-start.92 = (f32[77]{0:T(128)}, f32[77]{0:T(128)S(1)}, u32[]{:S(2)}) copy-start(f32[77]{0:T(128)S(1)} %add_rsqrt_fusion.3) | copy-start | bytes 928
  18.9 224.2 %copy-start.58 = (f32[1024]{0:T(1024)}, f32[1024]{0:T(1024)S(1)}, u32[]{:S(2)}) copy-start(f32[1024]{0:T(1024)S(1)} %broadcast_multiply_fusion.6) | copy-start | bytes 12292
  19.9 223.2 %copy-start.62 = (f32[1024]{0:T(1024)}, f32[1024]{0:T(1024)S(1)}, u32[]{:S(2)}) copy-start(f32[1024]{0:T(1024)S(1)} %add_rsqrt_fusion.1) | copy-start | bytes 12292
  238.8 10.9 copy-start.50
  239.5 10.2 copy-start.54
  239.5 10.2 copy-start.81
  260.1 13.7 slice-start.2
  260.1 97.5 %all-gather.6.cloned.1.call-start = ((), (), s32[]{:S(2)}) async-start(), calls=%async_computation.2 | async-start | bytes 5073408 | tf_op jit(solution)/shard_map/all_gather | solution.py:214
  270.7 288.8 %all-reduce.21.cloned.1.call-start = ((), (), s32[]{:S(2)}) async-start(), calls=%async_computation.9 | async-start | bytes 6782976 | tf_op jit(solution)/shard_map/psum | solution.py:229
  320.9 51.0 %copy-start.39 = (f32[6,1101]{1,0:T(8,128)S(1)}, f32[6,1101]{1,0:T(8,128)}, u32[]{:S(2)}) copy-start(f32[6,1101]{1,0:T(8,128)} %custom-call.3) | copy-start | bytes 79276
  320.9 51.0 %copy-start.67 = (f32[6,1101]{1,0:T(8,128)S(1)}, f32[6,1101]{1,0:T(8,128)}, u32[]{:S(2)}) copy-start(f32[6,1101]{1,0:T(8,128)} %custom-call.2) | copy-start | bytes 79276
  429.9 308.7 %all-reduce.19.cloned.1.call-start = ((), (), s32[]{:S(2)}) async-start(), calls=%async_computation.8 | async-start | bytes 6782976 | tf_op jit(solution)/shard_map/psum | solution.py:333
  431.8 187.7 %copy-start.87 = (f32[1,4,384]{2,1,0:T(4,128)}, f32[1,4,384]{2,1,0:T(4,128)S(1)}, u32[]{:S(2)}) copy-start(f32[1,4,384]{2,1,0:T(4,128)S(1)} %copy.183) | copy-start | bytes 18436
  433.2 320.8 %copy-start.41 = (f32[1536]{0:T(1024)}, f32[1536]{0:T(1024)S(1)}, u32[]{:S(2)}) copy-start(f32[1536]{0:T(1024)S(1)} %get-tuple-element.292) | copy-start | bytes 18436
  560.8 188.0 %copy-start.85 = (f32[77]{0:T(128)}, f32[77]{0:T(128)S(1)}, u32[]{:S(2)}) copy-start(f32[77]{0:T(128)S(1)} %broadcast_multiply_fusion.11) | copy-start | bytes 928
  562.1 186.8 %copy-start.90 = (f32[77]{0:T(128)}, f32[77]{0:T(128)S(1)}, u32[]{:S(2)}) copy-start(f32[77]{0:T(128)S(1)} %add_rsqrt_fusion.2) | copy-start | bytes 928
  567.2 186.8 %copy-start.65 = (f32[1024]{0:T(1024)}, f32[1024]{0:T(1024)S(1)}, u32[]{:S(2)}) copy-start(f32[1024]{0:T(1024)S(1)} %add_rsqrt_fusion) | copy-start | bytes 12292
  570.6 8.9 copy-start.27
  587.7 11.7 copy-start.95
  609.8 343.5 %all-reduce.15.cloned.1.call-start = ((), (), s32[]{:S(2)}) async-start(), calls=%async_computation.6 | async-start | bytes 3391488
  738.5 10.3 copy-start.14
  738.5 10.3 copy-start.22
  738.5 10.3 copy-start.29
  883.8 324.3 %all-reduce.17.cloned.1.call-start = ((), (), s32[]{:S(2)}) async-start(), calls=%async_computation.7 | async-start | bytes 13565952 | tf_op jit(solution)/shard_map/psum | solution.py:277
  928.4 11.3 collective-permute-start
  937.4 19.1 %copy-start.43 = (bf16[1,77,384]{2,1,0:T(8,128)(2,1)S(1)}, bf16[1,77,384]{2,1,0:T(8,128)(2,1)}, u32[]{:S(2)}) copy-start(bf16[1,77,384]{2,1,0:T(8,128)(2,1)} %copy.163) | copy-start | bytes 177412
  968.0 246.9 %copy-start.59 = (f32[1024]{0:T(1024)S(1)}, f32[1024]{0:T(1024)}, u32[]{:S(2)}) copy-start(f32[1024]{0:T(1024)} %copy-done.58) | copy-start | bytes 12292
  968.0 398.6 %all-reduce.13.cloned.1.call-start = ((), (), s32[]{:S(2)}) async-start(), calls=%async_computation.5 | async-start | bytes 344064 | tf_op jit(solution)/shard_map/psum | solution.py:503
  977.8 243.1 %copy-start.42 = (f32[1536]{0:T(1024)S(1)}, f32[1536]{0:T(1024)}, u32[]{:S(2)}) copy-start(f32[1536]{0:T(1024)} %copy-done.41) | copy-start | bytes 18436
  1208.1 12.8 copy-start.5
  1208.1 12.8 copy-start.8
  1208.1 12.8 copy-start.63
  1208.2 12.8 copy-start.68
  1208.2 12.8 copy-start.75
  1245.7 373.7 %reduce-scatter.6.cloned.1.call-start = ((), (), s32[]{:S(2)}) async-start(), calls=%async_computation.4 | async-start | bytes 47775744 | tf_op jit(solution)/shard_map/reduce_scatter | solution.py:495
  1245.8 14.9 slice-start
  1260.8 11.1 slice-start.3
  1272.0 11.2 copy-start.17
  1321.6 15.7 copy-start.78
  1321.6 46.2 %copy-start.40 = (f32[2,14,1536]{2,0,1:T(2,128)S(1)}, f32[2,14,1536]{2,0,1:T(2,128)}, u32[]{:S(2)}) copy-start(f32[2,14,1536]{2,0,1:T(2,128)} %param.23) | copy-start | bytes 516100
  1321.6 46.2 %copy-start.46 = (f32[2,14,1536]{2,0,1:T(2,128)S(1)}, f32[2,14,1536]{2,0,1:T(2,128)}, u32[]{:S(2)}) copy-start(f32[2,14,1536]{2,0,1:T(2,128)} %param.24) | copy-start | bytes 516100
  1321.6 46.2 %copy-start.47 = (f32[2,14,1536]{2,0,1:T(2,128)S(1)}, f32[2,14,1536]{2,0,1:T(2,128)}, u32[]{:S(2)}) copy-start(f32[2,14,1536]{2,0,1:T(2,128)} %param.25) | copy-start | bytes 516100
  1666.6 27.9 %copy-start.26 = (f32[2,14,1536]{2,0,1:T(2,128)S(1)}, f32[2,14,1536]{2,0,1:T(2,128)}, u32[]{:S(2)}) copy-start(f32[2,14,1536]{2,0,1:T(2,128)} %all-reduce.13.cloned.1.call-done) | copy-start | bytes 516100
  1666.6 28.6 %copy-start.1 = (f32[2,1536]{1,0:T(2,128)S(1)}, f32[2,1536]{1,0:T(2,128)}, u32[]{:S(2)}) copy-start(f32[2,1536]{1,0:T(2,128)} %param.18) | copy-start | bytes 36868
  (75 other events, 395.5 us)
Sparse Core Ops, SparseCore 0:
  14.7 201.9 all-gather.3
  260.2 47.5 all-gather.7
  310.0 47.5 all-gather.5
  430.0 129.5 all-reduce.20
  610.0 128.5 all-reduce.18
  883.9 69.3 all-reduce.14
  968.1 239.9 all-reduce.16
  1245.8 120.7 all-reduce.12
  1370.3 249.1 reduce-scatter.5
where the time goes:
time: 1720 us; the launch traced here: 1700 us
  waiting for transfers between devices  999 us (58%)
  matrix products  277 us (16%)
  other arithmetic  172 us (10%)
  local copies, waits for them, and re-layouts  136 us (8%)
  blocking collectives  96.6 us (6%)
  between operations  17.4 us (1%)
    reduce_scatter x1, waiting for transfers between devices, shards(): lax.psum_scatter(jnp.stack(full_list).astype(jnp.bfloat16), ('shard', 'ct...  249 us
    psum x1, waiting for transfers between devices, shards(): lax.psum(down_parts[0].astype(jnp.bfloat16), 'tensor').astype(jnp.float32)  223 us
    all_gather x1, waiting for transfers between devices, shards(): lax.all_gather(weights.astype(jnp.bfloat16), ('shard', 'ctx'), axis=1, ti...  197 us
    psum x1, waiting for transfers between devices, shards(): lax.psum(out_image_part.astype(jnp.bfloat16), 'tensor').astype(jnp.float32)  126 us
    psum x1, waiting for transfers between devices, shards(): lax.psum(back_two_parts[0].astype(jnp.bfloat16), 'tensor')  109 us
    unnamed x1, blocking collectives  43.7 us
    psum x1, blocking collectives, shards(): lax.psum((bias_spread, cond_local, local_squares), ('shard', 'ctx', 'tens...  39.5 us
    all_gather x1, waiting for transfers between devices, shards(): lax.all_gather(keys_all, 'ctx', axis=1, tiled=True)  36.7 us
  transfers between devices with their start and end apart: 10, of which 9 were waited for; matrix products, arithmetic and copies ran while one was open for 14% of the time, Pallas kernels for 0%

commit v1 on v0

v1 whole, which is shorter than its diff:
```python
import functools
import jax
import jax.numpy as jnp
from jax import lax
from jax.experimental import pallas as pl
from jax.experimental.pallas import tpu as pltpu
from jax.experimental.layout import Layout, with_layout_constraint
from jax.sharding import PartitionSpec as P

DH=64
NT=(((1,),(1,)),((),()))
TN=(((0,),(0,)),((),()))
NN=(((1,),(0,)),((),()))
bf=jnp.bfloat16; f32=jnp.float32


beta_one = 0.9
beta_two = 0.95
learn_rate = 0.1
decay_rate = 0.1
adam_eps = 1e-08
adam_step = 10.0
norm_eps = 1e-06
gelu_coef = 0.044715
root_two_pi = 0.7978845608028654
clip_unit = 0.0001
clip_eps = 1e-12


def layer_norm(drawn_values):
    center = drawn_values - jnp.mean(drawn_values, axis=-1, keepdims=True)
    inverse = lax.rsqrt(jnp.mean(center * center, axis=-1, keepdims=True) + norm_eps)
    return (center * inverse, inverse)


def norm_back(normed, inverse, upstream):
    mean_grad = jnp.mean(upstream, axis=-1, keepdims=True)
    mean_dot = jnp.mean(upstream * normed, axis=-1, keepdims=True)
    return inverse * (upstream - mean_grad - normed * mean_dot)


def gelu_parts(preact):
    inner = root_two_pi * (preact + gelu_coef * preact * preact * preact)
    tanh_value = jnp.tanh(inner)
    value_out = 0.5 * preact * (1.0 + tanh_value)
    slope_out = 0.5 * (1.0 + tanh_value) + 0.5 * preact * (
        1.0 - tanh_value * tanh_value
    ) * root_two_pi * (1.0 + 3.0 * gelu_coef * preact * preact)
    return (value_out, slope_out)


def silu_slope(drawn_values):
    sigmoid_val = jax.nn.sigmoid(drawn_values)
    return sigmoid_val * (1.0 + drawn_values * (1.0 - sigmoid_val))


def adam_update(parameter, moment_one, moment_two, gradient, decay_factor):
    new_one = beta_one * moment_one + (1.0 - beta_one) * gradient
    new_two = beta_two * moment_two + (1.0 - beta_two) * gradient * gradient
    first_hat = new_one / (1.0 - beta_one**adam_step)
    second_hat = new_two / (1.0 - beta_two**adam_step)
    new_param = parameter - learn_rate * (
        first_hat / (jnp.sqrt(second_hat) + adam_eps) + decay_factor * parameter
    )
    return (new_param, new_one, new_two)


def dotf(a,b,dims,precision=None):
    return lax.dot_general(a,b,dims,preferred_element_type=f32,precision=precision)

def attn_fwd_kernel(heads, img, live, q_ref, kv_ref, a_ref, lse_ref):
    T=kv_ref.shape[2]
    bq=q_ref.shape[1]
    lane=lax.broadcasted_iota(jnp.int32,(1,256),1)
    lane1=lax.broadcasted_iota(jnp.int32,(1,128),1)
    keep=lax.broadcasted_iota(jnp.int32,(1,T-img),1) < live-img
    q=q_ref[0]
    acc=jnp.zeros((bq,256),f32)
    lse_tile=jnp.zeros((bq,128),f32)
    for h in range(heads):
        qm=jnp.where((lane>>6)==h,q,jnp.zeros_like(q))
        parts=[]
        for b in range(2):
            parts.append((dotf(qm,kv_ref[0,b,:img,:256],NT), b, 0, img))
            s=dotf(qm,kv_ref[0,b,img:,:256],NT)
            parts.append((jnp.where(keep,s,-1e30), b, img, T))
        m=functools.reduce(jnp.maximum,[jnp.max(p[0],axis=1,keepdims=True) for p in parts])
        l=jnp.zeros((bq,1),f32)
        pv=jnp.zeros((bq,256),f32)
        for s,b,lo,hi in parts:
            e=jnp.exp(s-m)
            l=l+jnp.sum(e,axis=1,keepdims=True)
            pv=pv+dotf(e.astype(bf),kv_ref[0,b,lo:hi,128:384],NN)
        acc=jnp.where((lane>>6)==h+1,pv/l,acc)
        lse_tile=jnp.where(lane1==h,m+jnp.log(l),lse_tile)
    a_ref[0]=acc[:,64:256].astype(bf)
    lse_ref[0]=lse_tile.T[:8]

def attn_fwd(q,kv,img,live,bq=384,heads=3):
    S,T,_=q.shape
    return pl.pallas_call(
        functools.partial(attn_fwd_kernel,heads,img,live),
        grid=(S,T//bq),
        in_specs=[pl.BlockSpec((1,bq,256),lambda s,i:(s,i,0)),
                  pl.BlockSpec((1,2,T,384),lambda s,i:(s,0,0,0))],
        out_specs=[pl.BlockSpec((1,bq,192),lambda s,i:(s,i,0)),
                   pl.BlockSpec((1,8,bq),lambda s,i:(s,0,i))],
        out_shape=[jax.ShapeDtypeStruct((S,T,192),bf),jax.ShapeDtypeStruct((S,8,T),f32)],
        compiler_params=pltpu.CompilerParams(vmem_limit_bytes=56*2**20),
        cost_estimate=pl.CostEstimate(flops=16*S*T*T*256,bytes_accessed=4*S*T*384,transcendentals=S*T*T*6),
        name="attn_fwd",
    )(q,kv)

def attn_bwd_kernel(heads, q_ref, kv_ref, a_ref, da_ref, lse_ref, dq_ref, dkv_ref, daw, delta, dqa):
    kb=pl.program_id(1)
    T=q_ref.shape[1]
    bk=kv_ref.shape[1]
    lane=lax.broadcasted_iota(jnp.int32,(1,256),1)
    @pl.when(kb==0)
    def _():
        da=da_ref[0]
        daw[...]=jnp.concatenate([jnp.zeros((T,64),bf),da],axis=1)
        prod=da.astype(f32)*a_ref[0].astype(f32)
        hm=((lax.broadcasted_iota(jnp.int32,(8,192),1)>>6)==lax.broadcasted_iota(jnp.int32,(8,192),0)).astype(f32)
        delta[...]=dotf(hm,prod,NT,lax.Precision.HIGHEST)
        dqa[...]=jnp.zeros_like(dqa)
    kw=kv_ref[0,:,:256]
    vw=kv_ref[0,:,128:384]
    dk=jnp.zeros((bk,256),f32)
    dv=jnp.zeros((bk,256),f32)
    dq=jnp.zeros((T,256),f32)
    for h in range(heads):
        sel=(lane>>6)==h
        qm=jnp.where(sel,q_ref[0],jnp.zeros((),bf))
        dam=jnp.where((lane>>6)==h+1,daw[...],jnp.zeros((),bf))
        st=dotf(kw,qm,NT)
        p=jnp.exp(st-lse_ref[0,h:h+1,:])
        dv=dv+dotf(p.astype(bf),dam,NN)
        dpt=dotf(vw,dam,NT)
        ds=(p*(dpt-delta[h:h+1,:])).astype(bf)
        dk=dk+dotf(ds,qm,NN)
        km=jnp.where(sel,kw,jnp.zeros((),bf))
        dq=dq+dotf(ds,km,TN)
    dqa[...]+=dq
    dkv_ref[0]=jnp.concatenate([dk[:,:192],dv[:,64:256]],axis=1).astype(bf)
    @pl.when(kb==pl.num_programs(1)-1)
    def _():
        dq_ref[0]=(dqa[...][:,:192]*0.125).astype(bf)

def attn_bwd(q,kv,a,da,lse,bk=384,heads=3):
    S,T,_=q.shape
    kv=kv.reshape(S,2*T,384)
    dq,dkv=pl.pallas_call(
        functools.partial(attn_bwd_kernel,heads),
        grid=(S,2*T//bk),
        in_specs=[pl.BlockSpec((1,T,256),lambda s,i:(s,0,0)),
                  pl.BlockSpec((1,bk,384),lambda s,i:(s,i,0)),
                  pl.BlockSpec((1,T,192),lambda s,i:(s,0,0)),
                  pl.BlockSpec((1,T,192),lambda s,i:(s,0,0)),
                  pl.BlockSpec((1,8,T),lambda s,i:(s,0,0))],
        out_specs=[pl.BlockSpec((1,T,192),lambda s,i:(s,0,0)),
                   pl.BlockSpec((1,bk,384),lambda s,i:(s,i,0))],
        out_shape=[jax.ShapeDtypeStruct((S,T,192),bf),jax.ShapeDtypeStruct((S,2*T,384),bf)],
        scratch_shapes=[pltpu.VMEM((T,256),bf),pltpu.VMEM((8,T),f32),pltpu.VMEM((T,256),f32)],
        compiler_params=pltpu.CompilerParams(vmem_limit_bytes=56*2**20),
        cost_estimate=pl.CostEstimate(flops=32*S*T*T*256,bytes_accessed=8*S*T*384,transcendentals=S*T*T*6),
        name="attn_bwd",
    )(q,kv,a,da,lse)
    return dq,dkv.reshape(S,2,T,384)


def asm_kernel(count, spans, idx_ref, *refs):
    for p in range(count):
        o = idx_ref[p]
        for t, (lo, size) in enumerate(spans):
            refs[count + t][:, pl.ds(o, 1)] = refs[p][:, lo : lo + size][:, None]


def assemble(pieces, index, spans):
    n, _, width = pieces[0].shape
    count = len(pieces)
    return pl.pallas_call(
        functools.partial(asm_kernel, count, spans),
        in_specs=[pl.BlockSpec(memory_space=pltpu.SMEM)]
        + [pl.BlockSpec(memory_space=pltpu.VMEM)] * count,
        out_specs=[pl.BlockSpec(memory_space=pltpu.VMEM)] * len(spans),
        out_shape=[
            jax.ShapeDtypeStruct((n, count, size, width), pieces[0].dtype) for _, size in spans
        ],
        compiler_params=pltpu.CompilerParams(vmem_limit_bytes=40 * 2**20),
        name="assemble",
    )(index, *pieces)


def adam_kernel(f_ref, g_ref, w_ref, m_ref, v_ref, *refs):
    og, ow, om, ov = refs[-4:]
    s, i = pl.program_id(0), pl.program_id(1)
    for j in range(g_ref.shape[1]):
        g = g_ref[0, j].astype(f32)
        og[0, j] = g
        ow[0, j], om[0, j], ov[0, j] = adam_update(
            w_ref[0, j], m_ref[0, j], v_ref[0, j], g * f_ref[s, i * g_ref.shape[1] + j], decay_rate
        )


def adam_segments(factor, grad, start, w, m, v, before=None):
    _, count, rows, cols = grad.shape
    block = (1, 2, rows, cols)
    here = pl.BlockSpec(block, lambda s, i: (s, i + start // 2, 0, 0))
    before = [] if before is None else list(before)
    return pl.pallas_call(
        adam_kernel,
        grid=(2, count // 2),
        in_specs=[
            pl.BlockSpec(memory_space=pltpu.SMEM),
            pl.BlockSpec(block, lambda s, i: (s, i, 0, 0)),
            here,
            here,
            here,
        ]
        + [pl.BlockSpec(memory_space=pl.ANY)] * len(before),
        out_specs=[here] * 4,
        out_shape=[jax.ShapeDtypeStruct(w.shape, f32)] * 4,
        input_output_aliases={5 + k: k for k in range(len(before))},
        compiler_params=pltpu.CompilerParams(vmem_limit_bytes=40 * 2**20),
        name="adam",
    )(factor, grad, w, m, v, *before)


def make_shards(sizes):
    ns, nc, nt = sizes["shard"], sizes["ctx"], sizes["tensor"]
    owners = 2 * nt
    block_count = ns * nc
    cbits = nc.bit_length() - 1
    links = [("shard", 1 << b, (1 << b) << cbits) for b in range(1, ns.bit_length() - 1)]
    links += [("ctx", 1 << b, 1 << b) for b in range(cbits)]
    core_rel = 1 << cbits

    def pp(x, axis, xor):
        return lax.ppermute(x, axis, [(i, i ^ xor) for i in range(sizes[axis])])

    def all_sum(x):
        x = x + pp(x, "shard", 1)
        for axis, xor, _ in links:
            x = x + pp(x, axis, xor)
        for b in range(nt.bit_length() - 1):
            x = x + pp(x, "tensor", 1 << b)
        return x

    def after(x, *deps):
        return lax.optimization_barrier((x,) + deps)[0]

    def dyn(x, i, axis=0):
        return lax.dynamic_index_in_dim(x, i, axis, keepdims=False)

    def shards(
        image_rows,
        text_rows,
        condition,
        slot_table,
        weights,
        mom_one,
        mom_two,
        biases,
        bias_one,
        bias_two,
        image_cot,
        text_cot,
    ):
        hp = lax.Precision.HIGHEST
        nseq, D = condition.shape
        img = image_rows.shape[1]
        txt = text_rows.shape[1]
        ct = -(-txt // (owners * 16)) * 16
        ci = img // owners
        tpad = ct * owners
        T = img + tpad
        live_rows = img + txt
        cw = weights.shape[3]
        hw = cw // 2
        rows = weights.shape[1]
        shard_i, ctx_i, z = (lax.axis_index(a) for a in ("shard", "ctx", "tensor"))
        core = shard_i % 2
        first = core == 0
        me = shard_i * nc + ctx_i
        own = core * nt + z

        fixed = nseq == 2
        def pair(x):
            other = pp(x, "shard", 1)
            even = jnp.where(first, x, other)
            if fixed:
                return even
            return jnp.concatenate([even, jnp.where(first, other, x)], axis=0)

        def unpair(x):
            if fixed:
                return jnp.where(first, x, jnp.zeros_like(x))
            return jnp.where(first, x[:1], x[1:])

        table = pair(slot_table)
        S = table.shape[0]
        live = (table >= 0).astype(f32)
        picker = (table[:, None] == jnp.arange(nseq, dtype=jnp.int32)[None, :]).astype(f32)
        pad_txt = lambda x: jnp.pad(x, ((0, 0), (0, tpad - txt), (0, 0)))
        X = (pair(image_rows), pad_txt(pair(text_rows)))
        cots = (pair(image_cot), pad_txt(pair(text_cot)))

        wt = jnp.moveaxis(weights, 2, 1)
        wt = with_layout_constraint(wt, Layout(major_to_minor=(0, 1, 2, 3)))
        wb = wt.astype(bf)

        def halves(w):
            lo, hi = w[..., :hw], w[..., hw:]
            return lo, hi

        def cat(a, b):
            return jnp.concatenate([a, b], axis=-1)

        def group_one(w, which):
            k, v = halves(w[:, 7])[which], halves(w[:, 8])[which]
            q, o = halves(w[:, 6])[which], halves(w[:, 9])[which]
            return jnp.stack([cat(k[0], v[0]), cat(q[0], q[1]), cat(k[1], v[1]), cat(o[0], o[1])])

        one_lo, one_hi = group_one(wb, 0), group_one(wb, 1)
        up_pair = wb[:, 10:14].reshape(2, 2, 2, rows, cw)
        dn_pair = wb[:, 14:18].reshape(2, 2, 2, rows, cw)

        def gather_start(mine, theirs):
            return mine, pp(theirs, "shard", 1)

        def gather_step(state, step, ties=((), ())):
            if step == 0:
                mine, got = state
                n = mine.shape[0]
                state = [
                    {0: mine[part], core_rel: got[part]}
                    for part in (slice(0, n // 2), slice(n // 2, n))
                ]
            res = []
            for pieces, order, tie in zip(state, (links, links[::-1]), ties):
                axis, xor, rel = order[step]
                new = dict(pieces)
                for p, v in pieces.items():
                    new[p ^ rel] = pp(after(v, *tie) if tie else v, axis, xor)
                res.append(new)
            return res

        def gather_end(state):
            outs = []
            for pieces in state:
                keys = sorted(pieces)
                index = jnp.array(keys, jnp.int32) ^ me
                (full,) = assemble([pieces[p] for p in keys], index, [(0, rows)])
                outs.append(full.reshape(-1, D, cw))
            return outs

        def scatter_start(halves_in):
            res = []
            for g in halves_in:
                g = g.reshape(-1, block_count, rows, cw)
                res.append({p: dyn(g, me ^ p, 1) for p in range(block_count)})
            return res

        def scatter_send(state, step):
            res = []
            for pieces, order in zip(state, (links, links[::-1])):
                axis, xor, rel = order[step]
                res.append({p: pp(pieces[p ^ rel], axis, xor) for p in pieces if not p & rel})
            return res

        def scatter_add(state, got, tie=()):
            res = []
            for pieces, new in zip(state, got):
                res.append(
                    {
                        p: (pieces[p].astype(f32) + (after(v, *tie) if tie else v).astype(f32)).astype(bf)
                        for p, v in new.items()
                    }
                )
            return res

        def scatter_end(state):
            mine = jnp.concatenate([pieces[0] for pieces in state], axis=0)
            theirs = jnp.concatenate([pieces[core_rel] for pieces in state], axis=0)
            theirs = pp(theirs, "shard", 1)
            return jnp.where(first, mine, theirs), jnp.where(first, theirs, mine)

        def own_chunk(x, size):
            return lax.dynamic_slice_in_dim(x, own * size, size, 1)

        def fold(part_img, part_txt):
            buf = jnp.concatenate(
                [part_img.reshape(S, 2, nt, ci, D), part_txt.reshape(S, 2, nt, ct, D)], axis=3
            )
            buf = jnp.moveaxis(buf, 0, 2)
            got = pp(dyn(buf, 1 - core), "shard", 1)
            return (dyn(buf, core).astype(f32) + got.astype(f32)).astype(bf)

        def sum_scatter(half, tie=()):
            half = after(half, *tie) if tie else half
            got = [pp(dyn(half, z ^ k), "tensor", k) for k in range(nt - 1, 0, -1)]
            total = dyn(half, z).astype(f32)
            for g in got:
                total = total + g.astype(f32)
            return total[:, :ci], total[:, ci:]

        def spread_send(own_img, own_txt, tie=()):
            chunk = jnp.concatenate([own_img, own_txt], axis=1)
            chunk = after(chunk, *tie) if tie else chunk
            pieces = {0: chunk}
            for k in range(nt - 1, 0, -1):
                pieces[k] = pp(chunk, "tensor", k)
            return pieces

        def spread_end(pieces):
            pieces = dict(pieces)
            pieces.update({k + nt: pp(v, "shard", 1) for k, v in list(pieces.items())})
            keys = sorted(pieces)
            index = jnp.array(keys, jnp.int32) ^ own
            a, b = assemble([pieces[k] for k in keys], index, [(0, ci), (ci, ct)])
            return a.reshape(S, img, D), b.reshape(S, tpad, D)

        silu_all = jax.nn.silu(condition).astype(bf)
        sc_rows = lax.dynamic_slice_in_dim(silu_all, me * rows, rows, 1)
        mod = jnp.einsum("ni,sjie->nsje", sc_rows, wb[:, :6], preferred_element_type=f32)
        mod = mod + pp(mod, "shard", 1)
        for axis, xor, _ in links:
            mod = mod + pp(mod, axis, xor)
        mod = jnp.einsum("pn,nsje->psje", picker, mod, precision=hp)

        def over_tensor(x):
            stacked = jnp.stack([x] + [pp(x, "tensor", k) for k in range(1, nt)])
            return jnp.concatenate([dyn(stacked, z ^ k) for k in range(nt)], axis=-1)

        mod = over_tensor(mod) + biases[None, :, :6]
        row_of = lambda s, j: mod[:, s, j][:, None, :]


        steps = len(links)
        one = gather_start(jnp.where(first, one_lo, one_hi), jnp.where(first, one_hi, one_lo))
        for step in range(steps):
            one = gather_step(one, step)
        g_a, g_b = gather_end(one)
        w_kv = (g_a[0], g_b[0])
        w_q = (g_a[1][:, :hw], g_a[1][:, hw:])
        w_o = (g_b[1][:, :hw], g_b[1][:, hw:])
        mlp_half = lambda i: jnp.concatenate(
            [dyn(up_pair, i, 1), dyn(dn_pair, i, 1)], axis=1
        ).reshape(8, rows, cw)
        mlp = gather_start(mlp_half(core), mlp_half(1 - core))

        col = z * cw
        bias_half = lax.dynamic_slice_in_dim(biases, col + core * hw, hw, 2)
        bias_full = lax.dynamic_slice_in_dim(biases, col, cw, 2)

        hidden_one, q_parts, kv_parts = [], [], []
        token_live = jnp.arange(tpad) < txt
        for s in range(2):
            normed, _ = layer_norm(X[s].astype(f32))
            h = (normed * (1.0 + row_of(s, 1)) + row_of(s, 0)).astype(bf)
            hidden_one.append(h)
            q = jnp.einsum("sti,ie->ste", h, w_q[s], preferred_element_type=f32) + bias_half[s, 6]
            q = q.astype(bf) * jnp.asarray(DH**-0.5, bf)
            kv = jnp.einsum("sti,ie->ste", h, w_kv[s], preferred_element_type=f32)
            kv = kv + jnp.concatenate([jnp.zeros((hw,), f32), bias_half[s, 7]])
            if s == 1:
                kv = jnp.where(token_live[None, :, None], kv, 0.0)
            q_parts.append(jnp.pad(q, ((0, 0), (0, 0), (0, 64))))
            kv_parts.append(kv.astype(bf))
        q_all = jnp.concatenate(q_parts, axis=1)
        kv_own = jnp.concatenate(kv_parts, axis=1)
        kv_got = pp(kv_own, "ctx", 1)
        kv_all = jnp.stack([kv_own, kv_got], axis=1)
        mlp = gather_step(mlp, 0, ((kv_own,), (kv_got,)))
        attn, lse = attn_fwd(q_all, kv_all, img, live_rows)
        attn_split = (attn[:, :img], attn[:, img:])
        o_half = fold(
            *(
                jnp.einsum("ste,ie->sti", attn_split[s], w_o[s], preferred_element_type=f32).astype(bf)
                for s in range(2)
            )
        )
        o_sum = sum_scatter(o_half)
        for step in range(1, steps):
            mlp = gather_step(mlp, step, ((o_half,), (o_half,)))
        X_own = [own_chunk(X[s], (ci, ct)[s]).astype(f32) for s in range(2)]
        cot_live = [c * live.astype(bf)[:, None, None] for c in cots]
        dO = [own_chunk(cot_live[s], (ci, ct)[s]).astype(f32) for s in range(2)]
        o_proj, x1, n2, inv2, h2_own = [], [], [], [], []
        for s in range(2):
            o_proj.append(o_sum[s] + biases[s, 8])
            x1.append(X_own[s] + row_of(s, 2) * o_proj[s])
            n, i = layer_norm(x1[s])
            n2.append(n)
            inv2.append(i)
            h2_own.append((n * (1.0 + row_of(s, 4)) + row_of(s, 3)).astype(bf))
        h2 = spread_end(spread_send(*h2_own))
        mlp = [{p: after(v, h2[0]) for p, v in pieces.items()} for pieces in mlp]
        m_img, m_txt = gather_end(mlp)
        w_up, w_dn = (m_img[:2], m_txt[:2]), (m_img[2:], m_txt[2:])

        y_parts, dh_parts, up_bias, kept = [], [], [], []
        for s in range(2):
            dy_b = (cot_live[s].astype(f32) * row_of(s, 5)).astype(bf)
            dh_part = 0.0
            for j in range(2):
                u = jnp.einsum("sti,ie->ste", h2[s], w_up[s][j], preferred_element_type=f32)
                u = u + lax.dynamic_slice_in_dim(bias_full[s], 9 + 2 * core + j, 1, 0)[0]
                val, slope = gelu_parts(u)
                du = jnp.einsum("sti,ie->ste", dy_b, w_dn[s][j], preferred_element_type=f32) * slope
                du_b = du.astype(bf)
                up_bias.append(jnp.sum(du, axis=(0, 1)))
                dh_part = dh_part + jnp.einsum("ste,ie->sti", du_b, w_up[s][j], preferred_element_type=f32)
                kept.append((dy_b, val.astype(bf), du_b))
            dh_parts.append(dh_part.astype(bf))
        dh_half = fold(*dh_parts)
        dh2 = sum_scatter(dh_half)
        mlp_grads = []
        for s in range(2):
            ups, dns, y_part = [], [], 0.0
            for j in range(2):
                dy_b, G, du_b = kept[2 * s + j]
                G = after(G, dh_half)
                du_b = after(du_b, dh_half)
                y_part = y_part + jnp.einsum("ste,ie->sti", G, w_dn[s][j], preferred_element_type=f32)
                ups.append(jnp.einsum("sti,ste->ie", h2[s], du_b, preferred_element_type=f32).astype(bf))
                dns.append(jnp.einsum("sti,ste->ie", dy_b, G, preferred_element_type=f32).astype(bf))
            y_parts.append(y_part.astype(bf))
            mlp_grads.append(jnp.stack(ups + dns))
        mlp_state = scatter_start(mlp_grads)
        mlp_got = scatter_send(mlp_state, 0)
        y_half = fold(*y_parts)
        dx1, do_own, early, bias_own = [], [], [], []
        for s in range(2):
            g = dh2[s] * (1.0 + row_of(s, 4))
            d = dO[s] + norm_back(n2[s], inv2[s], g)
            dx1.append(d)
            do = d * row_of(s, 2)
            do_own.append(do.astype(bf))
            early.append(
                [
                    jnp.sum(d * o_proj[s], axis=1),
                    jnp.sum(dh2[s], axis=1),
                    jnp.sum(dh2[s] * n2[s], axis=1),
                ]
            )
            dy = dO[s] * row_of(s, 5)
            bias_own.append((jnp.sum(do, axis=(0, 1)), jnp.sum(dy, axis=(0, 1))))
        do_b = spread_end(spread_send(*do_own))
        mlp_state = scatter_add(mlp_state, mlp_got, (do_b[0],))
        y_sum = sum_scatter(y_half, (do_b[0],))
        out_own = []
        for s in range(2):
            y = y_sum[s] + biases[s, 13]
            out_own.append(((x1[s] + row_of(s, 5) * y) * live[:, None, None]).astype(bf))
            early[s] = jnp.stack(early[s] + [jnp.sum(dO[s] * y, axis=1)], axis=1)
        out_pieces = spread_send(*out_own)
        for step in range(1, steps):
            mlp_got = scatter_send(mlp_state, step)
            if step < steps - 1:
                mlp_state = scatter_add(mlp_state, mlp_got)

        da = jnp.concatenate(
            [
                jnp.einsum("sti,ie->ste", do_b[s], w_o[s], preferred_element_type=f32).astype(bf)
                for s in range(2)
            ],
            axis=1,
        )
        o_grads = [
            jnp.einsum("sti,ste->ie", do_b[s], attn_split[s], preferred_element_type=f32).astype(bf)
            for s in range(2)
        ]
        dq, dkv = attn_bwd(q_all, kv_all, attn, da, lse)
        dkv_got = pp(dkv[:, 1], "ctx", 1)
        dkv = dkv[:, 0].astype(f32) + dkv_got.astype(f32)
        out_pieces = {k: after(v, dq) for k, v in out_pieces.items()}
        out_img, out_txt = spread_end(out_pieces)
        mlp_state = scatter_add(mlp_state, mlp_got, (dq,))
        mlp_lo, mlp_hi = scatter_end(mlp_state)
        dkv = jnp.where((jnp.arange(T) < live_rows)[None, :, None], dkv, 0.0)
        dv_bias_src = dkv[:, :, hw:]
        dkv_b = dkv.astype(bf)
        q_grads, kv_grads, dh1_parts, qv_bias = [], [], [], []
        dqkv = []
        for s in range(2):
            part = slice(0, img) if s == 0 else slice(img, T)
            qs, kvs = dq[:, part], dkv_b[:, part]
            dqkv.append((qs, kvs))
            dh1_parts.append(
                (
                    jnp.einsum("ste,ie->sti", qs, w_q[s], preferred_element_type=f32)
                    + jnp.einsum("ste,ie->sti", kvs, w_kv[s], preferred_element_type=f32)
                ).astype(bf)
            )
            qv_bias.append((jnp.sum(qs.astype(f32), axis=(0, 1)), jnp.sum(dv_bias_src[:, part], axis=(0, 1))))
        d_half = fold(*dh1_parts)
        dh1 = sum_scatter(d_half)
        for s in range(2):
            qs, kvs = (after(x, d_half) for x in dqkv[s])
            q_grads.append(jnp.einsum("sti,ste->ie", hidden_one[s], qs, preferred_element_type=f32).astype(bf))
            kv_grads.append(jnp.einsum("sti,ste->ie", hidden_one[s], kvs, preferred_element_type=f32).astype(bf))
        one_state = scatter_start(
            [jnp.stack([kv_grads[0], cat(*q_grads)]), jnp.stack([kv_grads[1], cat(*o_grads)])]
        )
        one_got = scatter_send(one_state, 0)
        grad_own, late = [], []
        for s in range(2):
            n, i = layer_norm(X_own[s])
            g = dh1[s] * (1.0 + row_of(s, 1))
            grad_own.append((dx1[s] + norm_back(n, i, g)).astype(bf))
            late.append(jnp.stack([jnp.sum(dh1[s], axis=1), jnp.sum(dh1[s] * n, axis=1)], axis=1))
        grad_pieces = spread_send(*grad_own)
        one_state = scatter_add(one_state, one_got, (grad_own[0],))
        for step in range(1, steps):
            one_got = scatter_send(one_state, step)
            one_state = scatter_add(one_state, one_got)
        grad_img, grad_txt = spread_end(grad_pieces)
        one_lo, one_hi = scatter_end(one_state)
        join = lambda i, a: cat(one_lo[i, :, a * hw : (a + 1) * hw], one_hi[i, :, a * hw : (a + 1) * hw])
        dmod = jnp.stack([jnp.concatenate([late[s], early[s]], axis=1) for s in range(2)], axis=1)
        dmod = jnp.einsum("pn,psje->nsje", picker, dmod, precision=hp)

        def place(x, start):
            return lax.dynamic_update_slice_in_dim(jnp.zeros(x.shape[:-1] + (D,), f32), x, start, x.ndim - 1)

        bias_rows = []
        for s in range(2):
            qb, vb = qv_bias[s]
            up_place = jnp.stack(up_bias[2 * s : 2 * s + 2])
            up_rows = lax.dynamic_update_slice_in_dim(jnp.zeros((4, cw), f32), up_place, 2 * core, 0)
            bias_rows.append(
                jnp.concatenate(
                    [
                        place(jnp.stack([qb, vb]), col + core * hw),
                        bias_own[s][0][None],
                        place(up_rows, col),
                        bias_own[s][1][None],
                    ]
                )
            )
        packed = jnp.concatenate([dmod.reshape(-1, D), jnp.stack(bias_rows).reshape(-1, D)])
        packed = all_sum(packed)
        dmod = packed[: nseq * 12].reshape(nseq, 2, 6, D)
        bias_grad = jnp.concatenate(
            [jnp.sum(dmod, axis=0), packed[nseq * 12 :].reshape(2, 8, D)], axis=1
        )
        mod_cols = lax.dynamic_slice_in_dim(dmod, col, cw, 3)
        sc_wide = sc_rows.astype(f32)
        mod_grad = jnp.einsum("ni,nsje->sjie", sc_wide, mod_cols, precision=hp)
        cond_rows = jnp.einsum("nsje,sjie->ni", mod_cols, wb[:, :6].astype(f32), precision=hp)
        cond_part = place(cond_rows, me * rows)
        mlp_grad = jnp.stack([mlp_lo.reshape(2, 2, 2, rows, cw), mlp_hi.reshape(2, 2, 2, rows, cw)], axis=2)
        mlp_grad = mlp_grad.reshape(2, 8, rows, cw)
        one_grad = jnp.stack(
            [
                jnp.stack([join(1, s), join(2 * s, 0), join(2 * s, 1), join(3, s)])
                for s in range(2)
            ]
        )
        seg_sum = lambda g: jnp.sum(jnp.square(g.astype(f32)), axis=(2, 3))
        squares = jnp.concatenate([seg_sum(g) for g in (mod_grad, one_grad, mlp_grad)], axis=1)
        tail = jnp.concatenate([cond_part.reshape(-1), squares.reshape(-1)])
        tail = all_sum(tail)
        cond_grad = tail[: nseq * D].reshape(nseq, D) * silu_slope(condition)
        squares = tail[nseq * D :].reshape(2, 18)
        factor = jnp.minimum(1.0, clip_unit * D / jnp.sqrt(squares + clip_eps))
        moments = (wt, jnp.moveaxis(mom_one, 2, 1), jnp.moveaxis(mom_two, 2, 1))
        done = adam_segments(factor[:, 10:], mlp_grad, 10, *moments)
        done = adam_segments(factor[:, 6:10], one_grad, 6, *moments, before=done)
        done = adam_segments(factor[:, :6], mod_grad, 0, *moments, before=done)
        weight_grad, new_w, new_one, new_two = done
        bias_sq = jnp.sum(bias_grad * bias_grad, axis=2)
        bias_factor = jnp.minimum(1.0, clip_unit * D**0.5 / jnp.sqrt(bias_sq + clip_eps))
        new_b, new_b1, new_b2 = adam_update(
            biases, bias_one, bias_two, bias_grad * bias_factor[:, :, None], 0.0
        )
        back = lambda x: jnp.moveaxis(x, 1, 2)
        return (
            unpair(out_img),
            unpair(out_txt)[:, :txt],
            unpair(grad_img),
            unpair(grad_txt)[:, :txt],
            cond_grad,
            back(weight_grad),
            back(new_w),
            back(new_one),
            back(new_two),
            bias_grad,
            new_b,
            new_b1,
            new_b2,
        )

    return shards


def solution(mesh):
    sizes = dict(mesh.shape)
    rows = P("shard", "ctx", None)
    mat = P(None, ("shard", "ctx"), None, "tensor")
    return jax.shard_map(
        make_shards(sizes),
        mesh=mesh,
        in_specs=(rows, rows, P(), P("shard"), mat, mat, mat, P(), P(), P(), rows, rows),
        out_specs=(rows, rows, rows, rows, P(), mat, mat, mat, mat, P(), P(), P(), P()),
        check_vma=False,
    )
```

time: 1720 us -> 810 us (0.47)
  waiting for transfers between devices: 999 us -> 338 us
  matrix products: 277 us -> 60.9 us
  starting transfers between devices: 3.14 us -> 140 us
  blocking collectives: 96.6 us -> 0 us
  Pallas kernels: 0 us -> 85 us
  local copies, waits for them, and re-layouts: 136 us -> 65.2 us
  other arithmetic: 172 us -> 106 us
    psum x4 -> x0, waiting for transfers between devices: 487 us -> none  [the longest x1 223 us: shards(): lax.psum(down_parts[0].astype(jnp.bfloat16), 'tensor').astype(jnp.float32)]
    ppermute x0 -> x119, waiting for transfers between devices: none -> 338 us  [pp(): return lax.ppermute(x, axis, [(i, i ^ xor) for i in range(sizes[axis])])]
    all_gather x3 -> x0, waiting for transfers between devices: 258 us -> none  [the longest x1 197 us: shards(): lax.all_gather(weights.astype(jnp.bfloat16), ('shard', 'ctx'), axis=1, ti...]
    reduce_scatter x1 -> x0, waiting for transfers between devices: 249 us -> none  [shards(): lax.psum_scatter(jnp.stack(full_list).astype(jnp.bfloat16), ('shard', 'ct...]
    dot_general x71 -> x46, matrix products: 277 us -> 60.9 us  [the longest x4 7.39 us: shards(): jnp.einsum('ste,ie->sti', du_b, w_up[s][j], preferred_element_type=f32)]
    ppermute x0 -> x119, starting transfers between devices: none -> 140 us  [pp(): return lax.ppermute(x, axis, [(i, i ^ xor) for i in range(sizes[axis])])]
    pallas_call x0 -> x13, Pallas kernels: none -> 85 us  [the longest x3 30.5 us: adam_segments(): pl.pallas_call(adam_kernel, grid=(2, count // 2), in_specs=[pl.BlockSpec(...]
    reduce_sum x26 -> x16, other arithmetic: 69.9 us -> 12.6 us  [the longest x2 2.27 us: shards(): early[s] = jnp.stack(early[s] + [jnp.sum(dO[s] * y, axis=1)], axis=1)]
  transfers between devices with their start and end apart: 10 -> 119, of which waited for: 9 -> 47; matrix products, arithmetic and copies ran while one was open for 14% -> 20% of each run, Pallas kernels for 0% -> 5%
where the time goes in v1:
time: 810 us; the launch traced here: 801 us
  waiting for transfers between devices  338 us (42%)
  starting transfers between devices  140 us (17%)
  other arithmetic  106 us (13%)
  Pallas kernels  85 us (10%)
  local copies, waits for them, and re-layouts  65.2 us (8%)
  matrix products  60.9 us (8%)
    ppermute x119, waiting for transfers between devices, pp(): return lax.ppermute(x, axis, [(i, i ^ xor) for i in range(sizes[axis])])  338 us
    ppermute x119, starting transfers between devices, pp(): return lax.ppermute(x, axis, [(i, i ^ xor) for i in range(sizes[axis])])  140 us
    pallas_call x3, Pallas kernels, adam_segments(): pl.pallas_call(adam_kernel, grid=(2, count // 2), in_specs=[pl.BlockSpec(...  30.5 us
    pallas_call x1, Pallas kernels, attn_bwd(): pl.pallas_call(functools.partial(attn_bwd_kernel, heads), grid=(S, 2 * T...  30.1 us
    unnamed x267, local copies, waits for them, and re-layouts  20.5 us
    convert_element_type x10, other arithmetic, scatter_add(): (pieces[p].astype(f32) + (after(v, *tie) if tie else v).astype(f32)).asty...  17.7 us
    pallas_call x1, Pallas kernels, attn_fwd(): pl.pallas_call(functools.partial(attn_fwd_kernel, heads, img, live), grid...  16.7 us
  transfers between devices with their start and end apart: 119, of which 47 were waited for; matrix products, arithmetic and copies ran while one was open for 20% of the time, Pallas kernels for 5%

profile of v1, /device:TPU:0, one launch (start us, length us, event | category | flops | bytes accessed | tf_op | source)
XLA Modules:
  0.0 800.6 jit_solution(3310615337324614111)
XLA Ops:
  1.4 7.2 copy.129
  43.5 3.7 collective-permute-done.16.refs_1_
  49.4 4.1 collective-permute-done.12.refs_5_
  56.0 3.8 collective-permute-done.10.refs_3_
  62.3 3.8 collective-permute-done.17.refs_3_
  75.6 4.0 collective-permute-done.21.refs_7_
  81.7 3.7 convert_reduce_fusion
  97.7 13.2 %collective-permute-done.22 = bf16[1,1152,384]{2,1,0:T(8,128)(2,1)} collective-permute-done((bf16[1,1152,384]{2,1,0:T(8,128)(2,1)}, bf16[1,1152,384]{2,1,0:T(8,128)(2,1)}, u32[]{:S(2)}, u32[]{:S(2)}) %collective-permute-start.22) | collective-permute-done | bytes 884768 | tf_op jit(solution)/shard_map/ppermute | solution.py:240
  113.4 16.7 %attn_fwd.1 = (bf16[1,1152,192]{2,1,0:T(8,128)(2,1)}, f32[1,8,1152]{2,1,0:T(8,128)}) custom-call(bf16[1,1152,256]{2,1,0:T(8,128)(2,1)} %fusion.128.q_ref, bf16[1,2,1152,384]{3,2,1,0:T(8,128)(2,1)} %pad_maximum_fusion.3.kv_ref), custom_call_target="tpu_custom_call" | custom-call | flops 5435817984 | bytes 1769472 | tf_op jit(solution)/shard_map/attn_fwd/pallas_call | solution.py:101
  152.5 8.1 %collective-permute-done.24 = bf16[1,144,1536]{2,1,0:T(8,128)(2,1)S(1)} collective-permute-done((bf16[1,144,1536]{2,1,0:T(8,128)(2,1)S(1)}, bf16[1,144,1536]{2,1,0:T(8,128)(2,1)S(1)}, u32[]{:S(2)}, u32[]{:S(2)}) %collective-permute-start.24) | collective-permute-done | bytes 442400 | tf_op jit(solution)/shard_map/ppermute | solution.py:240
  160.6 24.8 %collective-permute-done.25 = bf16[1,144,1536]{2,1,0:T(8,128)(2,1)S(1)} collective-permute-done((bf16[1,144,1536]{2,1,0:T(8,128)(2,1)S(1)}, bf16[1,144,1536]{2,1,0:T(8,128)(2,1)S(1)}, u32[]{:S(2)}, u32[]{:S(2)}) %collective-permute-start.25) | collective-permute-done | bytes 442400 | tf_op jit(solution)/shard_map/ppermute | solution.py:240
  195.9 3.9 collective-permute-done.37.refs_4_
  202.3 5.4 collective-permute-done.27.refs_1_
  213.9 12.1 %collective-permute-done.28.refs_2_ = bf16[1,144,1536]{2,1,0:T(8,128)(2,1)S(1)} collective-permute-done((bf16[1,144,1536]{2,1,0:T(8,128)(2,1)S(1)}, bf16[1,144,1536]{2,1,0:T(8,128)(2,1)S(1)}, u32[]{:S(2)}, u32[]{:S(2)}) %collective-permute-start.28) | collective-permute-done | bytes 442400 | tf_op jit(solution)/shard_map/ppermute | solution.py:240
  237.0 5.4 collective-permute-done.38.refs_5_
  243.9 11.2 %collective-permute-done.36.refs_3_ = bf16[4,192,384]{2,1,0:T(8,128)(2,1)S(1)} collective-permute-done((bf16[4,192,384]{2,1,0:T(8,128)(2,1)S(1)}, bf16[4,192,384]{2,1,0:T(8,128)(2,1)S(1)}, u32[]{:S(2)}, u32[]{:S(2)}) %collective-permute-start.36) | collective-permute-done | bytes 589856 | tf_op jit(solution)/shard_map/ppermute | solution.py:240
  256.5 7.8 collective-permute-done.34.refs_1_
  275.1 4.5 fusion.149
  279.6 7.4 collective-permute-done.45.refs_4_
  309.8 5.2 collective-permute-start.52
  329.6 20.2 %collective-permute-done.52 = bf16[1,144,1536]{2,1,0:T(8,128)(2,1)S(1)} collective-permute-done((bf16[1,144,1536]{2,1,0:T(8,128)(2,1)S(1)}, bf16[1,144,1536]{2,1,0:T(8,128)(2,1)S(1)}, u32[]{:S(2)}, u32[]{:S(2)}) %collective-permute-start.52) | collective-permute-done | bytes 442400 | tf_op jit(solution)/shard_map/ppermute | solution.py:240
  358.5 15.2 %collective-permute-done.54.refs_1_ = bf16[1,144,1536]{2,1,0:T(8,128)(2,1)S(1)} collective-permute-done((bf16[1,144,1536]{2,1,0:T(8,128)(2,1)S(1)}, bf16[1,144,1536]{2,1,0:T(8,128)(2,1)S(1)}, u32[]{:S(2)}, u32[]{:S(2)}) %collective-permute-start.54) | collective-permute-done | bytes 442400 | tf_op jit(solution)/shard_map/ppermute | solution.py:240
  373.7 12.0 %collective-permute-done.55.refs_2_ = bf16[1,144,1536]{2,1,0:T(8,128)(2,1)S(1)} collective-permute-done((bf16[1,144,1536]{2,1,0:T(8,128)(2,1)S(1)}, bf16[1,144,1536]{2,1,0:T(8,128)(2,1)S(1)}, u32[]{:S(2)}, u32[]{:S(2)}) %collective-permute-start.55) | collective-permute-done | bytes 442400 | tf_op jit(solution)/shard_map/ppermute | solution.py:240
  400.8 30.1 %attn_bwd.1 = (bf16[1,1152,192]{2,1,0:T(8,128)(2,1)}, bf16[1,2304,384]{2,1,0:T(8,128)(2,1)}) custom-call(bf16[1,1152,256]{2,1,0:T(8,128)(2,1)} %fusion.128.q_ref, bf16[1,2304,384]{2,1,0:T(8,128)(2,1)} %bitcast.677, bf16[1,1152,192]{2,1,0:T(8,128)(2,1)} %get-tuple-element.102.a_ref, bf16[1,1152,192]{2,1,0:T(8,128)(2,1)} %pad_maximum_fusion.14.da_ref, ...), custom_call_target="tpu_custom_call" | custom-call | flops 10871635968 | bytes 3538944 | tf_op jit(solution)/shard_map/attn_bwd/pallas_call | solution.py:153
  442.0 5.3 collective-permute-done.111
  448.8 11.2 %collective-permute-done.104 = bf16[4,192,384]{2,1,0:T(8,128)(2,1)S(1)} collective-permute-done((bf16[4,192,384]{2,1,0:T(8,128)(2,1)}, bf16[4,192,384]{2,1,0:T(8,128)(2,1)S(1)}, u32[]{:S(2)}, u32[]{:S(2)}) %collective-permute-start.104) | collective-permute-done | bytes 589856 | tf_op jit(solution)/shard_map/ppermute | solution.py:240
  460.0 12.6 %collective-permute-done.105 = bf16[4,192,384]{2,1,0:T(8,128)(2,1)S(1)} collective-permute-done((bf16[4,192,384]{2,1,0:T(8,128)(2,1)}, bf16[4,192,384]{2,1,0:T(8,128)(2,1)S(1)}, u32[]{:S(2)}, u32[]{:S(2)}) %collective-permute-start.105) | collective-permute-done | bytes 589856 | tf_op jit(solution)/shard_map/ppermute | solution.py:240
  486.8 7.7 collective-permute-start.62
  494.5 9.4 %collective-permute-done.103 = bf16[4,192,384]{2,1,0:T(8,128)(2,1)} collective-permute-done((bf16[4,192,384]{2,1,0:T(8,128)(2,1)}, bf16[4,192,384]{2,1,0:T(8,128)(2,1)}, u32[]{:S(2)}, u32[]{:S(2)}) %collective-permute-start.103) | collective-permute-done | bytes 589856 | tf_op jit(solution)/shard_map/ppermute | solution.py:240
  503.9 8.6 %collective-permute-start.63 = (bf16[1,144,1536]{2,1,0:T(8,128)(2,1)S(1)}, bf16[1,144,1536]{2,1,0:T(8,128)(2,1)S(1)}, u32[]{:S(2)}, u32[]{:S(2)}) collective-permute-start(bf16[1,144,1536]{2,1,0:T(8,128)(2,1)S(1)} %get-tuple-element.316), channel_id=1, source_target_pairs={{0,1},{1,0},{2,3},{3,2},{4,5},{5,4},{6,7},{7,6},{8,9},{9,8},{10,11... | collective-permute-start | bytes 1327112 | tf_op jit(solution)/shard_map/ppermute | solution.py:240
  520.5 5.3 collective-permute-done.62
  525.8 6.2 collective-permute-done.63
  550.2 23.0 %collective-permute-done.65.refs_2_ = bf16[1,144,1536]{2,1,0:T(8,128)(2,1)S(1)} collective-permute-done((bf16[1,144,1536]{2,1,0:T(8,128)(2,1)S(1)}, bf16[1,144,1536]{2,1,0:T(8,128)(2,1)S(1)}, u32[]{:S(2)}, u32[]{:S(2)}) %collective-permute-start.65) | collective-permute-done | bytes 442400 | tf_op jit(solution)/shard_map/ppermute | solution.py:240
  601.6 23.1 %collective-permute-done.74 = bf16[1,144,1536]{2,1,0:T(8,128)(2,1)} collective-permute-done((bf16[1,144,1536]{2,1,0:T(8,128)(2,1)}, bf16[1,144,1536]{2,1,0:T(8,128)(2,1)}, u32[]{:S(2)}, u32[]{:S(2)}) %collective-permute-start.74) | collective-permute-done | bytes 442400 | tf_op jit(solution)/shard_map/ppermute | solution.py:240
  637.4 5.4 collective-permute-done.91
  643.5 5.6 collective-permute-done.98
  649.8 5.6 collective-permute-done.92
  661.8 4.4 collective-permute-done.96
  680.3 16.8 %collective-permute-done.77.refs_2_ = bf16[1,144,1536]{2,1,0:T(8,128)(2,1)S(1)} collective-permute-done((bf16[1,144,1536]{2,1,0:T(8,128)(2,1)S(1)}, bf16[1,144,1536]{2,1,0:T(8,128)(2,1)S(1)}, u32[]{:S(2)}, u32[]{:S(2)}) %collective-permute-start.77) | collective-permute-done | bytes 442400 | tf_op jit(solution)/shard_map/ppermute | solution.py:240
  698.8 8.6 %collective-permute-start.86 = (f32[40,1536]{1,0:T(8,128)S(1)}, f32[40,1536]{1,0:T(8,128)S(1)}, u32[]{:S(2)}, u32[]{:S(2)}) collective-permute-start(f32[40,1536]{1,0:T(8,128)S(1)} %add.897), channel_id=1, source_target_pairs={{0,1},{1,0},{2,3},{3,2},{4,5},{5,4},{6,7},{7,6},{8,9},{9,8},{10,11... | collective-permute-start | bytes 737288 | tf_op jit(solution)/shard_map/ppermute | solution.py:240
  709.9 3.6 collective-permute-done.86
  720.6 6.5 collective-permute-done.87
  736.6 3.8 broadcast_select_fusion.1
  750.6 3.7 collective-permute-done.117
  764.3 4.0 copy-done
  770.0 13.1 %adam.3 = (f32[2,18,192,384]{3,2,1,0:T(8,128)}, f32[2,18,192,384]{3,2,1,0:T(8,128)}, f32[2,18,192,384]{3,2,1,0:T(8,128)}, f32[2,18,192,384]{3,2,1,0:T(8,128)}) custom-call(f32[2,8]{1,0:T(2,128)S(1)} %slice.540.f_ref, bf16[2,8,192,384]{3,2,1,0:T(8,128)(2,1)S(1)} %bitcast.579, f32[2,18,192,384]{3,2,1,0:T(8,128)S(1)} %bitcast.576, ...), custom_call_target="tpu_custom_call" | custom-call | tf_op jit(solution)/shard_map/adam/pallas_call | solution.py:211
  783.1 7.4 adam.4
  790.4 10.0 %adam.5 = (f32[2,18,192,384]{3,2,1,0:T(8,128)}, f32[2,18,192,384]{3,2,1,0:T(8,128)}, f32[2,18,192,384]{3,2,1,0:T(8,128)}, f32[2,18,192,384]{3,2,1,0:T(8,128)}) custom-call(f32[2,6]{1,0:T(2,128)S(1)} %bitcast.586, f32[2,6,192,384]{3,2,1,0:T(8,128)S(1)} %get-tuple-element.397.g_ref, ...), custom_call_target="tpu_custom_call", output_to_operand_aliasing={{0}: (5, {}), {1}: (6, {}), {2}: (7, {}), {3}: (8, {})} | custom-call | tf_op jit(solution)/shard_map/adam/pallas_call | solution.py:211
  (774 shorter events, 351.2 us)
Async XLA Ops:
  11.7 70.0 %collective-permute-start = (bf16[1,1024,1536]{2,1,0:T(8,128)(2,1)}, bf16[1,1024,1536]{2,1,0:T(8,128)(2,1)}, u32[]{:S(2)}, u32[]{:S(2)}) collective-permute-start(bf16[1,1024,1536]{2,1,0:T(8,128)(2,1)} %param.20), channel_id=1, source_target_pairs={{0,8},{8,0},{16,24},{24,16},{1,9},{9,1},{17,25},{25,17},{2,10},{10... | collective-permute-start | bytes 9437192 | tf_op jit(solution)/shard_map/ppermute | solution.py:240
  140.6 49.3 %collective-permute-start.42 = (bf16[1,77,1536]{2,1,0:T(8,128)(2,1)}, bf16[1,77,1536]{2,1,0:T(8,128)(2,1)}, u32[]{:S(2)}, u32[]{:S(2)}) collective-permute-start(bf16[1,77,1536]{2,1,0:T(8,128)(2,1)} %param.31), channel_id=1, source_target_pairs={{0,8},{8,0},{16,24},{24,16},{1,9},{9,1},{17,25},{25,17},{2,10},{10... | collective-permute-start | bytes 709640 | tf_op jit(solution)/shard_map/ppermute | solution.py:240
  140.6 51.4 %collective-permute-start.41 = (bf16[1,1024,1536]{2,1,0:T(8,128)(2,1)}, bf16[1,1024,1536]{2,1,0:T(8,128)(2,1)}, u32[]{:S(2)}, u32[]{:S(2)}) collective-permute-start(bf16[1,1024,1536]{2,1,0:T(8,128)(2,1)} %param.30), channel_id=1, source_target_pairs={{0,8},{8,0},{16,24},{24,16},{1,9},{9,1},{17,25},{25,17},{2,10},{10... | collective-permute-start | bytes 9437192 | tf_op jit(solution)/shard_map/ppermute | solution.py:240
  147.1 38.2 %collective-permute-start.25 = (bf16[1,144,1536]{2,1,0:T(8,128)(2,1)S(1)}, bf16[1,144,1536]{2,1,0:T(8,128)(2,1)S(1)}, u32[]{:S(2)}, u32[]{:S(2)}) collective-permute-start(bf16[1,144,1536]{2,1,0:T(8,128)(2,1)S(1)} %get-tuple-element.323), channel_id=1, source_target_pairs={{0,2},{1,3},{2,0},{3,1},{4,6},{5,7},{6,4},{7,5},{8,10},{9,11},{10,... | collective-permute-start | bytes 1327112 | tf_op jit(solution)/shard_map/ppermute | solution.py:240
  147.1 38.6 %collective-permute-start.26 = (bf16[1,144,1536]{2,1,0:T(8,128)(2,1)S(1)}, bf16[1,144,1536]{2,1,0:T(8,128)(2,1)S(1)}, u32[]{:S(2)}, u32[]{:S(2)}) collective-permute-start(bf16[1,144,1536]{2,1,0:T(8,128)(2,1)S(1)} %get-tuple-element.322), channel_id=1, source_target_pairs={{0,1},{1,0},{2,3},{3,2},{4,5},{5,4},{6,7},{7,6},{8,9},{9,8},{10,11... | collective-permute-start | bytes 1327112 | tf_op jit(solution)/shard_map/ppermute | solution.py:240
  160.6 32.1 %collective-permute-start.39 = (bf16[4,192,384]{2,1,0:T(8,128)(2,1)S(1)}, bf16[4,192,384]{2,1,0:T(8,128)(2,1)}, u32[]{:S(2)}, u32[]{:S(2)}) collective-permute-start(bf16[4,192,384]{2,1,0:T(8,128)(2,1)S(1)} %get-tuple-element.114.refs_2_), channel_id=1, source_target_pairs={{0,16},{8,24},{16,0},{24,8},{1,17},{9,25},{17,1},{25,9},{2,18},{10... | collective-permute-start | bytes 1769480 | tf_op jit(solution)/shard_map/ppermute | solution.py:240
  192.7 33.2 %collective-permute-start.28 = (bf16[1,144,1536]{2,1,0:T(8,128)(2,1)S(1)}, bf16[1,144,1536]{2,1,0:T(8,128)(2,1)S(1)}, u32[]{:S(2)}, u32[]{:S(2)}) collective-permute-start(bf16[1,144,1536]{2,1,0:T(8,128)(2,1)S(1)} %pad_maximum_fusion.17.refs_0_), channel_id=1, source_target_pairs={{0,2},{1,3},{2,0},{3,1},{4,6},{5,7},{6,4},{7,5},{8,10},{9,11},{10,... | collective-permute-start | bytes 1327112 | tf_op jit(solution)/shard_map/ppermute | solution.py:240
  199.8 27.4 %collective-permute-start.29 = (bf16[1,144,1536]{2,1,0:T(8,128)(2,1)S(1)}, bf16[1,144,1536]{2,1,0:T(8,128)(2,1)S(1)}, u32[]{:S(2)}, u32[]{:S(2)}) collective-permute-start(bf16[1,144,1536]{2,1,0:T(8,128)(2,1)S(1)} %pad_maximum_fusion.17.refs_0_), channel_id=1, source_target_pairs={{0,3},{1,2},{2,1},{3,0},{4,7},{5,6},{6,5},{7,4},{8,11},{9,10},{10,... | collective-permute-start | bytes 1327112 | tf_op jit(solution)/shard_map/ppermute | solution.py:240
  227.2 27.8 %collective-permute-start.36 = (bf16[4,192,384]{2,1,0:T(8,128)(2,1)S(1)}, bf16[4,192,384]{2,1,0:T(8,128)(2,1)S(1)}, u32[]{:S(2)}, u32[]{:S(2)}) collective-permute-start(bf16[4,192,384]{2,1,0:T(8,128)(2,1)S(1)} %get-tuple-element.114.refs_2_), channel_id=1, source_target_pairs={{0,4},{4,0},{1,5},{5,1},{2,6},{6,2},{3,7},{7,3},{8,12},{12,8},{9,1... | collective-permute-start | bytes 1769480 | tf_op jit(solution)/shard_map/ppermute | solution.py:240
  228.0 36.4 %collective-permute-start.34 = (bf16[4,192,384]{2,1,0:T(8,128)(2,1)S(1)}, bf16[4,192,384]{2,1,0:T(8,128)(2,1)S(1)}, u32[]{:S(2)}, u32[]{:S(2)}) collective-permute-start(bf16[4,192,384]{2,1,0:T(8,128)(2,1)S(1)} %get-tuple-element.110.refs_0_), channel_id=1, source_target_pairs={{0,4},{4,0},{1,5},{5,1},{2,6},{6,2},{3,7},{7,3},{8,12},{12,8},{9,1... | collective-permute-start | bytes 1769480 | tf_op jit(solution)/shard_map/ppermute | solution.py:240
  233.7 38.5 %collective-permute-start.48 = (bf16[4,192,384]{2,1,0:T(8,128)(2,1)S(1)}, bf16[4,192,384]{2,1,0:T(8,128)(2,1)S(1)}, u32[]{:S(2)}, u32[]{:S(2)}) collective-permute-start(bf16[4,192,384]{2,1,0:T(8,128)(2,1)S(1)} %collective-permute-done.44.refs_3_), channel_id=1, source_target_pairs={{0,16},{8,24},{16,0},{24,8},{1,17},{9,25},{17,1},{25,9},{2,18},{10... | collective-permute-start | bytes 1769480 | tf_op jit(solution)/shard_map/ppermute | solution.py:240
  236.6 35.6 %collective-permute-start.47 = (bf16[4,192,384]{2,1,0:T(8,128)(2,1)S(1)}, bf16[4,192,384]{2,1,0:T(8,128)(2,1)S(1)}, u32[]{:S(2)}, u32[]{:S(2)}) collective-permute-start(bf16[4,192,384]{2,1,0:T(8,128)(2,1)S(1)} %get-tuple-element.128.refs_2_), channel_id=1, source_target_pairs={{0,16},{8,24},{16,0},{24,8},{1,17},{9,25},{17,1},{25,9},{2,18},{10... | collective-permute-start | bytes 1769480 | tf_op jit(solution)/shard_map/ppermute | solution.py:240
  242.4 32.7 %collective-permute-start.46 = (bf16[4,192,384]{2,1,0:T(8,128)(2,1)S(1)}, bf16[4,192,384]{2,1,0:T(8,128)(2,1)S(1)}, u32[]{:S(2)}, u32[]{:S(2)}) collective-permute-start(bf16[4,192,384]{2,1,0:T(8,128)(2,1)S(1)} %collective-permute-done.43.refs_1_), channel_id=1, source_target_pairs={{0,16},{8,24},{16,0},{24,8},{1,17},{9,25},{17,1},{25,9},{2,18},{10... | collective-permute-start | bytes 1769480 | tf_op jit(solution)/shard_map/ppermute | solution.py:240
  255.1 32.0 %collective-permute-start.45 = (bf16[4,192,384]{2,1,0:T(8,128)(2,1)S(1)}, bf16[4,192,384]{2,1,0:T(8,128)(2,1)S(1)}, u32[]{:S(2)}, u32[]{:S(2)}) collective-permute-start(bf16[4,192,384]{2,1,0:T(8,128)(2,1)S(1)} %get-tuple-element.124.refs_0_), channel_id=1, source_target_pairs={{0,16},{8,24},{16,0},{24,8},{1,17},{9,25},{17,1},{25,9},{2,18},{10... | collective-permute-start | bytes 1769480 | tf_op jit(solution)/shard_map/ppermute | solution.py:240
  309.8 40.1 %collective-permute-start.52 = (bf16[1,144,1536]{2,1,0:T(8,128)(2,1)S(1)}, bf16[1,144,1536]{2,1,0:T(8,128)(2,1)S(1)}, u32[]{:S(2)}, u32[]{:S(2)}) collective-permute-start(bf16[1,144,1536]{2,1,0:T(8,128)(2,1)S(1)} %get-tuple-element.320), channel_id=1, source_target_pairs={{0,2},{1,3},{2,0},{3,1},{4,6},{5,7},{6,4},{7,5},{8,10},{9,11},{10,... | collective-permute-start | bytes 1327112 | tf_op jit(solution)/shard_map/ppermute | solution.py:240
  314.9 34.9 %collective-permute-start.53 = (bf16[1,144,1536]{2,1,0:T(8,128)(2,1)S(1)}, bf16[1,144,1536]{2,1,0:T(8,128)(2,1)S(1)}, u32[]{:S(2)}, u32[]{:S(2)}) collective-permute-start(bf16[1,144,1536]{2,1,0:T(8,128)(2,1)S(1)} %get-tuple-element.319), channel_id=1, source_target_pairs={{0,1},{1,0},{2,3},{3,2},{4,5},{5,4},{6,7},{7,6},{8,9},{9,8},{10,11... | collective-permute-start | bytes 1327112 | tf_op jit(solution)/shard_map/ppermute | solution.py:240
  325.7 105.1 %collective-permute-start.107 = (bf16[4,192,384]{2,1,0:T(8,128)(2,1)}, bf16[4,192,384]{2,1,0:T(8,128)(2,1)}, u32[]{:S(2)}, u32[]{:S(2)}) collective-permute-start(bf16[4,192,384]{2,1,0:T(8,128)(2,1)} %get-tuple-element.272), channel_id=1, source_target_pairs={{0,16},{8,24},{16,0},{24,8},{1,17},{9,25},{17,1},{25,9},{2,18},{10... | collective-permute-start | bytes 1769480 | tf_op jit(solution)/shard_map/ppermute | solution.py:240
  352.7 33.0 %collective-permute-start.55 = (bf16[1,144,1536]{2,1,0:T(8,128)(2,1)S(1)}, bf16[1,144,1536]{2,1,0:T(8,128)(2,1)S(1)}, u32[]{:S(2)}, u32[]{:S(2)}) collective-permute-start(bf16[1,144,1536]{2,1,0:T(8,128)(2,1)S(1)} %pad_maximum_fusion.18.refs_0_), channel_id=1, source_target_pairs={{0,2},{1,3},{2,0},{3,1},{4,6},{5,7},{6,4},{7,5},{8,10},{9,11},{10,... | collective-permute-start | bytes 1327112 | tf_op jit(solution)/shard_map/ppermute | solution.py:240
  355.7 30.1 %collective-permute-start.56 = (bf16[1,144,1536]{2,1,0:T(8,128)(2,1)S(1)}, bf16[1,144,1536]{2,1,0:T(8,128)(2,1)S(1)}, u32[]{:S(2)}, u32[]{:S(2)}) collective-permute-start(bf16[1,144,1536]{2,1,0:T(8,128)(2,1)S(1)} %pad_maximum_fusion.18.refs_0_), channel_id=1, source_target_pairs={{0,3},{1,2},{2,1},{3,0},{4,7},{5,6},{6,5},{7,4},{8,11},{9,10},{10,... | collective-permute-start | bytes 1327112 | tf_op jit(solution)/shard_map/ppermute | solution.py:240
  358.4 34.9 %collective-permute-start.57 = (bf16[1,144,1536]{2,1,0:T(8,128)(2,1)S(1)}, bf16[1,144,1536]{2,1,0:T(8,128)(2,1)S(1)}, u32[]{:S(2)}, u32[]{:S(2)}) collective-permute-start(bf16[1,144,1536]{2,1,0:T(8,128)(2,1)S(1)} %pad_maximum_fusion.18.refs_0_), channel_id=1, source_target_pairs={{0,8},{8,0},{16,24},{24,16},{1,9},{9,1},{17,25},{25,17},{2,10},{10... | collective-permute-start | bytes 1327112 | tf_op jit(solution)/shard_map/ppermute | solution.py:240
  393.3 37.7 %collective-permute-start.108 = (bf16[4,192,384]{2,1,0:T(8,128)(2,1)}, bf16[4,192,384]{2,1,0:T(8,128)(2,1)}, u32[]{:S(2)}, u32[]{:S(2)}) collective-permute-start(bf16[4,192,384]{2,1,0:T(8,128)(2,1)} %get-tuple-element.274), channel_id=1, source_target_pairs={{0,16},{8,24},{16,0},{24,8},{1,17},{9,25},{17,1},{25,9},{2,18},{10... | collective-permute-start | bytes 1769480 | tf_op jit(solution)/shard_map/ppermute | solution.py:240
  394.9 37.5 %collective-permute-start.101 = (bf16[4,192,384]{2,1,0:T(8,128)(2,1)}, bf16[4,192,384]{2,1,0:T(8,128)(2,1)}, u32[]{:S(2)}, u32[]{:S(2)}) collective-permute-start(bf16[4,192,384]{2,1,0:T(8,128)(2,1)} %get-tuple-element.271), channel_id=1, source_target_pairs={{0,16},{8,24},{16,0},{24,8},{1,17},{9,25},{17,1},{25,9},{2,18},{10... | collective-permute-start | bytes 1769480 | tf_op jit(solution)/shard_map/ppermute | solution.py:240
  395.4 38.8 %collective-permute-start.102 = (bf16[4,192,384]{2,1,0:T(8,128)(2,1)}, bf16[4,192,384]{2,1,0:T(8,128)(2,1)}, u32[]{:S(2)}, u32[]{:S(2)}) collective-permute-start(bf16[4,192,384]{2,1,0:T(8,128)(2,1)} %get-tuple-element.273), channel_id=1, source_target_pairs={{0,16},{8,24},{16,0},{24,8},{1,17},{9,25},{17,1},{25,9},{2,18},{10... | collective-permute-start | bytes 1769480 | tf_op jit(solution)/shard_map/ppermute | solution.py:240
  397.0 41.5 %collective-permute-start.110 = (bf16[4,192,384]{2,1,0:T(8,128)(2,1)}, bf16[4,192,384]{2,1,0:T(8,128)(2,1)}, u32[]{:S(2)}, u32[]{:S(2)}) collective-permute-start(bf16[4,192,384]{2,1,0:T(8,128)(2,1)} %get-tuple-element.279), channel_id=1, source_target_pairs={{0,4},{4,0},{1,5},{5,1},{2,6},{6,2},{3,7},{7,3},{8,12},{12,8},{9,1... | collective-permute-start | bytes 1769480 | tf_op jit(solution)/shard_map/ppermute | solution.py:240
  430.8 51.4 %collective-permute-start.50 = (bf16[4,1,144,1536]{3,2,1,0:T(8,128)(2,1)}, bf16[4,1,144,1536]{3,2,1,0:T(8,128)(2,1)}, u32[]{:S(2)}, u32[]{:S(2)}) collective-permute-start(bf16[4,1,144,1536]{3,2,1,0:T(8,128)(2,1)} %fusion.26), channel_id=1, source_target_pairs={{0,8},{8,0},{16,24},{24,16},{1,9},{9,1},{17,25},{25,17},{2,10},{10... | collective-permute-start | bytes 5308424 | tf_op jit(solution)/shard_map/ppermute | solution.py:240
  432.5 27.5 %collective-permute-start.104 = (bf16[4,192,384]{2,1,0:T(8,128)(2,1)}, bf16[4,192,384]{2,1,0:T(8,128)(2,1)S(1)}, u32[]{:S(2)}, u32[]{:S(2)}) collective-permute-start(bf16[4,192,384]{2,1,0:T(8,128)(2,1)} %get-tuple-element.277), channel_id=1, source_target_pairs={{0,4},{4,0},{1,5},{5,1},{2,6},{6,2},{3,7},{7,3},{8,12},{12,8},{9,1... | collective-permute-start | bytes 1769480 | tf_op jit(solution)/shard_map/ppermute | solution.py:240
  434.2 38.5 %collective-permute-start.105 = (bf16[4,192,384]{2,1,0:T(8,128)(2,1)}, bf16[4,192,384]{2,1,0:T(8,128)(2,1)S(1)}, u32[]{:S(2)}, u32[]{:S(2)}) collective-permute-start(bf16[4,192,384]{2,1,0:T(8,128)(2,1)} %get-tuple-element.280), channel_id=1, source_target_pairs={{0,4},{4,0},{1,5},{5,1},{2,6},{6,2},{3,7},{7,3},{8,12},{12,8},{9,1... | collective-permute-start | bytes 1769480 | tf_op jit(solution)/shard_map/ppermute | solution.py:240
  438.5 98.6 %collective-permute-start.71 = (bf16[1,1152,384]{2,1,0:T(8,128)(2,1)}, bf16[1,1152,384]{2,1,0:T(8,128)(2,1)}, u32[]{:S(2)}, u32[]{:S(2)}) collective-permute-start(bf16[1,1152,384]{2,1,0:T(8,128)(2,1)} %slice_bitcast_fusion), channel_id=1, source_target_pairs={{0,4},{4,0},{1,5},{5,1},{2,6},{6,2},{3,7},{7,3},{8,12},{12,8},{9,1... | collective-permute-start | bytes 2654216 | tf_op jit(solution)/shard_map/ppermute | solution.py:240
  447.3 56.5 %collective-permute-start.103 = (bf16[4,192,384]{2,1,0:T(8,128)(2,1)}, bf16[4,192,384]{2,1,0:T(8,128)(2,1)}, u32[]{:S(2)}, u32[]{:S(2)}) collective-permute-start(bf16[4,192,384]{2,1,0:T(8,128)(2,1)} %fusion.67), channel_id=1, source_target_pairs={{0,4},{4,0},{1,5},{5,1},{2,6},{6,2},{3,7},{7,3},{8,12},{12,8},{9,1... | collective-permute-start | bytes 1769480 | tf_op jit(solution)/shard_map/ppermute | solution.py:240
  474.6 41.0 %collective-permute-start.106 = (bf16[4,192,384]{2,1,0:T(8,128)(2,1)}, bf16[4,192,384]{2,1,0:T(8,128)(2,1)}, u32[]{:S(2)}, u32[]{:S(2)}) collective-permute-start(bf16[4,192,384]{2,1,0:T(8,128)(2,1)} %fusion.65), channel_id=1, source_target_pairs={{0,16},{8,24},{16,0},{24,8},{1,17},{9,25},{17,1},{25,9},{2,18},{10... | collective-permute-start | bytes 1769480 | tf_op jit(solution)/shard_map/ppermute | solution.py:240
  484.4 35.7 %collective-permute-start.61 = (bf16[1,144,1536]{2,1,0:T(8,128)(2,1)S(1)}, bf16[1,144,1536]{2,1,0:T(8,128)(2,1)S(1)}, u32[]{:S(2)}, u32[]{:S(2)}) collective-permute-start(bf16[1,144,1536]{2,1,0:T(8,128)(2,1)S(1)} %get-tuple-element.315), channel_id=1, source_target_pairs={{0,3},{1,2},{2,1},{3,0},{4,7},{5,6},{6,5},{7,4},{8,11},{9,10},{10,... | collective-permute-start | bytes 1327112 | tf_op jit(solution)/shard_map/ppermute | solution.py:240
  486.8 39.0 %collective-permute-start.62 = (bf16[1,144,1536]{2,1,0:T(8,128)(2,1)S(1)}, bf16[1,144,1536]{2,1,0:T(8,128)(2,1)S(1)}, u32[]{:S(2)}, u32[]{:S(2)}) collective-permute-start(bf16[1,144,1536]{2,1,0:T(8,128)(2,1)S(1)} %get-tuple-element.317), channel_id=1, source_target_pairs={{0,2},{1,3},{2,0},{3,1},{4,6},{5,7},{6,4},{7,5},{8,10},{9,11},{10,... | collective-permute-start | bytes 1327112 | tf_op jit(solution)/shard_map/ppermute | solution.py:240
  503.9 28.1 %collective-permute-start.63 = (bf16[1,144,1536]{2,1,0:T(8,128)(2,1)S(1)}, bf16[1,144,1536]{2,1,0:T(8,128)(2,1)S(1)}, u32[]{:S(2)}, u32[]{:S(2)}) collective-permute-start(bf16[1,144,1536]{2,1,0:T(8,128)(2,1)S(1)} %get-tuple-element.316), channel_id=1, source_target_pairs={{0,1},{1,0},{2,3},{3,2},{4,5},{5,4},{6,7},{7,6},{8,9},{9,8},{10,11... | collective-permute-start | bytes 1327112 | tf_op jit(solution)/shard_map/ppermute | solution.py:240
  515.7 34.0 %collective-permute-start.109 = (bf16[4,192,384]{2,1,0:T(8,128)(2,1)}, bf16[4,192,384]{2,1,0:T(8,128)(2,1)}, u32[]{:S(2)}, u32[]{:S(2)}) collective-permute-start(bf16[4,192,384]{2,1,0:T(8,128)(2,1)} %get-tuple-element.270), channel_id=1, source_target_pairs={{0,4},{4,0},{1,5},{5,1},{2,6},{6,2},{3,7},{7,3},{8,12},{12,8},{9,1... | collective-permute-start | bytes 1769480 | tf_op jit(solution)/shard_map/ppermute | solution.py:240
  520.0 53.7 %collective-permute-start.112 = (bf16[4,192,384]{2,1,0:T(8,128)(2,1)}, bf16[4,192,384]{2,1,0:T(8,128)(2,1)}, u32[]{:S(2)}, u32[]{:S(2)}) collective-permute-start(bf16[4,192,384]{2,1,0:T(8,128)(2,1)} %get-tuple-element.276), channel_id=1, source_target_pairs={{0,16},{8,24},{16,0},{24,8},{1,17},{9,25},{17,1},{25,9},{2,18},{10... | collective-permute-start | bytes 1769480 | tf_op jit(solution)/shard_map/ppermute | solution.py:240
  537.0 36.2 %collective-permute-start.65 = (bf16[1,144,1536]{2,1,0:T(8,128)(2,1)S(1)}, bf16[1,144,1536]{2,1,0:T(8,128)(2,1)S(1)}, u32[]{:S(2)}, u32[]{:S(2)}) collective-permute-start(bf16[1,144,1536]{2,1,0:T(8,128)(2,1)S(1)} %pad_maximum_fusion.19.refs_0_), channel_id=1, source_target_pairs={{0,2},{1,3},{2,0},{3,1},{4,6},{5,7},{6,4},{7,5},{8,10},{9,11},{10,... | collective-permute-start | bytes 1327112 | tf_op jit(solution)/shard_map/ppermute | solution.py:240
  537.1 36.1 %collective-permute-start.64 = (bf16[1,144,1536]{2,1,0:T(8,128)(2,1)S(1)}, bf16[1,144,1536]{2,1,0:T(8,128)(2,1)S(1)}, u32[]{:S(2)}, u32[]{:S(2)}) collective-permute-start(bf16[1,144,1536]{2,1,0:T(8,128)(2,1)S(1)} %pad_maximum_fusion.19.refs_0_), channel_id=1, source_target_pairs={{0,1},{1,0},{2,3},{3,2},{4,5},{5,4},{6,7},{7,6},{8,9},{9,8},{10,11... | collective-permute-start | bytes 1327112 | tf_op jit(solution)/shard_map/ppermute | solution.py:240
  549.6 28.6 %collective-permute-start.67 = (bf16[1,144,1536]{2,1,0:T(8,128)(2,1)S(1)}, bf16[1,144,1536]{2,1,0:T(8,128)(2,1)S(1)}, u32[]{:S(2)}, u32[]{:S(2)}) collective-permute-start(bf16[1,144,1536]{2,1,0:T(8,128)(2,1)S(1)} %pad_maximum_fusion.19.refs_0_), channel_id=1, source_target_pairs={{0,8},{8,0},{16,24},{24,16},{1,9},{9,1},{17,25},{25,17},{2,10},{10... | collective-permute-start | bytes 1327112 | tf_op jit(solution)/shard_map/ppermute | solution.py:240
  549.7 31.9 %collective-permute-start.72 = (bf16[4,1,144,1536]{3,2,1,0:T(8,128)(2,1)S(1)}, bf16[4,1,144,1536]{3,2,1,0:T(8,128)(2,1)S(1)}, u32[]{:S(2)}, u32[]{:S(2)}) collective-permute-start(bf16[4,1,144,1536]{3,2,1,0:T(8,128)(2,1)S(1)} %fusion.22), channel_id=1, source_target_pairs={{0,8},{8,0},{16,24},{24,16},{1,9},{9,1},{17,25},{25,17},{2,10},{10... | collective-permute-start | bytes 5308424 | tf_op jit(solution)/shard_map/ppermute | solution.py:240
  586.8 37.9 %collective-permute-start.74 = (bf16[1,144,1536]{2,1,0:T(8,128)(2,1)}, bf16[1,144,1536]{2,1,0:T(8,128)(2,1)}, u32[]{:S(2)}, u32[]{:S(2)}) collective-permute-start(bf16[1,144,1536]{2,1,0:T(8,128)(2,1)} %get-tuple-element.314), channel_id=1, source_target_pairs={{0,2},{1,3},{2,0},{3,1},{4,6},{5,7},{6,4},{7,5},{8,10},{9,11},{10,... | collective-permute-start | bytes 1327112 | tf_op jit(solution)/shard_map/ppermute | solution.py:240
  586.8 38.4 %collective-permute-start.75 = (bf16[1,144,1536]{2,1,0:T(8,128)(2,1)}, bf16[1,144,1536]{2,1,0:T(8,128)(2,1)}, u32[]{:S(2)}, u32[]{:S(2)}) collective-permute-start(bf16[1,144,1536]{2,1,0:T(8,128)(2,1)} %get-tuple-element.313), channel_id=1, source_target_pairs={{0,1},{1,0},{2,3},{3,2},{4,5},{5,4},{6,7},{7,6},{8,9},{9,8},{10,11... | collective-permute-start | bytes 1327112 | tf_op jit(solution)/shard_map/ppermute | solution.py:240
  596.9 35.6 %collective-permute-start.94 = (bf16[2,192,384]{2,1,0:T(8,128)(2,1)}, bf16[2,192,384]{2,1,0:T(8,128)(2,1)}, u32[]{:S(2)}, u32[]{:S(2)}) collective-permute-start(bf16[2,192,384]{2,1,0:T(8,128)(2,1)} %get-tuple-element.294), channel_id=1, source_target_pairs={{0,16},{8,24},{16,0},{24,8},{1,17},{9,25},{17,1},{25,9},{2,18},{10... | collective-permute-start | bytes 884744 | tf_op jit(solution)/shard_map/ppermute | solution.py:240
  597.5 35.9 %collective-permute-start.88 = (bf16[2,192,384]{2,1,0:T(8,128)(2,1)}, bf16[2,192,384]{2,1,0:T(8,128)(2,1)}, u32[]{:S(2)}, u32[]{:S(2)}) collective-permute-start(bf16[2,192,384]{2,1,0:T(8,128)(2,1)} %get-tuple-element.292), channel_id=1, source_target_pairs={{0,16},{8,24},{16,0},{24,8},{1,17},{9,25},{17,1},{25,9},{2,18},{10... | collective-permute-start | bytes 884744 | tf_op jit(solution)/shard_map/ppermute | solution.py:240
  601.0 33.7 %collective-permute-start.95 = (bf16[2,192,384]{2,1,0:T(8,128)(2,1)}, bf16[2,192,384]{2,1,0:T(8,128)(2,1)}, u32[]{:S(2)}, u32[]{:S(2)}) collective-permute-start(bf16[2,192,384]{2,1,0:T(8,128)(2,1)} %get-tuple-element.295), channel_id=1, source_target_pairs={{0,16},{8,24},{16,0},{24,8},{1,17},{9,25},{17,1},{25,9},{2,18},{10... | collective-permute-start | bytes 884744 | tf_op jit(solution)/shard_map/ppermute | solution.py:240
  635.4 37.4 %collective-permute-start.113 = (bf16[8,192,384]{2,1,0:T(8,128)(2,1)}, bf16[8,192,384]{2,1,0:T(8,128)(2,1)S(1)}, u32[]{:S(2)}, u32[]{:S(2)}) collective-permute-start(bf16[8,192,384]{2,1,0:T(8,128)(2,1)} %pad_maximum_fusion.9), channel_id=1, source_target_pairs={{0,8},{8,0},{16,24},{24,16},{1,9},{9,1},{17,25},{25,17},{2,10},{10... | collective-permute-start | bytes 3538952 | tf_op jit(solution)/shard_map/ppermute | solution.py:240
  666.1 31.0 %collective-permute-start.77 = (bf16[1,144,1536]{2,1,0:T(8,128)(2,1)S(1)}, bf16[1,144,1536]{2,1,0:T(8,128)(2,1)S(1)}, u32[]{:S(2)}, u32[]{:S(2)}) collective-permute-start(bf16[1,144,1536]{2,1,0:T(8,128)(2,1)S(1)} %pad_maximum_fusion.20.refs_0_), channel_id=1, source_target_pairs={{0,2},{1,3},{2,0},{3,1},{4,6},{5,7},{6,4},{7,5},{8,10},{9,11},{10,... | collective-permute-start | bytes 1327112 | tf_op jit(solution)/shard_map/ppermute | solution.py:240
  667.5 29.6 %collective-permute-start.78 = (bf16[1,144,1536]{2,1,0:T(8,128)(2,1)S(1)}, bf16[1,144,1536]{2,1,0:T(8,128)(2,1)S(1)}, u32[]{:S(2)}, u32[]{:S(2)}) collective-permute-start(bf16[1,144,1536]{2,1,0:T(8,128)(2,1)S(1)} %pad_maximum_fusion.20.refs_0_), channel_id=1, source_target_pairs={{0,3},{1,2},{2,1},{3,0},{4,7},{5,6},{6,5},{7,4},{8,11},{9,10},{10,... | collective-permute-start | bytes 1327112 | tf_op jit(solution)/shard_map/ppermute | solution.py:240
  680.3 37.1 %collective-permute-start.79 = (bf16[1,144,1536]{2,1,0:T(8,128)(2,1)S(1)}, bf16[1,144,1536]{2,1,0:T(8,128)(2,1)S(1)}, u32[]{:S(2)}, u32[]{:S(2)}) collective-permute-start(bf16[1,144,1536]{2,1,0:T(8,128)(2,1)S(1)} %pad_maximum_fusion.20.refs_0_), channel_id=1, source_target_pairs={{0,8},{8,0},{16,24},{24,16},{1,9},{9,1},{17,25},{25,17},{2,10},{10... | collective-permute-start | bytes 1327112 | tf_op jit(solution)/shard_map/ppermute | solution.py:240
  (201 other events, 3088.4 us)

commit v2 on v1

v2 whole, which is shorter than its diff:
```python
import functools
import jax
import jax.numpy as jnp
from jax import lax
from jax.experimental import pallas as pl
from jax.experimental.pallas import tpu as pltpu
from jax.sharding import PartitionSpec as P

DH = 64
NT = (((1,), (1,)), ((), ()))
TN = (((0,), (0,)), ((), ()))
NN = (((1,), (0,)), ((), ()))
bf = jnp.bfloat16
f32 = jnp.float32

beta_one = 0.9
beta_two = 0.95
learn_rate = 0.1
decay_rate = 0.1
adam_eps = 1e-08
adam_step = 10.0
norm_eps = 1e-06
gelu_coef = 0.044715
root_two_pi = 0.7978845608028654
clip_unit = 0.0001
clip_eps = 1e-12


def norm_back(normed, inverse, upstream):
    mean_grad = jnp.mean(upstream, axis=-1, keepdims=True)
    mean_dot = jnp.mean(upstream * normed, axis=-1, keepdims=True)
    return inverse * (upstream - mean_grad - normed * mean_dot)


def gelu_parts(preact):
    inner = root_two_pi * (preact + gelu_coef * preact * preact * preact)
    tanh_value = jnp.tanh(inner)
    value_out = 0.5 * preact * (1.0 + tanh_value)
    slope_out = 0.5 * (1.0 + tanh_value) + 0.5 * preact * (
        1.0 - tanh_value * tanh_value
    ) * root_two_pi * (1.0 + 3.0 * gelu_coef * preact * preact)
    return (value_out, slope_out)


def silu_slope(drawn_values):
    sigmoid_val = jax.nn.sigmoid(drawn_values)
    return sigmoid_val * (1.0 + drawn_values * (1.0 - sigmoid_val))


def adam_update(parameter, moment_one, moment_two, gradient, decay_factor):
    new_one = beta_one * moment_one + (1.0 - beta_one) * gradient
    new_two = beta_two * moment_two + (1.0 - beta_two) * gradient * gradient
    first_hat = new_one / (1.0 - beta_one**adam_step)
    second_hat = new_two / (1.0 - beta_two**adam_step)
    new_param = parameter - learn_rate * (
        first_hat / (jnp.sqrt(second_hat) + adam_eps) + decay_factor * parameter
    )
    return (new_param, new_one, new_two)


def dotf(a, b, dims, precision=None):
    return lax.dot_general(a, b, dims, preferred_element_type=f32, precision=precision)


def vm():
    return pl.BlockSpec(memory_space=pltpu.VMEM)


def sm():
    return pl.BlockSpec(memory_space=pltpu.SMEM)


def shape(dims, dtype=bf):
    return jax.ShapeDtypeStruct(dims, dtype)


def params(mib=58):
    return pltpu.CompilerParams(vmem_limit_bytes=mib * 2**20)


def cost(flops, nbytes, trans=0):
    return pl.CostEstimate(flops=1024, bytes_accessed=1024, transcendentals=0)


def full(dims):
    return pl.BlockSpec(dims, lambda *_: (0,) * len(dims), pipeline_mode=pl.Buffered(1))


def prep_kernel(a_ref, b_ref, one_ref, o_ref):
    hw = a_ref.shape[3] // 2
    cat = lambda x, y: jnp.concatenate([x, y], axis=-1)
    q, k = ([a_ref[s, j].astype(bf) for s in range(2)] for j in range(2))
    v, o = ([b_ref[s, j].astype(bf) for s in range(2)] for j in range(2))
    for c in range(2):
        half = lambda w: w[:, c * hw : (c + 1) * hw]
        one_ref[3 * c] = cat(half(k[0]), half(v[0]))
        one_ref[3 * c + 1] = cat(half(q[0]), half(q[1]))
        one_ref[3 * c + 2] = cat(half(k[1]), half(v[1]))
        o_ref[c] = cat(half(o[0]), half(o[1]))


def prep_one(wt):
    _, _, rows, cw = wt.shape
    seg = lambda k: pl.BlockSpec((2, 2, rows, cw), lambda i: (0, k, 0, 0))
    outs = [shape((6, rows, cw)), shape((2, rows, cw))]
    return pl.pallas_call(
        prep_kernel,
        grid=(1,),
        in_specs=[seg(3), seg(4)],
        out_specs=[full(o.shape) for o in outs],
        out_shape=outs,
        compiler_params=params(),
        cost_estimate=cost(0, 0),
        name="prep_one",
    )(wt, wt)


def mod_kernel(sc_ref, w_ref, o_ref):
    for j in range(2):
        o_ref[0, j] = dotf(sc_ref[...], w_ref[0, j].astype(bf), NN)


def mod_partial(sc, wt):
    _, _, rows, cw = wt.shape
    n = sc.shape[0]
    return pl.pallas_call(
        mod_kernel,
        grid=(2, 3),
        in_specs=[
            pl.BlockSpec((n, rows), lambda s, i: (0, 0)),
            pl.BlockSpec((1, 2, rows, cw), lambda s, i: (s, i, 0, 0)),
        ],
        out_specs=pl.BlockSpec((1, 2, n, cw), lambda s, i: (s, i, 0, 0)),
        out_shape=shape((2, 6, n, cw), f32),
        compiler_params=params(),
        cost_estimate=cost(0, 0),
        name="mod_partial",
    )(sc, wt)


def normed_of(x):
    center = x - jnp.mean(x, axis=-1, keepdims=True)
    inverse = lax.rsqrt(jnp.mean(center * center, axis=-1, keepdims=True) + norm_eps)
    return center * inverse, inverse


def qkv_kernel(n_img, txt, hw, core_ref, xi_ref, xt_ref, mod_ref, bq_ref, bkv_ref, w_ref, hi_ref, ht_ref, ni_ref, nt_ref, q_ref, kv_ref):
    i = pl.program_id(0)
    rows = xi_ref.shape[0]

    def run(s, x, h_ref, n_ref, at, live):
        size = x.shape[0]
        n, _ = normed_of(x.astype(f32))
        n_ref[...] = n.astype(bf)
        h = (n * (1.0 + mod_ref[6 * s + 1 : 6 * s + 2]) + mod_ref[6 * s : 6 * s + 1]).astype(bf)
        h_ref[...] = h
        q = dotf(h, w_ref[1, :, hw * s : hw * (s + 1)], NN) + bq_ref[s : s + 1]
        q = (q.astype(bf).astype(f32) * DH**-0.5).astype(bf)
        q_ref[pl.ds(at, size)] = jnp.concatenate([q, jnp.zeros((size, 256 - hw), bf)], axis=1)
        kv = dotf(h, w_ref[2 * s], NN) + bkv_ref[s : s + 1]
        kv_ref[pl.ds(at, size)] = (kv if live is None else jnp.where(live, kv, 0.0)).astype(bf)

    @pl.when(i < n_img)
    def _():
        run(0, xi_ref[...], hi_ref, ni_ref, pl.multiple_of(i * rows, rows), None)

    @pl.when(i >= n_img)
    def _():
        live = lax.broadcasted_iota(jnp.int32, (xt_ref.shape[0], 1), 0) < txt
        run(1, xt_ref[...], ht_ref, nt_ref, n_img * rows, live)


def qkv(core, xi, xt, txt, mod, bq, bkv, w):
    img, D = xi.shape
    tpad = xt.shape[0]
    n_img = 2
    rows = img // n_img
    T = img + tpad
    hw, cw = bq.shape[1], w.shape[2]
    x_spec = pl.BlockSpec((rows, D), lambda i, c: (jnp.minimum(i, n_img - 1), 0))
    outs = [shape((img, D)), shape((tpad, D))] * 2 + [shape((T, 256)), shape((T, cw))]
    return pl.pallas_call(
        functools.partial(qkv_kernel, n_img, txt, hw),
        grid_spec=pltpu.PrefetchScalarGridSpec(
            num_scalar_prefetch=1,
            grid=(n_img + 1,),
            in_specs=[
                x_spec,
                full((tpad, D)),
                full(mod.shape),
                full(bq.shape),
                full(bkv.shape),
                pl.BlockSpec((3, D, cw), lambda i, c: (c[0], 0, 0), pipeline_mode=pl.Buffered(1)),
            ],
            out_specs=[x_spec, full((tpad, D))] * 2 + [full(o.shape) for o in outs[4:]],
        ),
        out_shape=outs,
        compiler_params=params(),
        cost_estimate=cost(2 * T * D * 3 * hw, 4 * T * D),
        name="qkv",
    )(core, xi, xt, mod, bq, bkv, w)


def store_chunks(core, send_ref, keep_ref, src, lo):
    nt = send_ref.shape[0]
    n = src.shape[0] // (2 * nt)
    for ref, c in ((send_ref, 1 - core), (keep_ref, core)):
        for t in range(nt):
            ref[t, lo : lo + n] = src[pl.ds(pl.multiple_of((c * nt + t) * n, n), n)].astype(bf)


def chunk_blocks(nt, chunk, width):
    return [pl.BlockSpec((nt, chunk, width), lambda i, c: (0, 0, i))] * 2


def oproj_kernel(img, core_ref, a_ref, w_ref, send_ref, keep_ref, acc):
    hw = a_ref.shape[1]
    acc[:img] = dotf(a_ref[:img], w_ref[0, :, :hw], NT)
    acc[img:] = dotf(a_ref[img:], w_ref[0, :, hw:], NT)
    store_chunks(core_ref[0], send_ref, keep_ref, acc.at[:img], 0)
    store_chunks(core_ref[0], send_ref, keep_ref, acc.at[img:], img // (2 * send_ref.shape[0]))


def oproj(core, a, w, nt, img):
    T, hw = a.shape
    _, D, cw = w.shape
    width = D // 3
    return pl.pallas_call(
        functools.partial(oproj_kernel, img),
        grid_spec=pltpu.PrefetchScalarGridSpec(
            num_scalar_prefetch=1,
            grid=(3,),
            in_specs=[full(a.shape), pl.BlockSpec((1, width, cw), lambda i, c: (c[0], i, 0))],
            out_specs=chunk_blocks(nt, T // (2 * nt), width),
            scratch_shapes=[pltpu.VMEM((T, width), f32)],
        ),
        out_shape=[shape((nt, T // (2 * nt), D))] * 2,
        compiler_params=params(),
        cost_estimate=cost(2 * T * D * hw, 2 * T * D),
        name="oproj",
    )(core, a, w)


def total(ref):
    t = ref[0].astype(f32)
    for k in range(1, ref.shape[0]):
        t = t + ref[k].astype(f32)
    return t


def store_copies(ref, rows, x):
    for k in range(ref.shape[0]):
        ref[k, rows] = x


def own_specs(ci, ct, D):
    return [
        pl.BlockSpec((ci, D), lambda i, o: (o[0], 0)),
        pl.BlockSpec((ct, D), lambda i, o: (o[0], 0)),
    ]


def whole(dims):
    return pl.BlockSpec(dims, lambda i, o: (0,) * len(dims))


def row_call(kernel, name, own, ci, ct, D, tokens, wholes, outs, deps=()):
    specs = [s for _ in tokens for s in own_specs(ci, ct, D)] + [whole(w.shape) for w in wholes]
    flat = [x for pair in tokens for x in pair]
    n_in = 1 + len(specs)
    return pl.pallas_call(
        lambda *refs: kernel(*refs[:n_in], *refs[n_in + len(deps) :]),
        grid_spec=pltpu.PrefetchScalarGridSpec(
            num_scalar_prefetch=1,
            grid=(1,),
            in_specs=specs + [pl.BlockSpec(memory_space=pl.ANY)] * len(deps),
            out_specs=[whole(o.shape) for o in outs],
        ),
        out_shape=outs,
        compiler_params=params(),
        cost_estimate=cost(0, 0),
        name=name,
    )(own, *flat, *wholes, *deps)


def after_attn_kernel(ci, own_ref, xi_ref, xt_ref, mod_ref, b_ref, part_ref, h_ref, o_ref):
    sums = total(part_ref)
    for s, x_ref in enumerate((xi_ref, xt_ref)):
        rows = slice(0, ci) if s == 0 else slice(ci, sums.shape[0])
        m = lambda j: mod_ref[6 * s + j : 6 * s + j + 1]
        o = sums[rows] + b_ref[14 * s + 8 : 14 * s + 9]
        n, _ = normed_of(x_ref[...].astype(f32) + m(2) * o)
        store_copies(h_ref, rows, (n * (1.0 + m(4)) + m(3)).astype(bf))
        o_ref[rows] = o


def colsum(x):
    return jnp.sum(x, axis=0, keepdims=True)


def after_mlp_kernel(ci, own_ref, xi_ref, xt_ref, ci_ref, ct_ref, mod_ref, o_ref, part_ref, do_ref, dx_ref, sum_ref):
    sums = total(part_ref)
    for s, (x_ref, c_ref) in enumerate(((xi_ref, ci_ref), (xt_ref, ct_ref))):
        rows = slice(0, ci) if s == 0 else slice(ci, sums.shape[0])
        m = lambda j: mod_ref[6 * s + j : 6 * s + j + 1]
        o = o_ref[rows]
        n, inv = normed_of(x_ref[...].astype(f32) + m(2) * o)
        dh = sums[rows]
        cot = c_ref[...].astype(f32)
        dx = cot + norm_back(n, inv, dh * (1.0 + m(4)))
        do = dx * m(2)
        store_copies(do_ref, rows, do.astype(bf))
        dx_ref[rows] = dx
        rows_out = [colsum(dx * o), colsum(dh), colsum(dh * n), colsum(do), colsum(cot * m(5))]
        sum_ref[8 * s : 8 * s + 8] = jnp.concatenate(rows_out + [jnp.zeros((3, dx.shape[1]), f32)], axis=0)


def after_down_kernel(
    ci, own_ref, xi_ref, xt_ref, ci_ref, ct_ref, mod_ref, b_ref, live_ref, o_ref, part_ref, out_ref, sum_ref
):
    sums = total(part_ref)
    for s, (x_ref, c_ref) in enumerate(((xi_ref, ci_ref), (xt_ref, ct_ref))):
        rows = slice(0, ci) if s == 0 else slice(ci, sums.shape[0])
        m = lambda j: mod_ref[6 * s + j : 6 * s + j + 1]
        y = sums[rows] + b_ref[14 * s + 13 : 14 * s + 14]
        x1 = x_ref[...].astype(f32) + m(2) * o_ref[rows]
        store_copies(out_ref, rows, ((x1 + m(5) * y) * live_ref[...]).astype(bf))
        top = colsum(c_ref[...].astype(f32) * y)
        sum_ref[8 * s : 8 * s + 8] = jnp.concatenate([top, jnp.zeros((7, y.shape[1]), f32)], axis=0)


def after_back_kernel(ci, own_ref, xi_ref, xt_ref, mod_ref, dx_ref, part_ref, g_ref):
    sums = total(part_ref)
    for s, x_ref in enumerate((xi_ref, xt_ref)):
        rows = slice(0, ci) if s == 0 else slice(ci, sums.shape[0])
        n, inv = normed_of(x_ref[...].astype(f32))
        dh = sums[rows]
        g = dx_ref[rows] + norm_back(n, inv, dh * (1.0 + mod_ref[6 * s + 1 : 6 * s + 2]))
        store_copies(g_ref, rows, g.astype(bf))


def stream_blocks(img, tpad, width):
    return [
        pl.BlockSpec((1, img, width), lambda k, c: (jnp.minimum(k, 1), 0, 0)),
        pl.BlockSpec((1, tpad, width), lambda k, c: (jnp.maximum(k - 2, 0), 0, 0)),
    ]


def seg_call(kernel, name, core, ins, in_specs, outs, out_specs, scratch=(), est=None):
    return pl.pallas_call(
        kernel,
        grid_spec=pltpu.PrefetchScalarGridSpec(
            num_scalar_prefetch=1,
            grid=(4,),
            in_specs=in_specs,
            out_specs=out_specs,
            scratch_shapes=list(scratch),
        ),
        out_shape=outs,
        compiler_params=params(),
        cost_estimate=est or cost(0, 0),
        name=name,
    )(core, *ins)


def zeros_kernel(core_ref, o_ref):
    o_ref[...] = jnp.zeros_like(o_ref)


def zeros(core, n, D, cw):
    return pl.pallas_call(
        zeros_kernel,
        grid=(n,),
        in_specs=[sm()],
        out_specs=pl.BlockSpec((1, D, cw), lambda i: (i, 0, 0)),
        out_shape=shape((n, D, cw)),
        compiler_params=params(),
        cost_estimate=cost(0, 0),
        name="zeros",
    )(core)


def seg_of(base):
    return lambda k, c: ((k // 2) * 8 + base + 2 * c[0] + lax.rem(k, 2), 0, 0)


def grad_gate_kernel(core_ref, ci_ref, ct_ref, mod_ref, w_ref, dyi_ref, dyt_ref, dgi_ref, dgt_ref):
    k = pl.program_id(0)
    for s, (c, dy, dg) in enumerate(((ci_ref, dyi_ref, dgi_ref), (ct_ref, dyt_ref, dgt_ref))):

        @pl.when(k == 2 * s)
        def _():
            dy[...] = (c[...].astype(f32) * mod_ref[6 * s + 5 : 6 * s + 6]).astype(bf)

        @pl.when(jnp.right_shift(k, 1) == s)
        def _():
            dg[0] = dotf(dy[...], w_ref[0], NN)


def grad_gate(core, cot_i, cot_t, mod, w):
    img, D = cot_i.shape
    tpad = cot_t.shape[0]
    T = img + tpad
    cw = w.shape[2]
    return seg_call(
        grad_gate_kernel,
        "grad_gate",
        core,
        [cot_i, cot_t, mod, w],
        [full(cot_i.shape), full(cot_t.shape), full(mod.shape), pl.BlockSpec((1, D, cw), seg_of(4))],
        [shape((img, D)), shape((tpad, D)), shape((2, img, cw), f32), shape((2, tpad, cw), f32)],
        [full(cot_i.shape), full(cot_t.shape)] + stream_blocks(img, tpad, cw),
        est=cost(4 * T * D * cw, 4 * T * D),
    )


def place_chunks(core, mine, other, img_ref, txt_ref):
    nt = mine.shape[0]
    ci, ct = img_ref.shape[0] // (2 * nt), txt_ref.shape[0] // (2 * nt)
    for ref, c in ((mine, core), (other, 1 - core)):
        for t in range(nt):
            o = c * nt + t
            img_ref[pl.ds(pl.multiple_of(o * ci, ci), ci)] = ref[t, :ci]
            txt_ref[pl.ds(pl.multiple_of(o * ct, ct), ct)] = ref[t, ci:]


def mlp_kernel(core_ref, mine, other, dgi, dgt, w_ref, b_ref, hi, ht, gi, gt, dui, dut, send_ref, keep_ref, bias_ref, acc_i, acc_t):
    k = pl.program_id(0)

    @pl.when(k == 0)
    def _():
        place_chunks(core_ref[0], mine, other, hi, ht)
        bias_ref[...] = jnp.zeros_like(bias_ref)

    lo = 0
    for s, (h, dg, g, du_ref, acc) in enumerate(((hi, dgi, gi, dui, acc_i), (ht, dgt, gt, dut, acc_t))):

        @pl.when(jnp.right_shift(k, 1) == s)
        def _():
            size = min(256, h.shape[0])
            sums = None
            for r in range(0, h.shape[0], size):
                at = slice(r, r + size)
                u = dotf(h[at], w_ref[0], NN) + b_ref[pl.ds(k, 1)]
                val, slope = gelu_parts(u)
                g[0, at] = val.astype(bf)
                du = dg[0, at] * slope
                du_b = du.astype(bf)
                du_ref[0, at] = du_b
                sums = colsum(du) if sums is None else sums + colsum(du)
                acc[at] = jnp.where(k == 2 * s, 0.0, acc[at]) + dotf(du_b, w_ref[0], NT)

            bias_ref[pl.ds(k, 1)] = sums

            @pl.when(k == 2 * s + 1)
            def _():
                store_chunks(core_ref[0], send_ref, keep_ref, acc, lo)

        lo += acc.shape[0] // (2 * send_ref.shape[0])


def mlp(core, mine, other, dgi, dgt, w, b):
    nt, chunk, D = mine.shape
    img, tpad, cw = dgi.shape[1], dgt.shape[1], w.shape[2]
    T = img + tpad
    blocks = stream_blocks(img, tpad, cw)
    whole_outs = [shape((img, D)), shape((tpad, D))]
    ends = [shape((nt, chunk, D)), shape((nt, chunk, D)), shape((8, cw), f32)]
    return seg_call(
        mlp_kernel,
        "mlp",
        core,
        [mine, other, dgi, dgt, w, b],
        [full(mine.shape)] * 2 + blocks + [pl.BlockSpec((1, D, cw), seg_of(0)), full(b.shape)],
        whole_outs + [shape((2, img, cw)), shape((2, tpad, cw))] * 2 + ends,
        [full(o.shape) for o in whole_outs] + blocks + blocks + [full(o.shape) for o in ends],
        [pltpu.VMEM((img, D), f32), pltpu.VMEM((tpad, D), f32)],
        cost(8 * T * D * cw, 4 * T * D, 2 * T * cw),
    )


def down_kernel(core_ref, gi, gt, w_ref, send_ref, keep_ref, acc_i, acc_t):
    k = pl.program_id(0)
    lo = 0
    for s, (g, acc) in enumerate(((gi, acc_i), (gt, acc_t))):

        @pl.when(jnp.right_shift(k, 1) == s)
        def _():
            y = dotf(g[0], w_ref[0], NT)

            @pl.when(k == 2 * s)
            def _():
                acc[...] = y

            @pl.when(k == 2 * s + 1)
            def _():
                acc[...] += y
                store_chunks(core_ref[0], send_ref, keep_ref, acc, lo)

        lo += acc.shape[0] // (2 * send_ref.shape[0])


def down(core, gi, gt, w, nt):
    img, tpad = gi.shape[1], gt.shape[1]
    D, cw = w.shape[1:]
    T = img + tpad
    ends = [shape((nt, T // (2 * nt), D))] * 2
    return seg_call(
        down_kernel,
        "down",
        core,
        [gi, gt, w],
        stream_blocks(img, tpad, cw) + [pl.BlockSpec((1, D, cw), seg_of(4))],
        ends,
        [full(o.shape) for o in ends],
        [pltpu.VMEM((img, D), f32), pltpu.VMEM((tpad, D), f32)],
        cost(4 * T * D * cw, 2 * T * D),
    )


def grad_attn_kernel(core_ref, mine, other, w_ref, doi_ref, dot_ref, da_ref):
    img, hw = doi_ref.shape[0], da_ref.shape[1]
    place_chunks(core_ref[0], mine, other, doi_ref, dot_ref)
    da_ref[:img] = dotf(doi_ref[...], w_ref[0, :, :hw], NN).astype(bf)
    da_ref[img:] = dotf(dot_ref[...], w_ref[0, :, hw:], NN).astype(bf)


def grad_attn(core, mine, other, w, img, tpad):
    _, D, cw = w.shape
    hw = cw // 2
    T = img + tpad
    outs = [shape((img, D)), shape((tpad, D)), shape((T, hw))]
    return pl.pallas_call(
        grad_attn_kernel,
        grid_spec=pltpu.PrefetchScalarGridSpec(
            num_scalar_prefetch=1,
            grid=(1,),
            in_specs=[full(mine.shape)] * 2 + [pl.BlockSpec((1, D, cw), lambda i, c: (c[0], 0, 0))],
            out_specs=[full(o.shape) for o in outs],
        ),
        out_shape=outs,
        compiler_params=params(),
        cost_estimate=cost(2 * T * D * hw, 4 * T * D),
        name="grad_attn",
    )(core, mine, other, w)


def grad_in_kernel(
    img, txt, core_ref, dep_ref, dep_two_ref, q_ref, a_ref, b_ref, ni_ref, nt_ref, w_ref, send_ref, keep_ref, kvi_ref, kvt_ref, qv_ref, sum_ref, acc
):
    T, hw = q_ref.shape

    @pl.when(pl.program_id(0) == 0)
    def _():
        for s, (at, out) in enumerate(((slice(0, img), kvi_ref), (slice(img, T), kvt_ref))):
            kv = a_ref[at].astype(f32) + b_ref[at].astype(f32)
            if s == 1:
                kv = jnp.where(lax.broadcasted_iota(jnp.int32, (T - img, 1), 0) < txt, kv, 0.0)
            out[...] = kv.astype(bf)
            sums = jnp.concatenate([colsum(q_ref[at].astype(f32)), colsum(kv)[:, hw:]], axis=1)
            qv_ref[4 * s : 4 * s + 4] = jnp.broadcast_to(sums, (4, 2 * hw))

    acc[:img] = dotf(q_ref[:img], w_ref[1, :, :hw], NT) + dotf(kvi_ref[...], w_ref[0], NT)
    acc[img:] = dotf(q_ref[img:], w_ref[1, :, hw:], NT) + dotf(kvt_ref[...], w_ref[2], NT)
    rows = []
    for at, n_ref in ((slice(0, img), ni_ref), (slice(img, T), nt_ref)):
        rows += [colsum(acc[at]), colsum(acc[at] * n_ref[...].astype(f32))]
    sum_ref[...] = jnp.concatenate(rows + [jnp.zeros((4, acc.shape[1]), f32)], axis=0)
    store_chunks(core_ref[0], send_ref, keep_ref, acc.at[:img], 0)
    store_chunks(core_ref[0], send_ref, keep_ref, acc.at[img:], img // (2 * send_ref.shape[0]))


def grad_in(core, deps, dq, kv_a, kv_b, n_img, n_txt, w, nt, txt):
    T, hw = dq.shape
    img, tpad = n_img.shape[0], n_txt.shape[0]
    cw = kv_a.shape[1]
    D = w.shape[1]
    width = D // 3
    ends = [shape((img, cw)), shape((tpad, cw)), shape((8, cw), f32)]
    column = lambda n: pl.BlockSpec((n, width), lambda i, c: (0, i))
    return pl.pallas_call(
        functools.partial(grad_in_kernel, img, txt),
        grid_spec=pltpu.PrefetchScalarGridSpec(
            num_scalar_prefetch=1,
            grid=(3,),
            in_specs=[pl.BlockSpec(memory_space=pl.ANY)] * 2
            + [full(dq.shape), full(kv_a.shape), full(kv_b.shape), column(img), column(tpad)]
            + [pl.BlockSpec((3, width, cw), lambda i, c: (c[0], i, 0))],
            out_specs=chunk_blocks(nt, T // (2 * nt), width) + [full(o.shape) for o in ends] + [column(8)],
            scratch_shapes=[pltpu.VMEM((T, width), f32)],
        ),
        out_shape=[shape((nt, T // (2 * nt), D))] * 2 + ends + [shape((8, D), f32)],
        compiler_params=params(),
        cost_estimate=cost(2 * T * D * 3 * hw, 2 * T * D),
        name="grad_in",
    )(core, *deps, dq, kv_a, kv_b, n_img, n_txt, w)


def tokens_kernel(core_ref, flag_ref, mine, other, *refs):
    oi_ref, ot_ref = refs[-2:]
    on = flag_ref[0] != 0

    @pl.when(on)
    def _():
        place_chunks(core_ref[0], mine, other, oi_ref, ot_ref)

    @pl.when(jnp.logical_not(on))
    def _():
        oi_ref[...] = jnp.zeros_like(oi_ref)
        ot_ref[...] = jnp.zeros_like(ot_ref)


def join_tokens(core, flag, mine, other, img, tpad, deps=()):
    D = mine.shape[2]
    return pl.pallas_call(
        tokens_kernel,
        in_specs=[sm(), sm(), vm(), vm()] + [pl.BlockSpec(memory_space=pl.ANY)] * len(deps),
        out_specs=[vm()] * 2,
        out_shape=[shape((img, D)), shape((tpad, D))],
        compiler_params=params(),
        cost_estimate=cost(0, 4 * (img + tpad) * D),
        name="join_tokens",
    )(core, flag, mine, other, *deps)


def pack_kernel(picker_ref, place_ref, mid_ref, low_ref, end_ref, up_ref, qv_ref, out_ref):
    nseq = picker_ref.shape[0]
    z, core = place_ref[0], place_ref[1]
    D, cw = mid_ref.shape[1], up_ref.shape[1]
    hw = cw // 2
    out_ref[...] = jnp.zeros_like(out_ref)
    for s in range(2):
        rows = jnp.concatenate(
            [end_ref[2 * s : 2 * s + 2], mid_ref[8 * s : 8 * s + 3], low_ref[8 * s : 8 * s + 1]], axis=0
        )
        for n in range(nseq):
            out_ref[12 * n + 6 * s : 12 * n + 6 * s + 6] = rows * picker_ref[n]
        at = 12 * nseq
        out_ref[at + 2 * s : at + 2 * s + 2] = mid_ref[8 * s + 3 : 8 * s + 5]
        lane = lax.broadcasted_iota(jnp.int32, (1, D), 1)
        inside = jnp.logical_and(lane >= z * cw, lane < (z + 1) * cw)
        up = jnp.concatenate([up_ref[2 * s : 2 * s + 2]] * (D // cw), axis=1)
        up = jnp.where(inside, up, 0.0)
        none = jnp.zeros_like(up)
        first = core == 0
        up = jnp.concatenate([jnp.where(first, up, none), jnp.where(first, none, up)], axis=0)
        out_ref[at + 4 + 4 * s : at + 8 + 4 * s] = up
        row = qv_ref[4 * s : 4 * s + 1]
        start = z * cw + core * hw
        inside = jnp.logical_and(lane >= start, lane < start + hw)
        for k in range(2):
            part = row[:, k * hw : (k + 1) * hw]
            part = jnp.concatenate([part, part], axis=1)
            part = jnp.concatenate([part] * (D // cw), axis=1)
            out_ref[at + 12 + 2 * s + k : at + 13 + 2 * s + k] = jnp.where(inside, part, 0.0)


def pack_sums(picker, place, mid, low, end, up, qv):
    D = mid.shape[1]
    rows = -(-(12 * picker.shape[0] + 16) // 8) * 8
    return pl.pallas_call(
        pack_kernel,
        in_specs=[sm(), sm()] + [vm()] * 5,
        out_specs=vm(),
        out_shape=shape((rows, D), f32),
        compiler_params=params(),
        cost_estimate=cost(0, 0),
        name="pack_sums",
    )(picker, place, mid, low, end, up, qv)


def attn_fwd_kernel(heads, img, live, q_ref, ka_ref, kb_ref, a_ref, lse_ref):
    T = ka_ref.shape[0]
    bq = q_ref.shape[0]
    lane = lax.broadcasted_iota(jnp.int32, (1, 256), 1)
    lane1 = lax.broadcasted_iota(jnp.int32, (1, 128), 1)
    keep = lax.broadcasted_iota(jnp.int32, (1, T - img), 1) < live - img
    q = q_ref[...]
    acc = jnp.zeros((bq, 256), f32)
    lse_tile = jnp.zeros((bq, 128), f32)
    for h in range(heads):
        qm = jnp.where((lane >> 6) == h, q, jnp.zeros_like(q))
        parts = []
        for kv in (ka_ref, kb_ref):
            parts.append((dotf(qm, kv[:img, :256], NT), kv, 0, img))
            s = dotf(qm, kv[img:, :256], NT)
            parts.append((jnp.where(keep, s, -1e30), kv, img, T))
        m = functools.reduce(jnp.maximum, [jnp.max(p[0], axis=1, keepdims=True) for p in parts])
        l = jnp.zeros((bq, 1), f32)
        pv = jnp.zeros((bq, 256), f32)
        for s, kv, lo, hi in parts:
            e = jnp.exp(s - m)
            l = l + jnp.sum(e, axis=1, keepdims=True)
            pv = pv + dotf(e.astype(bf), kv[lo:hi, 128:384], NN)
        acc = jnp.where((lane >> 6) == h + 1, pv / l, acc)
        lse_tile = jnp.where(lane1 == h, m + jnp.log(l), lse_tile)
    a_ref[...] = acc[:, 64:256].astype(bf)
    lse_ref[...] = lse_tile.T[:8]


def attn_fwd(q, kv_a, kv_b, img, live, bq=384, heads=3):
    T = q.shape[0]
    return pl.pallas_call(
        functools.partial(attn_fwd_kernel, heads, img, live),
        grid=(T // bq,),
        in_specs=[pl.BlockSpec((bq, 256), lambda i: (i, 0)), full((T, 384)), full((T, 384))],
        out_specs=[pl.BlockSpec((bq, 192), lambda i: (i, 0)), pl.BlockSpec((8, bq), lambda i: (0, i))],
        out_shape=[shape((T, 192)), shape((8, T), f32)],
        compiler_params=params(),
        cost_estimate=cost(16 * T * T * 256, 4 * T * 384, T * T * 6),
        name="attn_fwd",
    )(q, kv_a, kv_b)


def attn_bwd_kernel(heads, q_ref, ka_ref, kb_ref, a_ref, da_ref, lse_ref, dq_ref, dka_ref, dkb_ref, daw, delta, dqa):
    step = pl.program_id(0)
    T = q_ref.shape[0]
    lane = lax.broadcasted_iota(jnp.int32, (1, 256), 1)

    @pl.when(step == 0)
    def _():
        da = da_ref[...]
        daw[...] = jnp.concatenate([jnp.zeros((T, 64), bf), da], axis=1)
        prod = da.astype(f32) * a_ref[...].astype(f32)
        col = lax.broadcasted_iota(jnp.int32, (8, 192), 1)
        hm = ((col >> 6) == lax.broadcasted_iota(jnp.int32, (8, 192), 0)).astype(f32)
        delta[...] = dotf(hm, prod, NT, lax.Precision.HIGHEST)
        dqa[...] = jnp.zeros_like(dqa)

    dq = jnp.zeros((T, 256), f32)
    for kv_ref, out_ref in ((ka_ref, dka_ref), (kb_ref, dkb_ref)):
        kw = kv_ref[:, :256]
        vw = kv_ref[:, 128:384]
        dk = jnp.zeros(kw.shape, f32)
        dv = jnp.zeros(kw.shape, f32)
        for h in range(heads):
            sel = (lane >> 6) == h
            qm = jnp.where(sel, q_ref[...], jnp.zeros((), bf))
            dam = jnp.where((lane >> 6) == h + 1, daw[...], jnp.zeros((), bf))
            p = jnp.exp(dotf(kw, qm, NT) - lse_ref[h : h + 1, :])
            dv = dv + dotf(p.astype(bf), dam, NN)
            ds = (p * (dotf(vw, dam, NT) - delta[h : h + 1, :])).astype(bf)
            dk = dk + dotf(ds, qm, NN)
            dq = dq + dotf(ds, jnp.where(sel, kw, jnp.zeros((), bf)), TN)
        out_ref[...] = jnp.concatenate([dk[:, :192], dv[:, 64:256]], axis=1).astype(bf)
    dqa[...] += dq

    @pl.when(step == pl.num_programs(0) - 1)
    def _():
        dq_ref[...] = (dqa[...][:, :192] * DH**-0.5).astype(bf)


def attn_bwd(q, kv_a, kv_b, a, da, lse, bk=384, heads=3):
    T = q.shape[0]
    block = pl.BlockSpec((bk, 384), lambda i: (i, 0))
    return pl.pallas_call(
        functools.partial(attn_bwd_kernel, heads),
        grid=(T // bk,),
        in_specs=[full((T, 256)), block, block, full((T, 192)), full((T, 192)), full((8, T))],
        out_specs=[full((T, 192)), block, block],
        out_shape=[shape((T, 192)), shape((T, 384)), shape((T, 384))],
        scratch_shapes=[pltpu.VMEM((T, 256), bf), pltpu.VMEM((8, T), f32), pltpu.VMEM((T, 256), f32)],
        compiler_params=params(),
        cost_estimate=cost(32 * T * T * 256, 8 * T * 384, T * T * 6),
        name="attn_bwd",
    )(q, kv_a, kv_b, a, da, lse)


def adam_kernel(f_ref, g_ref, w_ref, m_ref, v_ref, *refs):
    og, ow, om, ov = refs[-4:]
    g = g_ref[0, 0].astype(f32)
    og[0, 0] = g
    factor = f_ref[pl.program_id(0), pl.program_id(1)]
    ow[0, 0], om[0, 0], ov[0, 0] = adam_update(w_ref[0, 0], m_ref[0, 0], v_ref[0, 0], g * factor, decay_rate)


def adam_segments(factor, grad, start, w, m, v, before=None):
    _, count, rows, cw = grad.shape
    here = pl.BlockSpec((1, 1, rows, cw), lambda s, i: (s, i + start, 0, 0))
    before = [] if before is None else list(before)
    return pl.pallas_call(
        adam_kernel,
        grid=(2, count),
        in_specs=[sm(), pl.BlockSpec((1, 1, rows, cw), lambda s, i: (s, i, 0, 0))]
        + [here] * 3
        + [pl.BlockSpec(memory_space=pl.ANY)] * len(before),
        out_specs=[here] * 4,
        out_shape=[shape(w.shape, f32)] * 4,
        input_output_aliases={5 + k: k for k in range(len(before))},
        compiler_params=params(),
        cost_estimate=cost(0, 60 * rows * cw * count),
        name="adam",
    )(factor, grad, w, m, v, *before)


def adam_one_kernel(f_ref, one_ref, o_ref, w_ref, m_ref, v_ref, *refs):
    og, ow, om, ov = refs[-4:]
    hw = w_ref.shape[3] // 2
    cat = lambda ref, k0, k1, lo: jnp.concatenate([ref[k0, :, lo : lo + hw], ref[k1, :, lo : lo + hw]], axis=1)

    def run(j, base, grads):
        for s in range(2):
            g = grads[s].astype(f32)
            og[s, j] = g
            ow[s, j], om[s, j], ov[s, j] = adam_update(
                w_ref[s, j], m_ref[s, j], v_ref[s, j], g * f_ref[s, base + j], decay_rate
            )

    @pl.when(pl.program_id(0) == 0)
    def _():
        run(0, 0, [cat(one_ref, 1, 4, s * hw) for s in range(2)])
        run(1, 0, [cat(one_ref, 2 * s, 3 + 2 * s, 0) for s in range(2)])

    @pl.when(pl.program_id(0) == 1)
    def _():
        run(0, 2, [cat(one_ref, 2 * s, 3 + 2 * s, hw) for s in range(2)])
        run(1, 2, [cat(o_ref, 0, 1, s * hw) for s in range(2)])


def adam_one(factor, one, o, w, m, v, before):
    _, _, rows, cw = w.shape
    here = pl.BlockSpec((2, 2, rows, cw), lambda i: (0, i + 3, 0, 0))
    return pl.pallas_call(
        adam_one_kernel,
        grid=(2,),
        in_specs=[sm(), full(one.shape), full(o.shape)] + [here] * 3 + [pl.BlockSpec(memory_space=pl.ANY)] * 4,
        out_specs=[here] * 4,
        out_shape=[shape(w.shape, f32)] * 4,
        input_output_aliases={6 + k: k for k in range(4)},
        compiler_params=params(),
        cost_estimate=cost(0, 32 * rows * cw * 8),
        name="adam_one",
    )(factor, one, o, w, m, v, *before)


def adam_mod_kernel(sc_ref, d_ref, f_ref, w_ref, m_ref, v_ref, *refs):
    og, ow, om, ov = refs[-4:]
    s, i = pl.program_id(0), pl.program_id(1)
    nseq = d_ref.shape[2]
    for j in range(2):
        g = sc_ref[:, 0:1] * d_ref[0, j, 0:1]
        for n in range(1, nseq):
            g = g + sc_ref[:, n : n + 1] * d_ref[0, j, n : n + 1]
        og[0, j] = g
        ow[0, j], om[0, j], ov[0, j] = adam_update(
            w_ref[0, j], m_ref[0, j], v_ref[0, j], g * f_ref[s, 2 * i + j], decay_rate
        )


def adam_mod(sc, dmod, factor, w, m, v, before):
    _, _, rows, cw = w.shape
    nseq = sc.shape[1]
    here = pl.BlockSpec((1, 2, rows, cw), lambda s, i: (s, i, 0, 0))
    return pl.pallas_call(
        adam_mod_kernel,
        grid=(2, 3),
        in_specs=[
            pl.BlockSpec((rows, nseq), lambda s, i: (0, 0)),
            pl.BlockSpec((1, 2, nseq, cw), lambda s, i: (s, i, 0, 0)),
            sm(),
        ]
        + [here] * 3
        + [pl.BlockSpec(memory_space=pl.ANY)] * 4,
        out_specs=[here] * 4,
        out_shape=[shape(w.shape, f32)] * 4,
        input_output_aliases={6 + k: k for k in range(4)},
        compiler_params=params(),
        cost_estimate=cost(0, 28 * rows * cw * 12),
        name="adam_mod",
    )(sc, dmod, factor, w, m, v, *before)


def make_shards(sizes):
    ns, nc, nt = sizes["shard"], sizes["ctx"], sizes["tensor"]
    owners = 2 * nt
    blocks = ns * nc
    hops = [("shard", 1)]
    hops += [("shard", 1 << b) for b in range(1, ns.bit_length() - 1)]
    hops += [("ctx", 1 << b) for b in range(nc.bit_length() - 1)]
    hops += [("tensor", 1 << b) for b in range(nt.bit_length() - 1)]

    def pp(x, axis, xor):
        return lax.ppermute(x, axis, [(i, i ^ xor) for i in range(sizes[axis])])

    def swap(x, axis):
        return lax.all_to_all(x, axis, 0, 0, tiled=True)

    def all_sum(x):
        for axis, xor in hops:
            x = x + pp(x, axis, xor)
        return x

    def after(x, *deps):
        return lax.optimization_barrier((x,) + deps)[0]

    def dyn(x, i, axis=0):
        return lax.dynamic_index_in_dim(x, i, axis, keepdims=False)

    def shards(
        image_rows,
        text_rows,
        condition,
        slot_table,
        weights,
        mom_one,
        mom_two,
        biases,
        bias_one,
        bias_two,
        image_cot,
        text_cot,
    ):
        hp = lax.Precision.HIGHEST
        nseq, D = condition.shape
        img = image_rows.shape[1]
        txt = text_rows.shape[1]
        ct = -(-txt // (owners * 16)) * 16
        ci = img // owners
        tpad = ct * owners
        T = img + tpad
        live_rows = img + txt
        cw = weights.shape[3]
        hw = cw // 2
        rows = weights.shape[1]
        shard_i, ctx_i, z = (lax.axis_index(a) for a in ("shard", "ctx", "tensor"))
        core = shard_i % 2
        first = core == 0
        me = shard_i * nc + ctx_i
        own = core * nt + z
        i32 = jnp.int32
        core_arr = core.reshape(1).astype(i32)
        own_arr = own.reshape(1).astype(i32)
        wt, m1, m2 = (jnp.moveaxis(x, 2, 1) for x in (weights, mom_one, mom_two))

        everyone = ("shard", "ctx")

        def gather(w):
            return lax.all_gather(w, everyone, axis=1, tiled=True)

        one_mine, o_mine = prep_one(wt)
        w_one = gather(one_mine)
        silu_all = jax.nn.silu(condition).astype(bf)
        sc_rows = lax.dynamic_slice_in_dim(silu_all, me * rows, rows, 1)
        mod = mod_partial(after(sc_rows, one_mine), wt)

        fixed = nseq == 2

        def pair(x):
            other = pp(x, "shard", 1)
            even = jnp.where(first, x, other)
            return [even] if fixed else [even, jnp.where(first, other, x)]

        tables = [t[0] for t in pair(slot_table)]
        lives = [(t >= 0).astype(f32) for t in tables]
        pickers = [(t == jnp.arange(nseq, dtype=i32)).astype(f32) for t in tables]
        pad_txt = lambda x: jnp.pad(x, ((0, tpad - txt), (0, 0)))
        x_img = [x[0] for x in pair(image_rows)]
        x_txt = [pad_txt(x[0]) for x in pair(text_rows)]
        mod = mod + pp(mod, "shard", 1)
        others = [r for r in range(1, blocks) if not r & nc]
        mod = sum(
            [lax.ppermute(mod, everyone, [(i, i ^ r) for i in range(blocks)]) for r in others], mod
        )
        mod = jnp.stack([mod] + [pp(mod, "tensor", k) for k in range(1, nt)])
        mod = jnp.concatenate([dyn(mod, z ^ k) for k in range(nt)], axis=-1)
        mods = [
            (jnp.einsum("n,sjne->sje", p, mod, precision=hp) + biases[:, :6]).reshape(12, D)
            for p in pickers
        ]
        col = z * cw
        bias_half = lax.dynamic_slice_in_dim(biases, col + core * hw, hw, 2)
        bias_cols = lax.dynamic_slice_in_dim(biases, col, cw, 2)
        bq = bias_half[:, 6]
        bkv = jnp.concatenate([jnp.zeros((2, hw), f32), bias_half[:, 7]], axis=1)
        b_up = lax.dynamic_slice_in_dim(bias_cols, 9 + 2 * core, 2, 1).reshape(4, cw)
        b_flat = biases.reshape(28, D)

        c_img = [(x[0] * l.astype(bf)) for x, l in zip(pair(image_cot), lives)]
        c_txt = [pad_txt(x[0] * l.astype(bf)) for x, l in zip(pair(text_cot), lives)]
        w_o = gather(after(o_mine, *mods))
        w_one = after(w_one, *mods, *x_img, *c_img)

        slots = range(len(tables))
        his, hts, nis, nts, qs, kvs, kv_gots = [], [], [], [], [], [], []
        for n in slots:
            hi, ht, ni, nt_, q, kv = qkv(core_arr, x_img[n], x_txt[n], txt, mods[n], bq, bkv, w_one)
            his.append(hi)
            hts.append(ht)
            nis.append(ni)
            nts.append(nt_)
            qs.append(q)
            kvs.append(kv)
            kv_gots.append(pp(kv, "ctx", 1))
        w_mlp = gather(after(wt[:, 10:18].astype(bf).reshape(16, rows, cw), kv_gots[-1]))

        def fold(send, keep):
            return (keep.astype(f32) + pp(send, "shard", 1).astype(f32)).astype(bf)

        def own_call(kernel, name, n, tokens, wholes, outs, deps=()):
            return row_call(functools.partial(kernel, ci), name, own_arr, ci, ct, D, tokens, wholes, outs, deps)

        chunk = ci + ct
        copies = shape((nt, chunk, D))
        attns, lses, o_parts = [], [], []
        for n in slots:
            a, lse = attn_fwd(qs[n], kvs[n], kv_gots[n], img, live_rows)
            attns.append(a)
            lses.append(lse)
            o_parts.append(swap(fold(*oproj(core_arr, a, w_o, nt, img)), "tensor"))

        mlp_all = zeros(after(core_arr, lses[-1]), 16, D, cw).reshape(2, 2, 2, 2, D, cw)
        dyis, dyts, gs, dus, up_sums, dh_parts, h2is, h2ts, o_sums = [], [], [], [], [], [], [], [], []
        for n in slots:
            h2, o_sum = own_call(
                after_attn_kernel,
                "after_attn",
                n,
                [(x_img[n], x_txt[n])],
                [mods[n], b_flat, after(o_parts[n], mlp_all)],
                [copies, shape((chunk, D), f32)],
            )
            o_sums.append(o_sum)
            dyi, dyt, *dg = grad_gate(core_arr, after(c_img[n], o_sum), c_txt[n], mods[n], w_mlp)
            mine = after(swap(h2, "tensor"), dyi)
            h2i, h2t, gi, gt, dui, dut, send, keep, up_sum = mlp(
                core_arr, mine, pp(mine, "shard", 1), *dg, w_mlp, b_up
            )
            dyis.append(dyi)
            dyts.append(dyt)
            h2is.append(h2i)
            h2ts.append(h2t)
            gs.append((gi, gt))
            dus.append((dui, dut))
            up_sums.append(up_sum)
            tie = fold(send, keep)
            dh_parts.append(swap(tie, "tensor"))

        def outer_sum(pairs):
            t = None
            for a, b in pairs:
                g = dotf(a, b, TN)
                t = g if t is None else t + g
            return t.astype(bf)

        def scatter(grads):
            return lax.psum_scatter(grads, everyone, scatter_dimension=1, tiled=True)

        def put(into, g, *at):
            return lax.dynamic_update_slice(into, g.reshape((1,) * len(at) + g.shape), at + (0, 0))

        for s, h2 in enumerate((h2is, h2ts)):
            for j in range(2):
                g = outer_sum([(h2[n], after(dus[n][s], tie)[j]) for n in slots])
                mlp_all = put(mlp_all, g, s, 0, core, j)
        for s, dy in enumerate((dyis, dyts)):
            for j in range(2):
                g = outer_sum([(dy[n], after(gs[n][s], tie)[j]) for n in slots])
                mlp_all = put(mlp_all, g, s, 1, core, j)
        mlp_sum = scatter(mlp_all.reshape(16, D, cw))
        do_owns, dxs, mid_sums = [], [], []
        for n in slots:
            do_own, dx, sums = own_call(
                after_mlp_kernel,
                "after_mlp",
                n,
                [(x_img[n], x_txt[n]), (c_img[n], c_txt[n])],
                [mods[n], o_sums[n], dh_parts[n]],
                [copies, shape((chunk, D), f32), shape((16, D), f32)],
                deps=[mlp_all],
            )
            dxs.append(dx)
            mid_sums.append(sums)
            do_owns.append(do_own)
        tie = do_owns[-1]
        y_halves = [fold(*down(core_arr, *(after(g, tie) for g in gs[n]), w_mlp, nt)) for n in slots]
        dois, dots, dqs, dkv_own, dkv_gots, out_owns, low_sums = [], [], [], [], [], [], []
        for n in slots:
            mine = after(swap(do_owns[n], "tensor"), y_halves[n])
            y_part = swap(after(y_halves[n], mine), "tensor")
            doi, dot, da = grad_attn(core_arr, mine, pp(mine, "shard", 1), w_o, img, tpad)
            dois.append(doi)
            dots.append(dot)
            dq, dkv_a, dkv_b = attn_bwd(qs[n], kvs[n], kv_gots[n], attns[n], da, lses[n])
            dqs.append(dq)
            dkv_own.append(dkv_a)
            dkv_gots.append(pp(after(dkv_b, y_part), "ctx", 1))
            out_own, sums = own_call(
                after_down_kernel,
                "after_down",
                n,
                [(x_img[n], x_txt[n]), (c_img[n], c_txt[n])],
                [mods[n], b_flat, lives[n].reshape(1, 1), o_sums[n], after(y_part, dq)],
                [copies, shape((16, D), f32)],
            )
            low_sums.append(sums)
            out_owns.append(swap(out_own, "tensor"))
        tie = dqs[-1]
        o_grads = [
            outer_sum([(after(dois[n], tie), attns[n][:img]) for n in slots]),
            outer_sum([(after(dots[n], tie), attns[n][img:]) for n in slots]),
        ]
        cat = lambda a, b: jnp.concatenate([a, b], axis=1)
        o_all = put(jnp.zeros((2, D, cw), bf), cat(*o_grads), core)
        o_rows = scatter(o_all)
        clip = lambda sq: jnp.minimum(1.0, clip_unit * D / jnp.sqrt(sq + clip_eps))

        def pad_row(x):
            x = x.reshape(1, -1)
            return jnp.pad(x, ((0, 0), (0, -x.shape[1] % 128)))

        mlp_sq = jnp.sum(jnp.sum(jnp.square(mlp_sum.astype(f32)), axis=1), axis=1)
        mlp_sq = all_sum(pad_row(mlp_sq))
        d_parts, dkv_img, dkv_txt, qv_sums, end_sums = [], [], [], [], []
        for n in slots:
            send, keep, kvi, kvt, qv, sums = grad_in(
                core_arr, [out_owns[n], mlp_sq], dqs[n], dkv_own[n], dkv_gots[n], nis[n], nts[n], w_one, nt, txt
            )
            dkv_img.append(kvi)
            dkv_txt.append(kvt)
            qv_sums.append(qv)
            end_sums.append(sums)
            tie = fold(send, keep)
            d_parts.append(swap(tie, "tensor"))
        q_grads, one_all = [], jnp.zeros((2, 3, D, cw), bf)
        for s, (part, left, right) in enumerate(((slice(0, img), his, dkv_img), (slice(img, T), hts, dkv_txt))):
            q_grads.append(outer_sum([(left[n], after(dqs[n], tie)[part]) for n in slots]))
            one_all = put(one_all, outer_sum([(left[n], right[n]) for n in slots]), core, 2 * s)
        one_all = put(one_all, cat(*q_grads), core, 1)
        one_rows = scatter(one_all.reshape(6, D, cw))

        place_arr = jnp.stack([z, core]).astype(i32)
        packed = all_sum(
            sum(
                pack_sums(pickers[n], place_arr, mid_sums[n], low_sums[n], end_sums[n], up_sums[n], qv_sums[n])
                for n in slots
            )
        )
        grad_owns = []
        for n in slots:
            (g,) = row_call(
                functools.partial(after_back_kernel, ci),
                "after_back",
                own_arr,
                ci,
                ct,
                D,
                [(x_img[n], x_txt[n])],
                [mods[n], dxs[n], d_parts[n]],
                [copies],
                deps=[one_all, packed],
            )
            grad_owns.append(swap(g, "tensor"))
        state = adam_segments(
            clip(mlp_sq[0, :16].reshape(2, 8)), mlp_sum.reshape(2, 8, rows, cw), 10, wt, m1, m2
        )
        e = nseq * 12
        dmod = packed[:e].reshape(nseq, 2, 6, D)
        od = packed[e : e + 4].reshape(2, 2, D)
        up_rows = packed[e + 4 : e + 12].reshape(2, 4, D)
        qv = packed[e + 12 : e + 16].reshape(2, 2, D)
        bias_grad = jnp.concatenate(
            [jnp.sum(dmod, axis=0), qv, od[:, :1], up_rows, od[:, 1:]], axis=1
        )
        wide = silu_all.astype(f32)
        gram_a = jnp.einsum("ni,mi->nm", wide, wide, precision=hp)
        gram_b = jnp.einsum("nsje,msje->sjnm", dmod, dmod, precision=hp)
        mod_sq = jnp.maximum(jnp.sum(gram_b * gram_a, axis=(2, 3)), 0.0)
        mod_cols = lax.dynamic_slice_in_dim(dmod, col, cw, 3)
        mod_cols = jnp.transpose(mod_cols, (1, 2, 0, 3))
        sc_wide = sc_rows.astype(f32)
        cond_rows = jnp.einsum("sjne,sjie->ni", mod_cols, wt[:, :6].astype(bf).astype(f32), precision=hp)
        cond_part = lax.dynamic_update_slice_in_dim(jnp.zeros((nseq, D), f32), cond_rows, me * rows, 1)

        def hsum(x, n):
            t = jnp.sum(jnp.square(x.astype(f32)), axis=1)
            t = t[:n] + t[n:]
            return jnp.stack([jnp.sum(t[:, :hw], axis=1), jnp.sum(t[:, hw:], axis=1)], axis=1)

        one_sq, o_sq = hsum(one_rows, 3), hsum(o_rows, 1)
        one_sq = jnp.stack(
            [jnp.stack([one_sq[1, s], one_sq[2 * s, 0], one_sq[2 * s, 1], o_sq[0, s]]) for s in range(2)]
        )
        tail = jnp.concatenate([cond_part.reshape(-1), one_sq.reshape(-1)])
        state = adam_mod(jnp.transpose(sc_wide), mod_cols, clip(mod_sq), wt, m1, m2, state)
        mod_state = state[0]
        tail = all_sum(tail)
        cond_grad = tail[: nseq * D].reshape(nseq, D) * silu_slope(condition)
        one_sq = tail[nseq * D :].reshape(2, 4)
        state = adam_one(clip(one_sq), one_rows, o_rows, wt, m1, m2, state)
        weight_grad, new_w, new_one, new_two = (jnp.moveaxis(x, 1, 2) for x in state)

        bias_sq = jnp.sum(bias_grad * bias_grad, axis=2)
        bias_factor = jnp.minimum(1.0, clip_unit * D**0.5 / jnp.sqrt(bias_sq + clip_eps))
        new_b, new_b1, new_b2 = adam_update(
            biases, bias_one, bias_two, bias_grad * bias_factor[:, :, None], 0.0
        )

        def finish(mine, deps=()):
            flag = first.astype(i32).reshape(1) if fixed else jnp.ones((1,), i32)
            done = [join_tokens(core_arr, flag, x, pp(x, "shard", 1), img, tpad, deps) for x in mine]
            return done[0] if fixed else [jnp.where(first, a, b) for a, b in zip(*done)]

        out_img, out_txt = finish(out_owns)
        grad_img, grad_txt = finish(grad_owns, [mod_state])
        return (
            out_img[None],
            out_txt[None, :txt],
            grad_img[None],
            grad_txt[None, :txt],
            cond_grad,
            weight_grad,
            new_w,
            new_one,
            new_two,
            bias_grad,
            new_b,
            new_b1,
            new_b2,
        )

    return shards


def solution(mesh):
    sizes = dict(mesh.shape)
    rows = P("shard", "ctx", None)
    mat = P(None, ("shard", "ctx"), None, "tensor")
    return jax.shard_map(
        make_shards(sizes),
        mesh=mesh,
        in_specs=(rows, rows, P(), P("shard"), mat, mat, mat, P(), P(), P(), rows, rows),
        out_specs=(rows, rows, rows, rows, P(), mat, mat, mat, mat, P(), P(), P(), P()),
        check_vma=False,
    )
```

time: 810 us -> 665 us (0.82)
  waiting for transfers between devices: 338 us -> 210 us
  Pallas kernels: 85 us -> 200 us
  starting transfers between devices: 140 us -> 62.2 us
  other arithmetic: 106 us -> 48.6 us
  blocking collectives: 0 us -> 45 us
  matrix products: 60.9 us -> 34 us
  local copies, waits for them, and re-layouts: 65.2 us -> 42.9 us
  between operations: 5.13 us -> 16.3 us
    ppermute x119 -> x34, waiting for transfers between devices: 338 us -> 103 us  [pp(): return lax.ppermute(x, axis, [(i, i ^ xor) for i in range(sizes[axis])])]
    pallas_call x12 -> x21, Pallas kernels: 68.2 us -> 184 us  [the longest x3 40 us: seg_call(): pl.pallas_call(kernel, grid_spec=pltpu.PrefetchScalarGridSpec(num_scalar_...]
    ppermute x119 -> x34, starting transfers between devices: 140 us -> 28 us  [pp(): return lax.ppermute(x, axis, [(i, i ^ xor) for i in range(sizes[axis])])]
    all_to_all x0 -> x7, waiting for transfers between devices: none -> 75.9 us  [swap(): return lax.all_to_all(x, axis, 0, 0, tiled=True)]
    all_to_all x0 -> x1, blocking collectives: none -> 45 us  [swap(): return lax.all_to_all(x, axis, 0, 0, tiled=True)]
    all_to_all x0 -> x7, starting transfers between devices: none -> 28.5 us  [swap(): return lax.all_to_all(x, axis, 0, 0, tiled=True)]
    dot_general x46 -> x18, matrix products: 60.9 us -> 34 us  [the longest x14 28 us: dotf(): lax.dot_general(a, b, dims, preferred_element_type=f32, precision=precision)]
    all_gather x0 -> x3, waiting for transfers between devices: none -> 25.1 us  [gather(): return lax.all_gather(w, everyone, axis=1, tiled=True)]
  transfers between devices with their start and end apart: 119 -> 50, of which waited for: 47 -> 35; matrix products, arithmetic and copies ran while one was open for 20% -> 14% of each run, Pallas kernels for 5% -> 26%
where the time goes in v2:
time: 665 us; the launch traced here: 659 us
  waiting for transfers between devices  210 us (32%)
  Pallas kernels  200 us (30%)
  starting transfers between devices  62.2 us (9%)
  other arithmetic  48.6 us (7%)
  blocking collectives  45 us (7%)
  local copies, waits for them, and re-layouts  42.9 us (6%)
  matrix products  34 us (5%)
  between operations  16.3 us (2%)
    ppermute x34, waiting for transfers between devices, pp(): return lax.ppermute(x, axis, [(i, i ^ xor) for i in range(sizes[axis])])  103 us
    all_to_all x7, waiting for transfers between devices, swap(): return lax.all_to_all(x, axis, 0, 0, tiled=True)  75.9 us
    all_to_all x1, blocking collectives, swap(): return lax.all_to_all(x, axis, 0, 0, tiled=True)  45 us
    pallas_call x3, Pallas kernels, seg_call(): pl.pallas_call(kernel, grid_spec=pltpu.PrefetchScalarGridSpec(num_scalar_...  40 us
    pallas_call x1, Pallas kernels, attn_bwd(): pl.pallas_call(functools.partial(attn_bwd_kernel, heads), grid=(T // bk,)...  31.9 us
    all_to_all x7, starting transfers between devices, swap(): return lax.all_to_all(x, axis, 0, 0, tiled=True)  28.5 us
    dot_general x14, matrix products, dotf(): lax.dot_general(a, b, dims, preferred_element_type=f32, precision=precision)  28 us
    ppermute x34, starting transfers between devices, pp(): return lax.ppermute(x, axis, [(i, i ^ xor) for i in range(sizes[axis])])  28 us
  transfers between devices with their start and end apart: 50, of which 35 were waited for; matrix products, arithmetic and copies ran while one was open for 14% of the time, Pallas kernels for 26%

profile of v2, /device:TPU:0, one launch (start us, length us, event | category | flops | bytes accessed | tf_op | source)
XLA Modules:
  0.0 659.3 jit_solution(11979071813636987745)
XLA Ops:
  13.6 5.0 mod_partial.1
  46.4 4.0 select_bitcast_fusion.xi_ref.refs_1_
  52.6 11.2 %all-gather.4.cloned.1.call-done.w_ref = bf16[6,1536,384]{2,1,0:T(8,128)(2,1)} async-done(((bf16[6,192,384]{2,1,0:T(8,128)(2,1)}), bf16[6,1536,384]{2,1,0:T(8,128)(2,1)}) %all-gather.4.cloned.1.call-update) | async-done | bytes 7077904 | tf_op jit(solution)/shard_map/all_gather | solution.py:938
  63.7 10.5 %qkv.1 = (bf16[1024,1536]{1,0:T(8,128)(2,1)}, bf16[128,1536]{1,0:T(8,128)(2,1)}, bf16[1024,1536]{1,0:T(8,128)(2,1)}, bf16[128,1536]{1,0:T(8,128)(2,1)}, bf16[115...) custom-call(s32[1]{0:T(128)} %bitcast.core_ref, bf16[1024,1536]{1,0:T(8,128)(2,1)} %select_bitcast_fusion.xi_ref.refs_1_, ...), custom_call_target="tpu_custom_call" | custom-call | flops 1024 | bytes 1024 | tf_op jit(solution)/shard_map/qkv/pallas_call | solution.py:182
  75.5 4.8 bitcast_convert_fusion
  84.3 20.7 %collective-permute-done.12.kb_ref = bf16[1152,384]{1,0:T(8,128)(2,1)S(1)} collective-permute-done((bf16[1152,384]{1,0:T(8,128)(2,1)}, bf16[1152,384]{1,0:T(8,128)(2,1)S(1)}, u32[]{:S(2)}, u32[]{:S(2)}) %collective-permute-start.12) | collective-permute-done | bytes 884768 | tf_op jit(solution)/shard_map/ppermute | solution.py:883
  105.9 16.3 %attn_fwd.1 = (bf16[1152,192]{1,0:T(8,128)(2,1)}, f32[8,1152]{1,0:T(8,128)}) custom-call(bf16[1152,256]{1,0:T(8,128)(2,1)} %get-tuple-element.99.q_ref, bf16[1152,384]{1,0:T(8,128)(2,1)} %get-tuple-element.100.ka_ref, bf16[1152,384]{1,0:T(8,128)(2,1)} %copy-done.12), custom_call_target="tpu_custom_call" | custom-call | flops 1024 | bytes 1024 | tf_op jit(solution)/shard_map/attn_fwd/pallas_call | solution.py:703
  122.2 4.8 oproj.1
  126.9 3.9 collective-permute-done.13
  134.0 4.6 all-to-all-start
  139.3 9.5 %zeros.1 = bf16[16,1536,384]{2,1,0:T(8,128)(2,1)} custom-call(s32[1]{0:T(128)} %bitcast.core_ref), custom_call_target="tpu_custom_call" | custom-call | flops 1024 | bytes 1024 | tf_op jit(solution)/shard_map/zeros/pallas_call | solution.py:371
  148.8 31.2 %all-to-all-done.refs_5_ = bf16[4,144,1536]{2,1,0:T(8,128)(2,1)S(1)} async-done(((bf16[4,144,1536]{2,1,0:T(8,128)(2,1)}), bf16[4,144,1536]{2,1,0:T(8,128)(2,1)S(1)}, u32[]{:S(2)}, u32[]{:S(2)}) %all-to-all-start) | async-done | bytes 1769504 | tf_op jit(solution)/shard_map/all_to_all | solution.py:886
  181.2 3.7 after_attn.1
  184.9 3.7 all-to-all-start.1
  191.6 13.9 %all-gather.8.cloned.1.call-done.w_ref = bf16[16,1536,384]{2,1,0:T(8,128)(2,1)} async-done(((bf16[16,192,384]{2,1,0:T(8,128)(2,1)}), bf16[16,1536,384]{2,1,0:T(8,128)(2,1)}) %all-gather.8.cloned.1.call-update) | async-done | bytes 18874384 | tf_op jit(solution)/shard_map/all_gather | solution.py:938
  205.5 10.6 %grad_gate.1 = (bf16[1024,1536]{1,0:T(8,128)(2,1)}, bf16[128,1536]{1,0:T(8,128)(2,1)}, f32[2,1024,384]{2,1,0:T(8,128)}, f32[2,128,384]{2,1,0:T(8,128)}) custom-call(s32[1]{0:T(128)} %bitcast.core_ref, bf16[1024,1536]{1,0:T(8,128)(2,1)} %multiply_bitcast_fusion.ci_ref.refs_3_, bf16[128,1536]{1,0:T(8,128)(2,1)} %pad.13.ct_ref.refs_4_, ...), custom_call_target="tpu_custom_call" | custom-call | flops 1024 | bytes 1024 | tf_op jit(solution)/shard_map/grad_gate/pallas_call | solution.py:350
  216.1 13.2 %all-to-all-done.1.mine = bf16[4,144,1536]{2,1,0:T(8,128)(2,1)S(1)} async-done(((bf16[4,144,1536]{2,1,0:T(8,128)(2,1)}), bf16[4,144,1536]{2,1,0:T(8,128)(2,1)S(1)}, u32[]{:S(2)}, u32[]{:S(2)}) %all-to-all-start.1) | async-done | bytes 1769504 | tf_op jit(solution)/shard_map/all_to_all | solution.py:886
  234.2 19.1 %mlp.1 = (bf16[1024,1536]{1,0:T(8,128)(2,1)}, bf16[128,1536]{1,0:T(8,128)(2,1)}, bf16[2,1024,384]{2,1,0:T(8,128)(2,1)}, bf16[2,128,384]{2,1,0:T(8,128)(2,1)}, bf...) custom-call(s32[1]{0:T(128)} %bitcast.core_ref, ...), custom_call_target="tpu_custom_call" | custom-call | flops 1024 | bytes 1024 | tf_op jit(solution)/shard_map/mlp/pallas_call | solution.py:350
  253.6 3.7 collective-permute-done.15
  277.1 45.0 %all_to_all.40.refs_7_ = bf16[4,144,1536]{2,1,0:T(8,128)(2,1)} all-to-all(bf16[4,144,1536]{2,1,0:T(8,128)(2,1)S(1)} %add_convert_fusion.2), channel_id=1, replica_groups=mesh['shard'=4,'ctx'=2,'tensor'=4] {'tensor'}, dimensions={0} | all-to-all | bytes 3538944 | tf_op jit(solution)/shard_map/all_to_all | solution.py:886
  322.1 5.2 after_mlp.1
  327.3 3.6 all-to-all-start.3
  330.9 10.3 %down.1 = (bf16[4,144,1536]{2,1,0:T(8,128)(2,1)}, bf16[4,144,1536]{2,1,0:T(8,128)(2,1)}) custom-call(s32[1]{0:T(128)} %bitcast.core_ref, bf16[2,1024,384]{2,1,0:T(8,128)(2,1)} %get-tuple-element.131.gi, bf16[2,128,384]{2,1,0:T(8,128)(2,1)} %get-tuple-element.132.gt, bf16[16,1536,384]{2,1,0:T(8,128)(2,1)} %all-gather.8.cloned.1.call-done.w_ref), custom_call_target="tpu_custom_call" | custom-call | flops 1024 | bytes 1024 | tf_op jit(solution)/shard_map/down/pallas_call | solution.py:350
  341.2 3.9 collective-permute-done.16
  348.3 23.1 %all-to-all-done.3.mine = bf16[4,144,1536]{2,1,0:T(8,128)(2,1)S(1)} async-done(((bf16[4,144,1536]{2,1,0:T(8,128)(2,1)}), bf16[4,144,1536]{2,1,0:T(8,128)(2,1)S(1)}, u32[]{:S(2)}, u32[]{:S(2)}) %all-to-all-start.3) | async-done | bytes 1769504 | tf_op jit(solution)/shard_map/all_to_all | solution.py:886
  371.4 3.8 all-to-all-start.4
  375.3 3.7 collective-permute-done.17.other
  380.2 5.2 grad_attn.1
  385.5 31.9 %attn_bwd.1 = (bf16[1152,192]{1,0:T(8,128)(2,1)}, bf16[1152,384]{1,0:T(8,128)(2,1)}, bf16[1152,384]{1,0:T(8,128)(2,1)}) custom-call(bf16[1152,256]{1,0:T(8,128)(2,1)} %get-tuple-element.99.q_ref, bf16[1152,384]{1,0:T(8,128)(2,1)} %get-tuple-element.100.ka_ref, bf16[1152,384]{1,0:T(8,128)(2,1)} %copy-done.12, bf16[1152,192]{1,0:T(8,128)(2,1)} %get-tuple-element.101.a_ref, ...), custom_call_target="tpu_custom_call" | custom-call | flops 1024 | bytes 1024 | tf_op jit(solution)/shard_map/attn_bwd/pallas_call | solution.py:756
  418.6 4.4 after_down.1
  423.0 5.2 all-to-all-start.5
  448.3 7.1 %collective-permute-done.21 = f32[1,128]{1,0:T(1,128)S(1)} collective-permute-done((f32[1,128]{1,0:T(1,128)S(1)}, f32[1,128]{1,0:T(1,128)S(1)}, u32[]{:S(2)}, u32[]{:S(2)}) %collective-permute-start.21) | collective-permute-done | bytes 544 | tf_op jit(solution)/shard_map/ppermute | solution.py:883
  461.9 8.0 %collective-permute-done.23 = f32[1,128]{1,0:T(1,128)S(1)} collective-permute-done((f32[1,128]{1,0:T(1,128)S(1)}, f32[1,128]{1,0:T(1,128)S(1)}, u32[]{:S(2)}, u32[]{:S(2)}) %collective-permute-start.23) | collective-permute-done | bytes 544 | tf_op jit(solution)/shard_map/ppermute | solution.py:883
  471.6 8.6 %grad_in.1 = (bf16[4,144,1536]{2,1,0:T(8,128)(2,1)}, bf16[4,144,1536]{2,1,0:T(8,128)(2,1)}, bf16[1024,384]{1,0:T(8,128)(2,1)}, bf16[128,384]{1,0:T(8,128)(2,1)}, f32[8,384]{1,0:T(8,128)}, /*index=5*/f32[8,1536]{1,0:T(8,128)}) custom-call(s32[1]{0:T(128)} %bitcast.core_ref, bf16[4,144,1536]{2,1,0:T(8,128)(2,1)} %copy-done, f32[1,128]{1,0:T(1,128)} %add.218.dep_two_ref, ...), custom_call_target="tpu_custom_call" | custom-call | flops 1024 | bytes 1024 | tf_op jit(solution)/shard_map/grad_in/pallas_call | solution.py:581
  480.3 3.7 broadcast_in_dim.26
  493.4 3.9 all-to-all-start.6
  504.9 6.8 %collective-permute-done.27 = f32[40,1536]{1,0:T(8,128)S(1)} collective-permute-done((f32[40,1536]{1,0:T(8,128)S(1)}, f32[40,1536]{1,0:T(8,128)S(1)}, u32[]{:S(2)}, u32[]{:S(2)}) %collective-permute-start.27) | collective-permute-done | bytes 245792 | tf_op jit(solution)/shard_map/ppermute | solution.py:883
  512.2 6.9 %collective-permute-done.28 = f32[40,1536]{1,0:T(8,128)S(1)} collective-permute-done((f32[40,1536]{1,0:T(8,128)S(1)}, f32[40,1536]{1,0:T(8,128)S(1)}, u32[]{:S(2)}, u32[]{:S(2)}) %collective-permute-start.28) | collective-permute-done | bytes 245792 | tf_op jit(solution)/shard_map/ppermute | solution.py:883
  523.4 8.9 %collective-permute-done.29 = f32[40,1536]{1,0:T(8,128)} collective-permute-done((f32[40,1536]{1,0:T(8,128)}, f32[40,1536]{1,0:T(8,128)}, u32[]{:S(2)}, u32[]{:S(2)}) %collective-permute-start.29) | collective-permute-done | bytes 245792 | tf_op jit(solution)/shard_map/ppermute | solution.py:883
  534.1 4.6 collective-permute-start.30
  541.9 8.3 %collective-permute-done.30 = f32[40,1536]{1,0:T(8,128)} collective-permute-done((f32[40,1536]{1,0:T(8,128)}, f32[40,1536]{1,0:T(8,128)}, u32[]{:S(2)}, u32[]{:S(2)}) %collective-permute-start.30) | collective-permute-done | bytes 245792 | tf_op jit(solution)/shard_map/ppermute | solution.py:883
  553.2 4.0 after_back.1
  563.9 4.0 join_tokens.2
  570.3 19.7 %adam.1 = (f32[2,18,192,384]{3,2,1,0:T(8,128)}, f32[2,18,192,384]{3,2,1,0:T(8,128)}, f32[2,18,192,384]{3,2,1,0:T(8,128)}, f32[2,18,192,384]{3,2,1,0:T(8,128)}) custom-call(f32[2,8]{1,0:T(2,128)} %min.22.f_ref, bf16[2,8,192,384]{3,2,1,0:T(8,128)(2,1)} %bitcast.181, f32[2,18,192,384]{3,2,1,0:T(8,128)} %bitcast.166, f32[2,18,192,384]{3,2,1,0:T(8,128)} %bitcast.171, ...), custom_call_target="tpu_custom_call" | custom-call | flops 1024 | bytes 1024 | tf_op jit(solution)/shard_map/adam/pallas_call | solution.py:781
  593.8 8.4 %all-to-all-done.7.mine = bf16[4,144,1536]{2,1,0:T(8,128)(2,1)S(1)} async-done(((bf16[4,144,1536]{2,1,0:T(8,128)(2,1)}), bf16[4,144,1536]{2,1,0:T(8,128)(2,1)S(1)}, u32[]{:S(2)}, u32[]{:S(2)}) %all-to-all-start.7) | async-done | bytes 1769504 | tf_op jit(solution)/shard_map/all_to_all | solution.py:886
  619.6 11.5 %adam_mod.1 = (f32[2,18,192,384]{3,2,1,0:T(8,128)}, f32[2,18,192,384]{3,2,1,0:T(8,128)}, f32[2,18,192,384]{3,2,1,0:T(8,128)}, f32[2,18,192,384]{3,2,1,0:T(8,128)}) custom-call(f32[192,2]{1,0:T(8,128)} %get-tuple-element.251.sc_ref, f32[2,6,2,384]{3,2,1,0:T(2,128)} %copy-done.33, ...), custom_call_target="tpu_custom_call", output_to_operand_aliasing={{0}: (6, {}), {1}: (7, {}), {2}: (8, {}), {3}: (9, {})} | custom-call | flops 1024 | bytes 1024 | tf_op jit(solution)/shard_map/adam_mod/pallas_call | solution.py:854
  634.3 4.2 join_tokens.3
  645.2 7.0 %adam_one.1 = (f32[2,18,192,384]{3,2,1,0:T(8,128)}, f32[2,18,192,384]{3,2,1,0:T(8,128)}, f32[2,18,192,384]{3,2,1,0:T(8,128)}, f32[2,18,192,384]{3,2,1,0:T(8,128)}) custom-call(f32[2,4]{1,0:T(2,128)} %min.24.f_ref, ...), custom_call_target="tpu_custom_call", output_to_operand_aliasing={{0}: (6, {}), {1}: (7, {}), {2}: (8, {}), {3}: (9, {})} | custom-call | flops 1024 | bytes 1024 | tf_op jit(solution)/shard_map/adam_one/pallas_call | solution.py:823
  (291 shorter events, 177.7 us)
Async XLA Ops:
  7.2 56.5 %all-gather.4.cloned.1.call-start = ((), (), s32[]{:S(2)}) async-start(), calls=%async_computation.11 | async-start | bytes 7962624 | tf_op jit(solution)/shard_map/all_gather | solution.py:938
  10.2 112.0 %all-gather.6.cloned.1.call-start = ((), (), s32[]{:S(2)}) async-start(), calls=%async_computation.12 | async-start | bytes 2654208 | tf_op jit(solution)/shard_map/all_gather | solution.py:938
  10.2 36.2 %collective-permute-start = (bf16[1,1024,1536]{2,1,0:T(8,128)(2,1)}, bf16[1,1024,1536]{2,1,0:T(8,128)(2,1)}, u32[]{:S(2)}, u32[]{:S(2)}) collective-permute-start(bf16[1,1024,1536]{2,1,0:T(8,128)(2,1)} %param.12), channel_id=1, source_target_pairs={{0,8},{8,0},{16,24},{24,16},{1,9},{9,1},{17,25},{25,17},{2,10},{10... | collective-permute-start | bytes 9437192 | tf_op jit(solution)/shard_map/ppermute | solution.py:883
  18.6 1.4 collective-permute-start.5
  20.8 5.3 collective-permute-start.6
  23.6 5.1 collective-permute-start.7
  25.1 5.6 collective-permute-start.8
  30.7 6.5 collective-permute-start.9
  32.4 5.6 collective-permute-start.10
  34.9 5.8 collective-permute-start.11
  35.2 1.2 collective-permute-start.3
  36.4 14.1 %collective-permute-start.2 = (bf16[1,1024,1536]{2,1,0:T(8,128)(2,1)}, bf16[1,1024,1536]{2,1,0:T(8,128)(2,1)S(1)}, u32[]{:S(2)}, u32[]{:S(2)}) collective-permute-start(bf16[1,1024,1536]{2,1,0:T(8,128)(2,1)} %param.22), channel_id=1, source_target_pairs={{0,8},{8,0},{16,24},{24,16},{1,9},{9,1},{17,25},{25,17},{2,10},{10... | collective-permute-start | bytes 9437192 | tf_op jit(solution)/shard_map/ppermute | solution.py:883
  42.0 163.5 %all-gather.8.cloned.1.call-start = ((), (), s32[]{:S(2)}) async-start(), calls=%async_computation.13 | async-start | bytes 21233664 | tf_op jit(solution)/shard_map/all_gather | solution.py:938
  42.4 2.3 collective-permute-start.1
  74.2 30.7 %collective-permute-start.12 = (bf16[1152,384]{1,0:T(8,128)(2,1)}, bf16[1152,384]{1,0:T(8,128)(2,1)S(1)}, u32[]{:S(2)}, u32[]{:S(2)}) collective-permute-start(bf16[1152,384]{1,0:T(8,128)(2,1)} %get-tuple-element.100.ka_ref), channel_id=1, source_target_pairs={{0,4},{4,0},{1,5},{5,1},{2,6},{6,2},{3,7},{7,3},{8,12},{12,8},{9,1... | collective-permute-start | bytes 2654216 | tf_op jit(solution)/shard_map/ppermute | solution.py:883
  126.9 3.9 collective-permute-start.13
  134.0 46.1 %all-to-all-start = ((bf16[4,144,1536]{2,1,0:T(8,128)(2,1)}), bf16[4,144,1536]{2,1,0:T(8,128)(2,1)S(1)}, u32[]{:S(2)}, u32[]{:S(2)}) async-start(bf16[4,144,1536]{2,1,0:T(8,128)(2,1)} %add_convert_fusion.3), calls=%async_computation | async-start | bytes 3538944 | tf_op jit(solution)/shard_map/all_to_all | solution.py:886
  184.9 44.4 %all-to-all-start.1 = ((bf16[4,144,1536]{2,1,0:T(8,128)(2,1)}), bf16[4,144,1536]{2,1,0:T(8,128)(2,1)S(1)}, u32[]{:S(2)}, u32[]{:S(2)}) async-start(bf16[4,144,1536]{2,1,0:T(8,128)(2,1)} %get-tuple-element.110), calls=%async_computation.1 | async-start | bytes 3538944 | tf_op jit(solution)/shard_map/all_to_all | solution.py:886
  188.6 251.2 %reduce-scatter.4.cloned.1.call-start = ((), (), s32[]{:S(2)}) async-start(), calls=%async_computation.14 | async-start | bytes 21233664 | tf_op jit(solution)/shard_map/reduce_scatter | solution.py:1046
  189.2 1.6 collective-permute-start.4
  229.3 3.7 collective-permute-start.14
  253.4 4.0 collective-permute-start.15
  327.3 44.2 %all-to-all-start.3 = ((bf16[4,144,1536]{2,1,0:T(8,128)(2,1)}), bf16[4,144,1536]{2,1,0:T(8,128)(2,1)S(1)}, u32[]{:S(2)}, u32[]{:S(2)}) async-start(bf16[4,144,1536]{2,1,0:T(8,128)(2,1)} %get-tuple-element.130), calls=%async_computation.3 | async-start | bytes 3538944 | tf_op jit(solution)/shard_map/all_to_all | solution.py:886
  341.2 3.9 collective-permute-start.16
  371.4 45.9 %all-to-all-start.4 = ((bf16[4,144,1536]{2,1,0:T(8,128)(2,1)}), bf16[4,144,1536]{2,1,0:T(8,128)(2,1)S(1)}, u32[]{:S(2)}, u32[]{:S(2)}) async-start(bf16[4,144,1536]{2,1,0:T(8,128)(2,1)} %add_convert_fusion.1), calls=%async_computation.4 | async-start | bytes 3538944 | tf_op jit(solution)/shard_map/all_to_all | solution.py:886
  375.2 3.8 collective-permute-start.17
  423.0 47.4 %all-to-all-start.5 = ((bf16[4,144,1536]{2,1,0:T(8,128)(2,1)}), bf16[4,144,1536]{2,1,0:T(8,128)(2,1)S(1)}, u32[]{:S(2)}, u32[]{:S(2)}) async-start(bf16[4,144,1536]{2,1,0:T(8,128)(2,1)} %get-tuple-element.140), calls=%async_computation.5 | async-start | bytes 3538944 | tf_op jit(solution)/shard_map/all_to_all | solution.py:886
  428.2 134.0 %reduce-scatter.8.cloned.1.call-start = ((), (), s32[]{:S(2)}) async-start(), calls=%async_computation.16 | async-start | bytes 2654208 | tf_op jit(solution)/shard_map/reduce_scatter | solution.py:1046
  433.5 36.9 %collective-permute-start.24 = (bf16[1152,384]{1,0:T(8,128)(2,1)}, bf16[1152,384]{1,0:T(8,128)(2,1)}, u32[]{:S(2)}, u32[]{:S(2)}) collective-permute-start(bf16[1152,384]{1,0:T(8,128)(2,1)} %get-tuple-element.146), channel_id=1, source_target_pairs={{0,4},{4,0},{1,5},{5,1},{2,6},{6,2},{3,7},{7,3},{8,12},{12,8},{9,1... | collective-permute-start | bytes 2654216 | tf_op jit(solution)/shard_map/ppermute | solution.py:883
  439.8 162.4 %reduce-scatter.6.cloned.1.call-start = ((), (), s32[]{:S(2)}) async-start(), calls=%async_computation.15 | async-start | bytes 7962624 | tf_op jit(solution)/shard_map/reduce_scatter | solution.py:1046
  443.3 3.5 collective-permute-start.20
  446.9 8.6 %collective-permute-start.21 = (f32[1,128]{1,0:T(1,128)S(1)}, f32[1,128]{1,0:T(1,128)S(1)}, u32[]{:S(2)}, u32[]{:S(2)}) collective-permute-start(f32[1,128]{1,0:T(1,128)S(1)} %add.215), channel_id=1, source_target_pairs={{0,4},{4,0},{1,5},{5,1},{2,6},{6,2},{3,7},{7,3},{8,12},{12,8},{9,1... | collective-permute-start | bytes 1544 | tf_op jit(solution)/shard_map/ppermute | solution.py:883
  455.5 3.5 collective-permute-start.22
  459.0 10.9 %collective-permute-start.23 = (f32[1,128]{1,0:T(1,128)S(1)}, f32[1,128]{1,0:T(1,128)S(1)}, u32[]{:S(2)}, u32[]{:S(2)}) collective-permute-start(f32[1,128]{1,0:T(1,128)S(1)} %add.217), channel_id=1, source_target_pairs={{0,2},{1,3},{2,0},{3,1},{4,6},{5,7},{6,4},{7,5},{8,10},{9,11},{10,... | collective-permute-start | bytes 1544 | tf_op jit(solution)/shard_map/ppermute | solution.py:883
  480.2 8.2 %collective-permute-start.25 = (bf16[4,144,1536]{2,1,0:T(8,128)(2,1)}, bf16[4,144,1536]{2,1,0:T(8,128)(2,1)S(1)}, u32[]{:S(2)}, u32[]{:S(2)}) collective-permute-start(bf16[4,144,1536]{2,1,0:T(8,128)(2,1)} %get-tuple-element.150), channel_id=1, source_target_pairs={{0,8},{8,0},{16,24},{24,16},{1,9},{9,1},{17,25},{25,17},{2,10},{10... | collective-permute-start | bytes 5308424 | tf_op jit(solution)/shard_map/ppermute | solution.py:883
  493.4 58.5 %all-to-all-start.6 = ((bf16[4,144,1536]{2,1,0:T(8,128)(2,1)}), bf16[4,144,1536]{2,1,0:T(8,128)(2,1)S(1)}, u32[]{:S(2)}, u32[]{:S(2)}) async-start(bf16[4,144,1536]{2,1,0:T(8,128)(2,1)} %add_convert_fusion), calls=%async_computation.7 | async-start | bytes 3538944 | tf_op jit(solution)/shard_map/all_to_all | solution.py:886
  500.2 2.1 collective-permute-start.26
  503.3 8.3 %collective-permute-start.27 = (f32[40,1536]{1,0:T(8,128)S(1)}, f32[40,1536]{1,0:T(8,128)S(1)}, u32[]{:S(2)}, u32[]{:S(2)}) collective-permute-start(f32[40,1536]{1,0:T(8,128)S(1)} %add.220), channel_id=1, source_target_pairs={{0,16},{8,24},{16,0},{24,8},{1,17},{9,25},{17,1},{25,9},{2,18},{10... | collective-permute-start | bytes 737288 | tf_op jit(solution)/shard_map/ppermute | solution.py:883
  504.8 59.1 %collective-permute-start.18 = (bf16[4,144,1536]{2,1,0:T(8,128)(2,1)S(1)}, bf16[4,144,1536]{2,1,0:T(8,128)(2,1)}, u32[]{:S(2)}, u32[]{:S(2)}) collective-permute-start(bf16[4,144,1536]{2,1,0:T(8,128)(2,1)S(1)} %copy-done.1), channel_id=1, source_target_pairs={{0,8},{8,0},{16,24},{24,16},{1,9},{9,1},{17,25},{25,17},{2,10},{10... | collective-permute-start | bytes 5308424 | tf_op jit(solution)/shard_map/ppermute | solution.py:883
  511.7 7.5 %collective-permute-start.28 = (f32[40,1536]{1,0:T(8,128)S(1)}, f32[40,1536]{1,0:T(8,128)S(1)}, u32[]{:S(2)}, u32[]{:S(2)}) collective-permute-start(f32[40,1536]{1,0:T(8,128)S(1)} %add.221), channel_id=1, source_target_pairs={{0,4},{4,0},{1,5},{5,1},{2,6},{6,2},{3,7},{7,3},{8,12},{12,8},{9,1... | collective-permute-start | bytes 737288 | tf_op jit(solution)/shard_map/ppermute | solution.py:883
  519.9 12.4 %collective-permute-start.29 = (f32[40,1536]{1,0:T(8,128)}, f32[40,1536]{1,0:T(8,128)}, u32[]{:S(2)}, u32[]{:S(2)}) collective-permute-start(f32[40,1536]{1,0:T(8,128)} %add.222), channel_id=1, source_target_pairs={{0,1},{1,0},{2,3},{3,2},{4,5},{5,4},{6,7},{7,6},{8,9},{9,8},{10,11... | collective-permute-start | bytes 737288 | tf_op jit(solution)/shard_map/ppermute | solution.py:883
  534.1 16.1 %collective-permute-start.30 = (f32[40,1536]{1,0:T(8,128)}, f32[40,1536]{1,0:T(8,128)}, u32[]{:S(2)}, u32[]{:S(2)}) collective-permute-start(f32[40,1536]{1,0:T(8,128)} %add.223), channel_id=1, source_target_pairs={{0,2},{1,3},{2,0},{3,1},{4,6},{5,7},{6,4},{7,5},{8,10},{9,11},{10,... | collective-permute-start | bytes 737288 | tf_op jit(solution)/shard_map/ppermute | solution.py:883
  557.1 45.0 %all-to-all-start.7 = ((bf16[4,144,1536]{2,1,0:T(8,128)(2,1)}), bf16[4,144,1536]{2,1,0:T(8,128)(2,1)S(1)}, u32[]{:S(2)}, u32[]{:S(2)}) async-start(bf16[4,144,1536]{2,1,0:T(8,128)(2,1)} %after_back.1), calls=%async_computation.8 | async-start | bytes 3538944 | tf_op jit(solution)/shard_map/all_to_all | solution.py:886
  602.2 32.2 %collective-permute-start.31 = (bf16[4,144,1536]{2,1,0:T(8,128)(2,1)S(1)}, bf16[4,144,1536]{2,1,0:T(8,128)(2,1)}, u32[]{:S(2)}, u32[]{:S(2)}) collective-permute-start(bf16[4,144,1536]{2,1,0:T(8,128)(2,1)S(1)} %all-to-all-done.7.mine), channel_id=1, source_target_pairs={{0,8},{8,0},{16,24},{24,16},{1,9},{9,1},{17,25},{25,17},{2,10},{10... | collective-permute-start | bytes 5308424 | tf_op jit(solution)/shard_map/ppermute | solution.py:883
  611.5 3.7 collective-permute-start.33
  615.2 3.7 collective-permute-start.34
  619.0 19.5 %collective-permute-start.35 = (f32[3080]{0:T(1024)S(1)}, f32[3080]{0:T(1024)S(1)}, u32[]{:S(2)}, u32[]{:S(2)}) collective-permute-start(f32[3080]{0:T(1024)S(1)} %add.231), channel_id=1, source_target_pairs={{0,1},{1,0},{2,3},{3,2},{4,5},{5,4},{6,7},{7,6},{8,9},{9,8},{10,11... | collective-permute-start | bytes 36968 | tf_op jit(solution)/shard_map/ppermute | solution.py:883
  638.5 4.7 collective-permute-start.36
  (45 other events, 347.9 us)
Sparse Core Ops, SparseCore 0:
  10.5 53.1 all-gather.3
  66.2 38.0 all-gather.5
  106.7 98.7 all-gather.7
  277.2 124.2 reduce-scatter.3
  439.9 44.0 reduce-scatter.7
  493.5 65.8 reduce-scatter.5

commit v3 on v2

--- a/solution.py
+++ b/solution.py
@@ -253,6 +253,22 @@
         ref[k, rows] = x
 
 
+def copy_kernel(x_ref, dep_ref, o_ref):
+    o_ref[...] = x_ref[...]
+
+
+def copy_after(x, dep):
+    return pl.pallas_call(
+        copy_kernel,
+        in_specs=[vm(), pl.BlockSpec(memory_space=pl.ANY)],
+        out_specs=vm(),
+        out_shape=shape(x.shape),
+        compiler_params=params(),
+        cost_estimate=cost(0, 0),
+        name="copy_after",
+    )(x, dep)
+
+
 def own_specs(ci, ct, D):
     return [
         pl.BlockSpec((ci, D), lambda i, o: (o[0], 0)),
@@ -363,21 +379,25 @@
     )(core, *ins)
 
 
-def zeros_kernel(core_ref, o_ref):
-    o_ref[...] = jnp.zeros_like(o_ref)
-
-
-def zeros(core, n, D, cw):
-    return pl.pallas_call(
+def zeros_kernel(core_ref, *outs):
+    for o in outs:
+        o[...] = jnp.zeros_like(o)
+
+
+def zeros(core, counts, D, cw):
+    n = 8
+    height = lambda c: c * D // n
+    flat = pl.pallas_call(
         zeros_kernel,
         grid=(n,),
         in_specs=[sm()],
-        out_specs=pl.BlockSpec((1, D, cw), lambda i: (i, 0, 0)),
-        out_shape=shape((n, D, cw)),
+        out_specs=[pl.BlockSpec((height(c), cw), lambda i: (i, 0)) for c in counts],
+        out_shape=[shape((c * D, cw)) for c in counts],
         compiler_params=params(),
         cost_estimate=cost(0, 0),
         name="zeros",
     )(core)
+    return [x.reshape(-1, D, cw) for x in flat]
 
 
 def seg_of(base):
@@ -623,12 +643,14 @@
     )(core, flag, mine, other, *deps)
 
 
-def pack_kernel(picker_ref, place_ref, mid_ref, low_ref, end_ref, up_ref, qv_ref, out_ref):
+def pack_kernel(picker_ref, place_ref, mid_ref, low_ref, end_ref, up_ref, qv_ref, sq_ref, out_ref):
     nseq = picker_ref.shape[0]
     z, core = place_ref[0], place_ref[1]
     D, cw = mid_ref.shape[1], up_ref.shape[1]
     hw = cw // 2
     out_ref[...] = jnp.zeros_like(out_ref)
+    at = 12 * nseq + 16
+    out_ref[at : at + 1, :128] = sq_ref[...]
     for s in range(2):
         rows = jnp.concatenate(
             [end_ref[2 * s : 2 * s + 2], mid_ref[8 * s : 8 * s + 3], low_ref[8 * s : 8 * s + 1]], axis=0
@@ -655,18 +677,37 @@
             out_ref[at + 12 + 2 * s + k : at + 13 + 2 * s + k] = jnp.where(inside, part, 0.0)
 
 
-def pack_sums(picker, place, mid, low, end, up, qv):
+def pack_sums(picker, place, mid, low, end, up, qv, sq):
     D = mid.shape[1]
-    rows = -(-(12 * picker.shape[0] + 16) // 8) * 8
+    rows = -(-(12 * picker.shape[0] + 17) // 8) * 8
     return pl.pallas_call(
         pack_kernel,
-        in_specs=[sm(), sm()] + [vm()] * 5,
+        in_specs=[sm(), sm()] + [vm()] * 6,
         out_specs=vm(),
         out_shape=shape((rows, D), f32),
         compiler_params=params(),
         cost_estimate=cost(0, 0),
         name="pack_sums",
-    )(picker, place, mid, low, end, up, qv)
+    )(picker, place, mid, low, end, up, qv, sq)
+
+
+def squares_kernel(x_ref, dep_ref, o_ref):
+    for p in range(x_ref.shape[0]):
+        x = x_ref[p].astype(f32)
+        o_ref[p : p + 1] = colsum(x * x)
+
+
+def column_squares(x, dep):
+    n, _, cw = x.shape
+    return pl.pallas_call(
+        squares_kernel,
+        in_specs=[vm(), pl.BlockSpec(memory_space=pl.ANY)],
+        out_specs=vm(),
+        out_shape=shape((n, cw), f32),
+        compiler_params=params(),
+        cost_estimate=cost(0, 0),
+        name="column_squares",
+    )(x, dep)
 
 
 def attn_fwd_kernel(heads, img, live, q_ref, ka_ref, kb_ref, a_ref, lse_ref):
@@ -793,7 +834,7 @@
     )(factor, grad, w, m, v, *before)
 
 
-def adam_one_kernel(f_ref, one_ref, o_ref, w_ref, m_ref, v_ref, *refs):
+def adam_one_kernel(f_ref, one_ref, w_ref, m_ref, v_ref, *refs):
     og, ow, om, ov = refs[-4:]
     hw = w_ref.shape[3] // 2
     cat = lambda ref, k0, k1, lo: jnp.concatenate([ref[k0, :, lo : lo + hw], ref[k1, :, lo : lo + hw]], axis=1)
@@ -808,29 +849,29 @@
 
     @pl.when(pl.program_id(0) == 0)
     def _():
-        run(0, 0, [cat(one_ref, 1, 4, s * hw) for s in range(2)])
-        run(1, 0, [cat(one_ref, 2 * s, 3 + 2 * s, 0) for s in range(2)])
+        run(0, 0, [cat(one_ref, 1, 5, s * hw) for s in range(2)])
+        run(1, 0, [cat(one_ref, 2 * s, 4 + 2 * s, 0) for s in range(2)])
 
     @pl.when(pl.program_id(0) == 1)
     def _():
-        run(0, 2, [cat(one_ref, 2 * s, 3 + 2 * s, hw) for s in range(2)])
-        run(1, 2, [cat(o_ref, 0, 1, s * hw) for s in range(2)])
-
-
-def adam_one(factor, one, o, w, m, v, before):
+        run(0, 2, [cat(one_ref, 2 * s, 4 + 2 * s, hw) for s in range(2)])
+        run(1, 2, [cat(one_ref, 3, 7, s * hw) for s in range(2)])
+
+
+def adam_one(factor, one, w, m, v, before):
     _, _, rows, cw = w.shape
     here = pl.BlockSpec((2, 2, rows, cw), lambda i: (0, i + 3, 0, 0))
     return pl.pallas_call(
         adam_one_kernel,
         grid=(2,),
-        in_specs=[sm(), full(one.shape), full(o.shape)] + [here] * 3 + [pl.BlockSpec(memory_space=pl.ANY)] * 4,
+        in_specs=[sm(), full(one.shape)] + [here] * 3 + [pl.BlockSpec(memory_space=pl.ANY)] * 4,
         out_specs=[here] * 4,
         out_shape=[shape(w.shape, f32)] * 4,
-        input_output_aliases={6 + k: k for k in range(4)},
+        input_output_aliases={5 + k: k for k in range(4)},
         compiler_params=params(),
         cost_estimate=cost(0, 32 * rows * cw * 8),
         name="adam_one",
-    )(factor, one, o, w, m, v, *before)
+    )(factor, one, w, m, v, *before)
 
 
 def adam_mod_kernel(sc_ref, d_ref, f_ref, w_ref, m_ref, v_ref, *refs):
@@ -889,6 +930,16 @@
         for axis, xor in hops:
             x = x + pp(x, axis, xor)
         return x
+
+    def all_sum_halved(x):
+        core = lax.axis_index("shard") % 2
+        half = x.shape[0] // 2
+        part = lambda c: lax.dynamic_slice_in_dim(x, c * half, half, 0)
+        mine = part(core) + pp(part(1 - core), "shard", 1)
+        for axis, xor in hops[1:]:
+            mine = mine + pp(mine, axis, xor)
+        other = pp(mine, "shard", 1)
+        return jnp.concatenate([jnp.where(core == 0, mine, other), jnp.where(core == 0, other, mine)], axis=0)
 
     def after(x, *deps):
         return lax.optimization_barrier((x,) + deps)[0]
@@ -1008,7 +1059,9 @@
             lses.append(lse)
             o_parts.append(swap(fold(*oproj(core_arr, a, w_o, nt, img)), "tensor"))
 
-        mlp_all = zeros(after(core_arr, lses[-1]), 16, D, cw).reshape(2, 2, 2, 2, D, cw)
+        mlp_all, one_all = zeros(after(core_arr, lses[-1]), (16, 8), D, cw)
+        mlp_all = mlp_all.reshape(2, 2, 2, 2, D, cw)
+        one_all = one_all.reshape(2, 4, D, cw)
         dyis, dyts, gs, dus, up_sums, dh_parts, h2is, h2ts, o_sums = [], [], [], [], [], [], [], [], []
         for n in slots:
             h2, o_sum = own_call(
@@ -1048,15 +1101,13 @@
         def put(into, g, *at):
             return lax.dynamic_update_slice(into, g.reshape((1,) * len(at) + g.shape), at + (0, 0))
 
-        for s, h2 in enumerate((h2is, h2ts)):
+        for s, (h2, dy) in enumerate(((h2is, dyis), (h2ts, dyts))):
             for j in range(2):
-                g = outer_sum([(h2[n], after(dus[n][s], tie)[j]) for n in slots])
-                mlp_all = put(mlp_all, g, s, 0, core, j)
-        for s, dy in enumerate((dyis, dyts)):
-            for j in range(2):
-                g = outer_sum([(dy[n], after(gs[n][s], tie)[j]) for n in slots])
-                mlp_all = put(mlp_all, g, s, 1, core, j)
-        mlp_sum = scatter(mlp_all.reshape(16, D, cw))
+                up = outer_sum([(h2[n], dus[n][s][j]) for n in slots])
+                mlp_all = put(mlp_all, up, s, 0, core, j)
+                dn = outer_sum([(dy[n], gs[n][s][j]) for n in slots])
+                if (s, j) != (1, 1):
+                    mlp_all = put(mlp_all, dn, s, 1, core, j)
         do_owns, dxs, mid_sums = [], [], []
         for n in slots:
             do_own, dx, sums = own_call(
@@ -1066,11 +1117,14 @@
                 [(x_img[n], x_txt[n]), (c_img[n], c_txt[n])],
                 [mods[n], o_sums[n], dh_parts[n]],
                 [copies, shape((chunk, D), f32), shape((16, D), f32)],
-                deps=[mlp_all],
+                deps=[mlp_all, dn],
             )
             dxs.append(dx)
             mid_sums.append(sums)
             do_owns.append(do_own)
+        probe = mid_sums[-1][0, 0]
+        mlp_all = put(mlp_all, dn, 1, 1, core + (probe != probe).astype(core.dtype), 1)
+        mlp_sum = scatter(mlp_all.reshape(16, D, cw))
         tie = do_owns[-1]
         y_halves = [fold(*down(core_arr, *(after(g, tie) for g in gs[n]), w_mlp, nt)) for n in slots]
         dois, dots, dqs, dkv_own, dkv_gots, out_owns, low_sums = [], [], [], [], [], [], []
@@ -1100,20 +1154,17 @@
             outer_sum([(after(dots[n], tie), attns[n][img:]) for n in slots]),
         ]
         cat = lambda a, b: jnp.concatenate([a, b], axis=1)
-        o_all = put(jnp.zeros((2, D, cw), bf), cat(*o_grads), core)
-        o_rows = scatter(o_all)
+        one_all = put(one_all, cat(*o_grads), core, 3)
         clip = lambda sq: jnp.minimum(1.0, clip_unit * D / jnp.sqrt(sq + clip_eps))
 
         def pad_row(x):
             x = x.reshape(1, -1)
             return jnp.pad(x, ((0, 0), (0, -x.shape[1] % 128)))
 
-        mlp_sq = jnp.sum(jnp.sum(jnp.square(mlp_sum.astype(f32)), axis=1), axis=1)
-        mlp_sq = all_sum(pad_row(mlp_sq))
         d_parts, dkv_img, dkv_txt, qv_sums, end_sums = [], [], [], [], []
         for n in slots:
             send, keep, kvi, kvt, qv, sums = grad_in(
-                core_arr, [out_owns[n], mlp_sq], dqs[n], dkv_own[n], dkv_gots[n], nis[n], nts[n], w_one, nt, txt
+                core_arr, [out_owns[n], one_all], dqs[n], dkv_own[n], dkv_gots[n], nis[n], nts[n], w_one, nt, txt
             )
             dkv_img.append(kvi)
             dkv_txt.append(kvt)
@@ -1121,17 +1172,20 @@
             end_sums.append(sums)
             tie = fold(send, keep)
             d_parts.append(swap(tie, "tensor"))
-        q_grads, one_all = [], jnp.zeros((2, 3, D, cw), bf)
+        q_grads = []
         for s, (part, left, right) in enumerate(((slice(0, img), his, dkv_img), (slice(img, T), hts, dkv_txt))):
             q_grads.append(outer_sum([(left[n], after(dqs[n], tie)[part]) for n in slots]))
             one_all = put(one_all, outer_sum([(left[n], right[n]) for n in slots]), core, 2 * s)
         one_all = put(one_all, cat(*q_grads), core, 1)
-        one_rows = scatter(one_all.reshape(6, D, cw))
-
+        one_rows = scatter(one_all.reshape(8, D, cw))
+
+        mlp_sq = pad_row(jnp.sum(jnp.sum(jnp.square(mlp_sum.astype(f32)), axis=1), axis=1))
         place_arr = jnp.stack([z, core]).astype(i32)
-        packed = all_sum(
+        packed = all_sum_halved(
             sum(
-                pack_sums(pickers[n], place_arr, mid_sums[n], low_sums[n], end_sums[n], up_sums[n], qv_sums[n])
+                pack_sums(
+                    pickers[n], place_arr, mid_sums[n], low_sums[n], end_sums[n], up_sums[n], qv_sums[n], mlp_sq if n == 0 else jnp.zeros_like(mlp_sq)
+                )
                 for n in slots
             )
         )
@@ -1147,11 +1201,11 @@
                 [(x_img[n], x_txt[n])],
                 [mods[n], dxs[n], d_parts[n]],
                 [copies],
-                deps=[one_all, packed],
+                deps=[one_all],
             )
             grad_owns.append(swap(g, "tensor"))
         state = adam_segments(
-            clip(mlp_sq[0, :16].reshape(2, 8)), mlp_sum.reshape(2, 8, rows, cw), 10, wt, m1, m2
+            clip(packed[nseq * 12 + 16, :16].reshape(2, 8)), mlp_sum.reshape(2, 8, rows, cw), 10, wt, m1, m2
         )
         e = nseq * 12
         dmod = packed[:e].reshape(nseq, 2, 6, D)
@@ -1171,22 +1225,19 @@
         cond_rows = jnp.einsum("sjne,sjie->ni", mod_cols, wt[:, :6].astype(bf).astype(f32), precision=hp)
         cond_part = lax.dynamic_update_slice_in_dim(jnp.zeros((nseq, D), f32), cond_rows, me * rows, 1)
 
-        def hsum(x, n):
-            t = jnp.sum(jnp.square(x.astype(f32)), axis=1)
-            t = t[:n] + t[n:]
-            return jnp.stack([jnp.sum(t[:, :hw], axis=1), jnp.sum(t[:, hw:], axis=1)], axis=1)
-
-        one_sq, o_sq = hsum(one_rows, 3), hsum(o_rows, 1)
+        state = adam_mod(jnp.transpose(sc_wide), mod_cols, clip(mod_sq), wt, m1, m2, state)
+        mod_state = state[0]
+        t = column_squares(one_rows, mod_state)
+        t = t[:4] + t[4:]
+        one_sq = jnp.stack([jnp.sum(t[:, :hw], axis=1), jnp.sum(t[:, hw:], axis=1)], axis=1)
         one_sq = jnp.stack(
-            [jnp.stack([one_sq[1, s], one_sq[2 * s, 0], one_sq[2 * s, 1], o_sq[0, s]]) for s in range(2)]
+            [jnp.stack([one_sq[1, s], one_sq[2 * s, 0], one_sq[2 * s, 1], one_sq[3, s]]) for s in range(2)]
         )
         tail = jnp.concatenate([cond_part.reshape(-1), one_sq.reshape(-1)])
-        state = adam_mod(jnp.transpose(sc_wide), mod_cols, clip(mod_sq), wt, m1, m2, state)
-        mod_state = state[0]
         tail = all_sum(tail)
         cond_grad = tail[: nseq * D].reshape(nseq, D) * silu_slope(condition)
         one_sq = tail[nseq * D :].reshape(2, 4)
-        state = adam_one(clip(one_sq), one_rows, o_rows, wt, m1, m2, state)
+        state = adam_one(clip(one_sq), one_rows, wt, m1, m2, state)
         weight_grad, new_w, new_one, new_two = (jnp.moveaxis(x, 1, 2) for x in state)
 
         bias_sq = jnp.sum(bias_grad * bias_grad, axis=2)
@@ -1195,13 +1246,14 @@
             biases, bias_one, bias_two, bias_grad * bias_factor[:, :, None], 0.0
         )
 
-        def finish(mine, deps=()):
+        def finish(mine, dep=None):
             flag = first.astype(i32).reshape(1) if fixed else jnp.ones((1,), i32)
-            done = [join_tokens(core_arr, flag, x, pp(x, "shard", 1), img, tpad, deps) for x in mine]
+            send = mine if dep is None else [copy_after(x, dep) for x in mine]
+            done = [join_tokens(core_arr, flag, x, pp(y, "shard", 1), img, tpad) for x, y in zip(mine, send)]
             return done[0] if fixed else [jnp.where(first, a, b) for a, b in zip(*done)]
 
         out_img, out_txt = finish(out_owns)
-        grad_img, grad_txt = finish(grad_owns, [mod_state])
+        grad_img, grad_txt = finish(grad_owns, mod_state)
         return (
             out_img[None],
             out_txt[None, :txt],

time: 665 us -> 643 us (0.967)
  blocking collectives: 45 us -> 0 us
  waiting for transfers between devices: 210 us -> 219 us
    all_to_all x1 -> x0, blocking collectives: 45 us -> none  [swap(): return lax.all_to_all(x, axis, 0, 0, tiled=True)]
    all_to_all x7 -> x8, waiting for transfers between devices: 75.9 us -> 87.1 us  [swap(): return lax.all_to_all(x, axis, 0, 0, tiled=True)]
    all_to_all x7 -> x8, starting transfers between devices: 28.5 us -> 33.5 us  [swap(): return lax.all_to_all(x, axis, 0, 0, tiled=True)]
    pallas_call x2 -> x4, Pallas kernels: 11.3 us -> 16.3 us  [the longest x1 9.61 us: zeros(): pl.pallas_call(zeros_kernel, grid=(n,), in_specs=[sm()], out_specs=[pl.Bl...]
    ppermute x34 -> x30, waiting for transfers between devices: 103 us -> 100 us  [pp(): return lax.ppermute(x, axis, [(i, i ^ xor) for i in range(sizes[axis])])]
    ppermute x34 -> x30, starting transfers between devices: 28 us -> 24.8 us  [pp(): return lax.ppermute(x, axis, [(i, i ^ xor) for i in range(sizes[axis])])]
    unnamed x92 -> x88, local copies, waits for them, and re-layouts: 15.1 us -> 17.5 us
  transfers between devices with their start and end apart: 50 -> 46, of which waited for: 35 -> 29; matrix products, arithmetic and copies ran while one was open for 14% -> 17% of each run, Pallas kernels for 26% -> 27%
where the time goes in v3:
time: 643 us; the launch traced here: 637 us
  waiting for transfers between devices  219 us (34%)
  Pallas kernels  205 us (32%)
  starting transfers between devices  63.7 us (10%)
  other arithmetic  46.3 us (7%)
  local copies, waits for them, and re-layouts  45.2 us (7%)
  matrix products  40.2 us (6%)
  between operations  17.3 us (3%)
    ppermute x30, waiting for transfers between devices, pp(): return lax.ppermute(x, axis, [(i, i ^ xor) for i in range(sizes[axis])])  100 us
    all_to_all x8, waiting for transfers between devices, swap(): return lax.all_to_all(x, axis, 0, 0, tiled=True)  87.1 us
    pallas_call x3, Pallas kernels, seg_call(): pl.pallas_call(kernel, grid_spec=pltpu.PrefetchScalarGridSpec(num_scalar_...  40.5 us
    dot_general x14, matrix products, dotf(): lax.dot_general(a, b, dims, preferred_element_type=f32, precision=precision)  34.3 us
    all_to_all x8, starting transfers between devices, swap(): return lax.all_to_all(x, axis, 0, 0, tiled=True)  33.5 us
    pallas_call x1, Pallas kernels, attn_bwd(): pl.pallas_call(functools.partial(attn_bwd_kernel, heads), grid=(T // bk,)...  31.8 us
    all_gather x3, waiting for transfers between devices, gather(): return lax.all_gather(w, everyone, axis=1, tiled=True)  27.6 us
    ppermute x30, starting transfers between devices, pp(): return lax.ppermute(x, axis, [(i, i ^ xor) for i in range(sizes[axis])])  24.8 us
  transfers between devices with their start and end apart: 46, of which 29 were waited for; matrix products, arithmetic and copies ran while one was open for 17% of the time, Pallas kernels for 27%

profile of v3, /device:TPU:0, one launch (start us, length us, event | category | flops | bytes accessed | tf_op | source)
XLA Modules:
  0.0 637.4 jit_solution(13274549829398185544)
XLA Ops:
  13.6 5.0 mod_partial.1
  20.9 3.7 collective-permute-start.8
  29.8 3.7 collective-permute-start.11
  44.3 4.0 select_bitcast_fusion.xi_ref.refs_1_
  50.4 13.3 %all-gather.4.cloned.1.call-done.w_ref = bf16[6,1536,384]{2,1,0:T(8,128)(2,1)} async-done(((bf16[6,192,384]{2,1,0:T(8,128)(2,1)}), bf16[6,1536,384]{2,1,0:T(8,128)(2,1)}) %all-gather.4.cloned.1.call-update) | async-done | bytes 7077904 | tf_op jit(solution)/shard_map/all_gather | solution.py:989
  63.7 10.5 %qkv.1 = (bf16[1024,1536]{1,0:T(8,128)(2,1)}, bf16[128,1536]{1,0:T(8,128)(2,1)}, bf16[1024,1536]{1,0:T(8,128)(2,1)}, bf16[128,1536]{1,0:T(8,128)(2,1)}, bf16[115...) custom-call(s32[1]{0:T(128)} %bitcast.core_ref, bf16[1024,1536]{1,0:T(8,128)(2,1)} %select_bitcast_fusion.xi_ref.refs_1_, ...), custom_call_target="tpu_custom_call" | custom-call | flops 1024 | bytes 1024 | tf_op jit(solution)/shard_map/qkv/pallas_call | solution.py:182
  75.5 4.8 bitcast_convert_fusion
  84.3 20.6 %collective-permute-done.12.kb_ref = bf16[1152,384]{1,0:T(8,128)(2,1)S(1)} collective-permute-done((bf16[1152,384]{1,0:T(8,128)(2,1)}, bf16[1152,384]{1,0:T(8,128)(2,1)S(1)}, u32[]{:S(2)}, u32[]{:S(2)}) %collective-permute-start.12) | collective-permute-done | bytes 884768 | tf_op jit(solution)/shard_map/ppermute | solution.py:924
  105.9 16.3 %attn_fwd.1 = (bf16[1152,192]{1,0:T(8,128)(2,1)}, f32[8,1152]{1,0:T(8,128)}) custom-call(bf16[1152,256]{1,0:T(8,128)(2,1)} %get-tuple-element.97.q_ref, bf16[1152,384]{1,0:T(8,128)(2,1)} %get-tuple-element.98.ka_ref, bf16[1152,384]{1,0:T(8,128)(2,1)} %copy-done.14), custom_call_target="tpu_custom_call" | custom-call | flops 1024 | bytes 1024 | tf_op jit(solution)/shard_map/attn_fwd/pallas_call | solution.py:744
  122.1 4.8 oproj.1
  126.9 3.9 collective-permute-done.13
  133.9 4.6 all-to-all-start
  139.3 9.6 %zeros.1 = (bf16[24576,384]{1,0:T(8,128)(2,1)}, bf16[12288,384]{1,0:T(8,128)(2,1)}) custom-call(s32[1]{0:T(128)} %bitcast.core_ref), custom_call_target="tpu_custom_call" | custom-call | flops 1024 | bytes 1024 | tf_op jit(solution)/shard_map/zeros/pallas_call | solution.py:390
  148.9 31.1 %all-to-all-done.refs_5_ = bf16[4,144,1536]{2,1,0:T(8,128)(2,1)S(1)} async-done(((bf16[4,144,1536]{2,1,0:T(8,128)(2,1)}), bf16[4,144,1536]{2,1,0:T(8,128)(2,1)S(1)}, u32[]{:S(2)}, u32[]{:S(2)}) %all-to-all-start) | async-done | bytes 1769504 | tf_op jit(solution)/shard_map/all_to_all | solution.py:927
  181.2 3.7 after_attn.1
  184.9 3.9 all-to-all-start.1
  191.2 14.3 %all-gather.8.cloned.1.call-done.w_ref = bf16[16,1536,384]{2,1,0:T(8,128)(2,1)} async-done(((bf16[16,192,384]{2,1,0:T(8,128)(2,1)}), bf16[16,1536,384]{2,1,0:T(8,128)(2,1)}) %all-gather.8.cloned.1.call-update) | async-done | bytes 18874384 | tf_op jit(solution)/shard_map/all_gather | solution.py:989
  205.5 10.6 %grad_gate.1 = (bf16[1024,1536]{1,0:T(8,128)(2,1)}, bf16[128,1536]{1,0:T(8,128)(2,1)}, f32[2,1024,384]{2,1,0:T(8,128)}, f32[2,128,384]{2,1,0:T(8,128)}) custom-call(s32[1]{0:T(128)} %bitcast.core_ref, bf16[1024,1536]{1,0:T(8,128)(2,1)} %multiply_bitcast_fusion.ci_ref.refs_3_, bf16[128,1536]{1,0:T(8,128)(2,1)} %pad.13.ct_ref.refs_4_, ...), custom_call_target="tpu_custom_call" | custom-call | flops 1024 | bytes 1024 | tf_op jit(solution)/shard_map/grad_gate/pallas_call | solution.py:366
  216.1 13.4 %all-to-all-done.1.mine = bf16[4,144,1536]{2,1,0:T(8,128)(2,1)S(1)} async-done(((bf16[4,144,1536]{2,1,0:T(8,128)(2,1)}), bf16[4,144,1536]{2,1,0:T(8,128)(2,1)S(1)}, u32[]{:S(2)}, u32[]{:S(2)}) %all-to-all-start.1) | async-done | bytes 1769504 | tf_op jit(solution)/shard_map/all_to_all | solution.py:927
  234.4 19.0 %mlp.1 = (bf16[1024,1536]{1,0:T(8,128)(2,1)}, bf16[128,1536]{1,0:T(8,128)(2,1)}, bf16[2,1024,384]{2,1,0:T(8,128)(2,1)}, bf16[2,128,384]{2,1,0:T(8,128)(2,1)}, bf...) custom-call(s32[1]{0:T(128)} %bitcast.core_ref, ...), custom_call_target="tpu_custom_call" | custom-call | flops 1024 | bytes 1024 | tf_op jit(solution)/shard_map/mlp/pallas_call | solution.py:366
  253.6 3.8 collective-permute-done.15
  266.0 5.1 fusion.1
  284.4 21.5 %all-to-all-done.2.refs_7_ = bf16[4,144,1536]{2,1,0:T(8,128)(2,1)S(1)} async-done(((bf16[4,144,1536]{2,1,0:T(8,128)(2,1)}), bf16[4,144,1536]{2,1,0:T(8,128)(2,1)S(1)}, u32[]{:S(2)}, u32[]{:S(2)}) %all-to-all-start.2) | async-done | bytes 1769504 | tf_op jit(solution)/shard_map/all_to_all | solution.py:927
  307.1 4.8 after_mlp.1
  315.6 3.6 all-to-all-start.3
  319.2 10.9 %down.1 = (bf16[4,144,1536]{2,1,0:T(8,128)(2,1)}, bf16[4,144,1536]{2,1,0:T(8,128)(2,1)}) custom-call(s32[1]{0:T(128)} %bitcast.core_ref, bf16[2,1024,384]{2,1,0:T(8,128)(2,1)} %get-tuple-element.126.gi, bf16[2,128,384]{2,1,0:T(8,128)(2,1)} %get-tuple-element.127.gt, bf16[16,1536,384]{2,1,0:T(8,128)(2,1)} %all-gather.8.cloned.1.call-done.w_ref), custom_call_target="tpu_custom_call" | custom-call | flops 1024 | bytes 1024 | tf_op jit(solution)/shard_map/down/pallas_call | solution.py:366
  330.1 5.6 collective-permute-done.16
  339.0 21.1 %all-to-all-done.3.mine = bf16[4,144,1536]{2,1,0:T(8,128)(2,1)S(1)} async-done(((bf16[4,144,1536]{2,1,0:T(8,128)(2,1)}), bf16[4,144,1536]{2,1,0:T(8,128)(2,1)S(1)}, u32[]{:S(2)}, u32[]{:S(2)}) %all-to-all-start.3) | async-done | bytes 1769504 | tf_op jit(solution)/shard_map/all_to_all | solution.py:927
  360.1 4.0 all-to-all-start.4
  364.3 3.7 collective-permute-done.17.other
  369.2 5.5 grad_attn.1
  374.7 31.8 %attn_bwd.1 = (bf16[1152,192]{1,0:T(8,128)(2,1)}, bf16[1152,384]{1,0:T(8,128)(2,1)}, bf16[1152,384]{1,0:T(8,128)(2,1)}) custom-call(bf16[1152,256]{1,0:T(8,128)(2,1)} %get-tuple-element.97.q_ref, bf16[1152,384]{1,0:T(8,128)(2,1)} %get-tuple-element.98.ka_ref, bf16[1152,384]{1,0:T(8,128)(2,1)} %copy-done.14, bf16[1152,192]{1,0:T(8,128)(2,1)} %get-tuple-element.99.a_ref, ...), custom_call_target="tpu_custom_call" | custom-call | flops 1024 | bytes 1024 | tf_op jit(solution)/shard_map/attn_bwd/pallas_call | solution.py:797
  407.7 4.4 after_down.1
  412.0 5.2 all-to-all-start.5
  427.1 31.7 %collective-permute-done.19.b_ref = bf16[1152,384]{1,0:T(8,128)(2,1)} collective-permute-done((bf16[1152,384]{1,0:T(8,128)(2,1)}, bf16[1152,384]{1,0:T(8,128)(2,1)}, u32[]{:S(2)}, u32[]{:S(2)}) %collective-permute-start.19) | collective-permute-done | bytes 884768 | tf_op jit(solution)/shard_map/ppermute | solution.py:924
  460.1 8.6 %grad_in.1 = (bf16[4,144,1536]{2,1,0:T(8,128)(2,1)}, bf16[4,144,1536]{2,1,0:T(8,128)(2,1)}, bf16[1024,384]{1,0:T(8,128)(2,1)}, bf16[128,384]{1,0:T(8,128)(2,1)}, f32[8,384]{1,0:T(8,128)}, /*index=5*/f32[8,1536]{1,0:T(8,128)}) custom-call(s32[1]{0:T(128)} %bitcast.core_ref, bf16[4,144,1536]{2,1,0:T(8,128)(2,1)} %copy-done.1, ...), custom_call_target="tpu_custom_call" | custom-call | flops 1024 | bytes 1024 | tf_op jit(solution)/shard_map/grad_in/pallas_call | solution.py:601
  468.8 5.1 fusion.9
  482.9 4.9 all-to-all-start.6
  499.3 4.6 collective-permute-done.22
  521.3 4.7 collective-permute-start.25
  527.4 4.1 join_tokens.2
  531.5 4.4 collective-permute-done.25
  539.4 4.0 after_back.1
  543.4 3.8 all-to-all-start.7
  548.9 19.4 %adam.1 = (f32[2,18,192,384]{3,2,1,0:T(8,128)}, f32[2,18,192,384]{3,2,1,0:T(8,128)}, f32[2,18,192,384]{3,2,1,0:T(8,128)}, f32[2,18,192,384]{3,2,1,0:T(8,128)}) custom-call(f32[2,8]{1,0:T(2,128)} %min.22.f_ref, bf16[2,8,192,384]{3,2,1,0:T(8,128)(2,1)} %bitcast.181, f32[2,18,192,384]{3,2,1,0:T(8,128)} %bitcast.164, f32[2,18,192,384]{3,2,1,0:T(8,128)} %bitcast.168, ...), custom_call_target="tpu_custom_call" | custom-call | flops 1024 | bytes 1024 | tf_op jit(solution)/shard_map/adam/pallas_call | solution.py:822
  570.8 11.5 %adam_mod.1 = (f32[2,18,192,384]{3,2,1,0:T(8,128)}, f32[2,18,192,384]{3,2,1,0:T(8,128)}, f32[2,18,192,384]{3,2,1,0:T(8,128)}, f32[2,18,192,384]{3,2,1,0:T(8,128)}) custom-call(f32[192,2]{1,0:T(8,128)} %get-tuple-element.232.sc_ref, ...), custom_call_target="tpu_custom_call", output_to_operand_aliasing={{0}: (6, {}), {1}: (7, {}), {2}: (8, {}), {3}: (9, {})} | custom-call | flops 1024 | bytes 1024 | tf_op jit(solution)/shard_map/adam_mod/pallas_call | solution.py:895
  616.3 7.2 %adam_one.1 = (f32[2,18,192,384]{3,2,1,0:T(8,128)}, f32[2,18,192,384]{3,2,1,0:T(8,128)}, f32[2,18,192,384]{3,2,1,0:T(8,128)}, f32[2,18,192,384]{3,2,1,0:T(8,128)}) custom-call(f32[2,4]{1,0:T(2,128)} %min.24.f_ref, ...), custom_call_target="tpu_custom_call", output_to_operand_aliasing={{0}: (5, {}), {1}: (6, {}), {2}: (7, {}), {3}: (8, {})} | custom-call | flops 1024 | bytes 1024 | tf_op jit(solution)/shard_map/adam_one/pallas_call | solution.py:864
  624.9 4.0 join_tokens.3
  (271 shorter events, 170.4 us)
Async XLA Ops:
  7.2 56.6 %all-gather.4.cloned.1.call-start = ((), (), s32[]{:S(2)}) async-start(), calls=%async_computation.10 | async-start | bytes 7962624 | tf_op jit(solution)/shard_map/all_gather | solution.py:989
  10.1 112.0 %all-gather.6.cloned.1.call-start = ((), (), s32[]{:S(2)}) async-start(), calls=%async_computation.11 | async-start | bytes 2654208 | tf_op jit(solution)/shard_map/all_gather | solution.py:989
  10.2 34.1 %collective-permute-start = (bf16[1,1024,1536]{2,1,0:T(8,128)(2,1)}, bf16[1,1024,1536]{2,1,0:T(8,128)(2,1)}, u32[]{:S(2)}, u32[]{:S(2)}) collective-permute-start(bf16[1,1024,1536]{2,1,0:T(8,128)(2,1)} %param.12), channel_id=1, source_target_pairs={{0,8},{8,0},{16,24},{24,16},{1,9},{9,1},{17,25},{25,17},{2,10},{10... | collective-permute-start | bytes 9437192 | tf_op jit(solution)/shard_map/ppermute | solution.py:924
  13.6 25.3 %copy-start.25 = (f32[2,14,1536]{2,0,1:T(2,128)S(1)}, f32[2,14,1536]{2,0,1:T(2,128)}, u32[]{:S(2)}) copy-start(f32[2,14,1536]{2,0,1:T(2,128)} %param.19) | copy-start | bytes 516100
  18.6 1.4 collective-permute-start.5
  20.9 6.5 %collective-permute-start.8 = (f32[2,6,2,384]{3,2,1,0:T(2,128)S(1)}, f32[2,6,2,384]{3,2,1,0:T(2,128)S(1)}, u32[]{:S(2)}, u32[]{:S(2)}) collective-permute-start(f32[2,6,2,384]{3,2,1,0:T(2,128)S(1)} %add.189), channel_id=1, source_target_pairs={{0,20},{4,16},{8,28},{12,24},{16,4},{20,0},{24,12},{28,8},{1,21},{... | collective-permute-start | bytes 110600 | tf_op jit(solution)/shard_map/ppermute | solution.py:1013
  24.5 5.0 collective-permute-start.7
  25.1 4.7 collective-permute-start.6
  29.8 6.5 %collective-permute-start.11 = (f32[2,6,2,384]{3,2,1,0:T(2,128)S(1)}, f32[2,6,2,384]{3,2,1,0:T(2,128)S(1)}, u32[]{:S(2)}, u32[]{:S(2)}) collective-permute-start(f32[2,6,2,384]{3,2,1,0:T(2,128)S(1)} %add_add_fusion), channel_id=1, source_target_pairs={{0,3},{1,2},{2,1},{3,0},{4,7},{5,6},{6,5},{7,4},{8,11},{9,10},{10,... | collective-permute-start | bytes 110600 | tf_op jit(solution)/shard_map/ppermute | solution.py:924
  33.5 4.9 collective-permute-start.10
  33.5 4.9 collective-permute-start.9
  34.3 1.2 collective-permute-start.3
  35.5 12.9 %collective-permute-start.2 = (bf16[1,1024,1536]{2,1,0:T(8,128)(2,1)}, bf16[1,1024,1536]{2,1,0:T(8,128)(2,1)S(1)}, u32[]{:S(2)}, u32[]{:S(2)}) collective-permute-start(bf16[1,1024,1536]{2,1,0:T(8,128)(2,1)} %param.22), channel_id=1, source_target_pairs={{0,8},{8,0},{16,24},{24,16},{1,9},{9,1},{17,25},{25,17},{2,10},{10... | collective-permute-start | bytes 9437192 | tf_op jit(solution)/shard_map/ppermute | solution.py:924
  39.7 165.7 %all-gather.8.cloned.1.call-start = ((), (), s32[]{:S(2)}) async-start(), calls=%async_computation.12 | async-start | bytes 21233664 | tf_op jit(solution)/shard_map/all_gather | solution.py:989
  40.3 2.3 collective-permute-start.1
  74.3 30.7 %collective-permute-start.12 = (bf16[1152,384]{1,0:T(8,128)(2,1)}, bf16[1152,384]{1,0:T(8,128)(2,1)S(1)}, u32[]{:S(2)}, u32[]{:S(2)}) collective-permute-start(bf16[1152,384]{1,0:T(8,128)(2,1)} %get-tuple-element.98.ka_ref), channel_id=1, source_target_pairs={{0,4},{4,0},{1,5},{5,1},{2,6},{6,2},{3,7},{7,3},{8,12},{12,8},{9,1... | collective-permute-start | bytes 2654216 | tf_op jit(solution)/shard_map/ppermute | solution.py:924
  126.9 3.9 collective-permute-start.13
  133.9 46.1 %all-to-all-start = ((bf16[4,144,1536]{2,1,0:T(8,128)(2,1)}), bf16[4,144,1536]{2,1,0:T(8,128)(2,1)S(1)}, u32[]{:S(2)}, u32[]{:S(2)}) async-start(bf16[4,144,1536]{2,1,0:T(8,128)(2,1)} %add_convert_fusion.3), calls=%async_computation | async-start | bytes 3538944 | tf_op jit(solution)/shard_map/all_to_all | solution.py:927
  184.9 44.6 %all-to-all-start.1 = ((bf16[4,144,1536]{2,1,0:T(8,128)(2,1)}), bf16[4,144,1536]{2,1,0:T(8,128)(2,1)S(1)}, u32[]{:S(2)}, u32[]{:S(2)}) async-start(bf16[4,144,1536]{2,1,0:T(8,128)(2,1)} %get-tuple-element.109), calls=%async_computation.1 | async-start | bytes 3538944 | tf_op jit(solution)/shard_map/all_to_all | solution.py:927
  188.8 1.6 collective-permute-start.4
  229.5 3.7 collective-permute-start.14
  253.5 4.0 collective-permute-start.15
  260.6 45.3 %all-to-all-start.2 = ((bf16[4,144,1536]{2,1,0:T(8,128)(2,1)}), bf16[4,144,1536]{2,1,0:T(8,128)(2,1)S(1)}, u32[]{:S(2)}, u32[]{:S(2)}) async-start(bf16[4,144,1536]{2,1,0:T(8,128)(2,1)} %add_convert_fusion.2), calls=%async_computation.2 | async-start | bytes 3538944 | tf_op jit(solution)/shard_map/all_to_all | solution.py:927
  264.2 224.3 %reduce-scatter.3.cloned.1.call-start = ((), (), s32[]{:S(2)}) async-start(), calls=%async_computation.13 | async-start | bytes 21233664 | tf_op jit(solution)/shard_map/reduce_scatter | solution.py:1099
  284.4 30.1 %copy-start.4 = (bf16[1536,384]{1,0:T(8,128)(2,1)S(1)}, bf16[1536,384]{1,0:T(8,128)(2,1)}, u32[]{:S(2)}) copy-start(bf16[1536,384]{1,0:T(8,128)(2,1)} %convolution_convert_fusion.1.refs_9_) | copy-start | bytes 3538948
  315.6 44.5 %all-to-all-start.3 = ((bf16[4,144,1536]{2,1,0:T(8,128)(2,1)}), bf16[4,144,1536]{2,1,0:T(8,128)(2,1)S(1)}, u32[]{:S(2)}, u32[]{:S(2)}) async-start(bf16[4,144,1536]{2,1,0:T(8,128)(2,1)} %get-tuple-element.125), calls=%async_computation.3 | async-start | bytes 3538944 | tf_op jit(solution)/shard_map/all_to_all | solution.py:927
  330.1 5.6 collective-permute-start.16
  360.1 46.3 %all-to-all-start.4 = ((bf16[4,144,1536]{2,1,0:T(8,128)(2,1)}), bf16[4,144,1536]{2,1,0:T(8,128)(2,1)S(1)}, u32[]{:S(2)}, u32[]{:S(2)}) async-start(bf16[4,144,1536]{2,1,0:T(8,128)(2,1)} %add_convert_fusion.1), calls=%async_computation.4 | async-start | bytes 3538944 | tf_op jit(solution)/shard_map/all_to_all | solution.py:927
  364.2 3.8 collective-permute-start.17
  412.0 46.8 %all-to-all-start.5 = ((bf16[4,144,1536]{2,1,0:T(8,128)(2,1)}), bf16[4,144,1536]{2,1,0:T(8,128)(2,1)S(1)}, u32[]{:S(2)}, u32[]{:S(2)}) async-start(bf16[4,144,1536]{2,1,0:T(8,128)(2,1)} %get-tuple-element.135), calls=%async_computation.5 | async-start | bytes 3538944 | tf_op jit(solution)/shard_map/all_to_all | solution.py:927
  417.2 165.1 %reduce-scatter.5.cloned.1.call-start = ((), (), s32[]{:S(2)}) async-start(), calls=%async_computation.14 | async-start | bytes 10616832 | tf_op jit(solution)/shard_map/reduce_scatter | solution.py:1099
  417.4 41.4 %collective-permute-start.19 = (bf16[1152,384]{1,0:T(8,128)(2,1)}, bf16[1152,384]{1,0:T(8,128)(2,1)}, u32[]{:S(2)}, u32[]{:S(2)}) collective-permute-start(bf16[1152,384]{1,0:T(8,128)(2,1)} %get-tuple-element.146), channel_id=1, source_target_pairs={{0,4},{4,0},{1,5},{5,1},{2,6},{6,2},{3,7},{7,3},{8,12},{12,8},{9,1... | collective-permute-start | bytes 2654216 | tf_op jit(solution)/shard_map/ppermute | solution.py:924
  468.7 6.8 %collective-permute-start.20 = (bf16[4,144,1536]{2,1,0:T(8,128)(2,1)}, bf16[4,144,1536]{2,1,0:T(8,128)(2,1)S(1)}, u32[]{:S(2)}, u32[]{:S(2)}) collective-permute-start(bf16[4,144,1536]{2,1,0:T(8,128)(2,1)} %get-tuple-element.150), channel_id=1, source_target_pairs={{0,8},{8,0},{16,24},{24,16},{1,9},{9,1},{17,25},{25,17},{2,10},{10... | collective-permute-start | bytes 5308424 | tf_op jit(solution)/shard_map/ppermute | solution.py:924
  482.9 55.3 %all-to-all-start.6 = ((bf16[4,144,1536]{2,1,0:T(8,128)(2,1)}), bf16[4,144,1536]{2,1,0:T(8,128)(2,1)S(1)}, u32[]{:S(2)}, u32[]{:S(2)}) async-start(bf16[4,144,1536]{2,1,0:T(8,128)(2,1)} %add_convert_fusion), calls=%async_computation.6 | async-start | bytes 3538944 | tf_op jit(solution)/shard_map/all_to_all | solution.py:927
  488.3 39.1 %collective-permute-start.18 = (bf16[4,144,1536]{2,1,0:T(8,128)(2,1)S(1)}, bf16[4,144,1536]{2,1,0:T(8,128)(2,1)}, u32[]{:S(2)}, u32[]{:S(2)}) collective-permute-start(bf16[4,144,1536]{2,1,0:T(8,128)(2,1)S(1)} %copy-done.2), channel_id=1, source_target_pairs={{0,8},{8,0},{16,24},{24,16},{1,9},{9,1},{17,25},{25,17},{2,10},{10... | collective-permute-start | bytes 5308424 | tf_op jit(solution)/shard_map/ppermute | solution.py:924
  494.8 1.9 collective-permute-start.21
  497.7 6.1 collective-permute-start.22
  504.5 5.6 collective-permute-start.23
  511.8 8.5 %collective-permute-start.24 = (f32[24,1536]{1,0:T(8,128)}, f32[24,1536]{1,0:T(8,128)}, u32[]{:S(2)}, u32[]{:S(2)}) collective-permute-start(f32[24,1536]{1,0:T(8,128)} %add.213), channel_id=1, source_target_pairs={{0,1},{1,0},{2,3},{3,2},{4,5},{5,4},{6,7},{7,6},{8,9},{9,8},{10,11... | collective-permute-start | bytes 442376 | tf_op jit(solution)/shard_map/ppermute | solution.py:924
  521.3 14.6 %collective-permute-start.25 = (f32[24,1536]{1,0:T(8,128)S(1)}, f32[24,1536]{1,0:T(8,128)S(1)}, u32[]{:S(2)}, u32[]{:S(2)}) collective-permute-start(f32[24,1536]{1,0:T(8,128)S(1)} %add.214), channel_id=1, source_target_pairs={{0,2},{1,3},{2,0},{3,1},{4,6},{5,7},{6,4},{7,5},{8,10},{9,11},{10,... | collective-permute-start | bytes 442376 | tf_op jit(solution)/shard_map/ppermute | solution.py:924
  536.6 10.6 %collective-permute-start.26 = (f32[24,1536]{1,0:T(8,128)}, f32[24,1536]{1,0:T(8,128)}, u32[]{:S(2)}, u32[]{:S(2)}) collective-permute-start(f32[24,1536]{1,0:T(8,128)} %add.215), channel_id=1, source_target_pairs={{0,8},{8,0},{16,24},{24,16},{1,9},{9,1},{17,25},{25,17},{2,10},{10... | collective-permute-start | bytes 442376 | tf_op jit(solution)/shard_map/ppermute | solution.py:924
  543.4 50.6 %all-to-all-start.7 = ((bf16[4,144,1536]{2,1,0:T(8,128)(2,1)}), bf16[4,144,1536]{2,1,0:T(8,128)(2,1)S(1)}, u32[]{:S(2)}, u32[]{:S(2)}) async-start(bf16[4,144,1536]{2,1,0:T(8,128)(2,1)} %after_back.1), calls=%async_computation.7 | async-start | bytes 3538944 | tf_op jit(solution)/shard_map/all_to_all | solution.py:927
  593.4 4.7 collective-permute-start.28
  598.0 26.9 %collective-permute-start.27 = (bf16[4,144,1536]{2,1,0:T(8,128)(2,1)}, bf16[4,144,1536]{2,1,0:T(8,128)(2,1)}, u32[]{:S(2)}, u32[]{:S(2)}) collective-permute-start(bf16[4,144,1536]{2,1,0:T(8,128)(2,1)} %copy_after.1), channel_id=1, source_target_pairs={{0,8},{8,0},{16,24},{24,16},{1,9},{9,1},{17,25},{25,17},{2,10},{10... | collective-permute-start | bytes 5308424 | tf_op jit(solution)/shard_map/ppermute | solution.py:924
  598.1 3.8 collective-permute-start.29
  601.9 3.7 collective-permute-start.30
  605.7 3.7 collective-permute-start.31
  609.4 6.2 collective-permute-start.32
  (38 other events, 195.8 us)
Sparse Core Ops, SparseCore 0:
  10.5 53.2 all-gather.3
  66.2 37.9 all-gather.5
  106.7 98.7 all-gather.7
  315.8 144.9 reduce-scatter.2
  482.4 77.6 reduce-scatter.4

commit v4 on v3

--- a/solution.py
+++ b/solution.py
@@ -267,6 +267,24 @@
         cost_estimate=cost(0, 0),
         name="copy_after",
     )(x, dep)
+
+
+def fold_kernel(x_ref, y_ref, dep_ref, o_ref):
+    o_ref[...] = (x_ref[...].astype(f32) + y_ref[...].astype(f32)).astype(bf)
+
+
+def fold_after(x, y, dep):
+    block = pl.BlockSpec((1,) + x.shape[1:], lambda i: (i, 0, 0))
+    return pl.pallas_call(
+        fold_kernel,
+        grid=(x.shape[0],),
+        in_specs=[block, block, pl.BlockSpec(memory_space=pl.ANY)],
+        out_specs=block,
+        out_shape=shape(x.shape),
+        compiler_params=params(),
+        cost_estimate=cost(0, 0),
+        name="fold_after",
+    )(x, y, dep)
 
 
 def own_specs(ci, ct, D):
@@ -710,50 +728,68 @@
     )(x, dep)
 
 
-def attn_fwd_kernel(heads, img, live, q_ref, ka_ref, kb_ref, a_ref, lse_ref):
-    T = ka_ref.shape[0]
+def attn_fwd_kernel(heads, img, live, last, q_ref, kv_ref, *refs):
+    T = kv_ref.shape[0]
     bq = q_ref.shape[0]
     lane = lax.broadcasted_iota(jnp.int32, (1, 256), 1)
     lane1 = lax.broadcasted_iota(jnp.int32, (1, 128), 1)
     keep = lax.broadcasted_iota(jnp.int32, (1, T - img), 1) < live - img
     q = q_ref[...]
     acc = jnp.zeros((bq, 256), f32)
-    lse_tile = jnp.zeros((bq, 128), f32)
+    tile = jnp.zeros((bq, 128), f32)
+    if last:
+        acc_ref, stat_ref, a_ref, lse_ref = refs
+        before, stat = acc_ref[...], stat_ref[...]
     for h in range(heads):
         qm = jnp.where((lane >> 6) == h, q, jnp.zeros_like(q))
-        parts = []
-        for kv in (ka_ref, kb_ref):
-            parts.append((dotf(qm, kv[:img, :256], NT), kv, 0, img))
-            s = dotf(qm, kv[img:, :256], NT)
-            parts.append((jnp.where(keep, s, -1e30), kv, img, T))
-        m = functools.reduce(jnp.maximum, [jnp.max(p[0], axis=1, keepdims=True) for p in parts])
-        l = jnp.zeros((bq, 1), f32)
-        pv = jnp.zeros((bq, 256), f32)
-        for s, kv, lo, hi in parts:
-            e = jnp.exp(s - m)
-            l = l + jnp.sum(e, axis=1, keepdims=True)
-            pv = pv + dotf(e.astype(bf), kv[lo:hi, 128:384], NN)
-        acc = jnp.where((lane >> 6) == h + 1, pv / l, acc)
-        lse_tile = jnp.where(lane1 == h, m + jnp.log(l), lse_tile)
-    a_ref[...] = acc[:, 64:256].astype(bf)
-    lse_ref[...] = lse_tile.T[:8]
-
-
-def attn_fwd(q, kv_a, kv_b, img, live, bq=384, heads=3):
+        s_img = dotf(qm, kv_ref[:img, :256], NT)
+        s_txt = jnp.where(keep, dotf(qm, kv_ref[img:, :256], NT), -1e30)
+        m = jnp.maximum(jnp.max(s_img, axis=1, keepdims=True), jnp.max(s_txt, axis=1, keepdims=True))
+        if last:
+            m_old = stat[:, h : h + 1]
+            m = jnp.maximum(m, m_old)
+        e_img, e_txt = jnp.exp(s_img - m), jnp.exp(s_txt - m)
+        l = jnp.sum(e_img, axis=1, keepdims=True) + jnp.sum(e_txt, axis=1, keepdims=True)
+        pv = dotf(e_img.astype(bf), kv_ref[:img, 128:384], NN) + dotf(e_txt.astype(bf), kv_ref[img:, 128:384], NN)
+        if last:
+            scale = jnp.exp(m_old - m)
+            l = l + stat[:, heads + h : heads + h + 1] * scale
+            pv = (pv + before * scale) / l
+            tile = jnp.where(lane1 == h, m + jnp.log(l), tile)
+        else:
+            tile = jnp.where(lane1 == h, m, jnp.where(lane1 == heads + h, l, tile))
+        acc = jnp.where((lane >> 6) == h + 1, pv, acc)
+    if last:
+        a_ref[...] = acc[:, 64:256].astype(bf)
+        lse_ref[...] = tile.T[:8]
+    else:
+        refs[0][...] = acc
+        refs[1][...] = tile
+
+
+def attn_half(q, kv, img, live, before=None, bq=384, heads=3):
     T = q.shape[0]
-    return pl.pallas_call(
-        functools.partial(attn_fwd_kernel, heads, img, live),
+    block = lambda width: pl.BlockSpec((bq, width), lambda i: (i, 0))
+    last = before is not None
+    if last:
+        outs = [shape((T, 192)), shape((8, T), f32)]
+        out_specs = [block(192), pl.BlockSpec((8, bq), lambda i: (0, i))]
+    else:
+        outs = [shape((T, 256), f32), shape((T, 128), f32)]
+        out_specs = [block(256), block(128)]
+    return pl.pallas_call(
+        functools.partial(attn_fwd_kernel, heads, img, live, last),
         grid=(T // bq,),
-        in_specs=[pl.BlockSpec((bq, 256), lambda i: (i, 0)), full((T, 384)), full((T, 384))],
-        out_specs=[pl.BlockSpec((bq, 192), lambda i: (i, 0)), pl.BlockSpec((8, bq), lambda i: (0, i))],
-        out_shape=[shape((T, 192)), shape((8, T), f32)],
-        compiler_params=params(),
-        cost_estimate=cost(16 * T * T * 256, 4 * T * 384, T * T * 6),
-        name="attn_fwd",
-    )(q, kv_a, kv_b)
-
-
-def attn_bwd_kernel(heads, q_ref, ka_ref, kb_ref, a_ref, da_ref, lse_ref, dq_ref, dka_ref, dkb_ref, daw, delta, dqa):
+        in_specs=[block(256), full((T, 384))] + ([block(256), block(128)] if last else []),
+        out_specs=out_specs,
+        out_shape=outs,
+        compiler_params=params(),
+        cost_estimate=cost(0, 0),
+        name="attn_last" if last else "attn_first",
+    )(q, kv, *(before if last else ()))
+
+
+def attn_bwd_kernel(heads, q_ref, kv_ref, a_ref, da_ref, lse_ref, dep_ref, dq_ref, dkv_ref, daw, delta, dqa):
     step = pl.program_id(0)
     T = q_ref.shape[0]
     lane = lax.broadcasted_iota(jnp.int32, (1, 256), 1)
@@ -768,43 +804,42 @@
         delta[...] = dotf(hm, prod, NT, lax.Precision.HIGHEST)
         dqa[...] = jnp.zeros_like(dqa)
 
+    kw = kv_ref[:, :256]
+    vw = kv_ref[:, 128:384]
     dq = jnp.zeros((T, 256), f32)
-    for kv_ref, out_ref in ((ka_ref, dka_ref), (kb_ref, dkb_ref)):
-        kw = kv_ref[:, :256]
-        vw = kv_ref[:, 128:384]
-        dk = jnp.zeros(kw.shape, f32)
-        dv = jnp.zeros(kw.shape, f32)
-        for h in range(heads):
-            sel = (lane >> 6) == h
-            qm = jnp.where(sel, q_ref[...], jnp.zeros((), bf))
-            dam = jnp.where((lane >> 6) == h + 1, daw[...], jnp.zeros((), bf))
-            p = jnp.exp(dotf(kw, qm, NT) - lse_ref[h : h + 1, :])
-            dv = dv + dotf(p.astype(bf), dam, NN)
-            ds = (p * (dotf(vw, dam, NT) - delta[h : h + 1, :])).astype(bf)
-            dk = dk + dotf(ds, qm, NN)
-            dq = dq + dotf(ds, jnp.where(sel, kw, jnp.zeros((), bf)), TN)
-        out_ref[...] = jnp.concatenate([dk[:, :192], dv[:, 64:256]], axis=1).astype(bf)
+    dk = jnp.zeros(kw.shape, f32)
+    dv = jnp.zeros(kw.shape, f32)
+    for h in range(heads):
+        sel = (lane >> 6) == h
+        qm = jnp.where(sel, q_ref[...], jnp.zeros((), bf))
+        dam = jnp.where((lane >> 6) == h + 1, daw[...], jnp.zeros((), bf))
+        p = jnp.exp(dotf(kw, qm, NT) - lse_ref[h : h + 1, :])
+        dv = dv + dotf(p.astype(bf), dam, NN)
+        ds = (p * (dotf(vw, dam, NT) - delta[h : h + 1, :])).astype(bf)
+        dk = dk + dotf(ds, qm, NN)
+        dq = dq + dotf(ds, jnp.where(sel, kw, jnp.zeros((), bf)), TN)
+    dkv_ref[...] = jnp.concatenate([dk[:, :192], dv[:, 64:256]], axis=1).astype(bf)
     dqa[...] += dq
 
     @pl.when(step == pl.num_programs(0) - 1)
     def _():
-        dq_ref[...] = (dqa[...][:, :192] * DH**-0.5).astype(bf)
-
-
-def attn_bwd(q, kv_a, kv_b, a, da, lse, bk=384, heads=3):
+        dq_ref[...] = dqa[...][:, :192] * DH**-0.5
+
+
+def attn_bwd_half(q, kv, a, da, lse, dep, bk=576, heads=3):
     T = q.shape[0]
     block = pl.BlockSpec((bk, 384), lambda i: (i, 0))
     return pl.pallas_call(
         functools.partial(attn_bwd_kernel, heads),
         grid=(T // bk,),
-        in_specs=[full((T, 256)), block, block, full((T, 192)), full((T, 192)), full((8, T))],
-        out_specs=[full((T, 192)), block, block],
-        out_shape=[shape((T, 192)), shape((T, 384)), shape((T, 384))],
+        in_specs=[full((T, 256)), block, full((T, 192)), full((T, 192)), full((8, T)), pl.BlockSpec(memory_space=pl.ANY)],
+        out_specs=[full((T, 192)), block],
+        out_shape=[shape((T, 192), f32), shape((T, 384))],
         scratch_shapes=[pltpu.VMEM((T, 256), bf), pltpu.VMEM((8, T), f32), pltpu.VMEM((T, 256), f32)],
         compiler_params=params(),
-        cost_estimate=cost(32 * T * T * 256, 8 * T * 384, T * T * 6),
+        cost_estimate=cost(0, 0),
         name="attn_bwd",
-    )(q, kv_a, kv_b, a, da, lse)
+    )(q, kv, a, da, lse, dep)
 
 
 def adam_kernel(f_ref, g_ref, w_ref, m_ref, v_ref, *refs):
@@ -1042,7 +1077,8 @@
             qs.append(q)
             kvs.append(kv)
             kv_gots.append(pp(kv, "ctx", 1))
-        w_mlp = gather(after(wt[:, 10:18].astype(bf).reshape(16, rows, cw), kv_gots[-1]))
+        firsts = [attn_half(qs[n], kvs[n], img, live_rows) for n in slots]
+        w_mlp = gather(after(wt[:, 10:18].astype(bf).reshape(16, rows, cw), kv_gots[-1], firsts[-1][0]))
 
         def fold(send, keep):
             return (keep.astype(f32) + pp(send, "shard", 1).astype(f32)).astype(bf)
@@ -1054,7 +1090,7 @@
         copies = shape((nt, chunk, D))
         attns, lses, o_parts = [], [], []
         for n in slots:
-            a, lse = attn_fwd(qs[n], kvs[n], kv_gots[n], img, live_rows)
+            a, lse = attn_half(qs[n], kv_gots[n], img, live_rows, firsts[n])
             attns.append(a)
             lses.append(lse)
             o_parts.append(swap(fold(*oproj(core_arr, a, w_o, nt, img)), "tensor"))
@@ -1134,10 +1170,12 @@
             doi, dot, da = grad_attn(core_arr, mine, pp(mine, "shard", 1), w_o, img, tpad)
             dois.append(doi)
             dots.append(dot)
-            dq, dkv_a, dkv_b = attn_bwd(qs[n], kvs[n], kv_gots[n], attns[n], da, lses[n])
+            dq_b, dkv_b = attn_bwd_half(qs[n], kv_gots[n], attns[n], da, lses[n], da)
+            dq_a, dkv_a = attn_bwd_half(qs[n], kvs[n], attns[n], da, lses[n], dkv_b)
+            dq = (dq_a + dq_b).astype(bf)
             dqs.append(dq)
             dkv_own.append(dkv_a)
-            dkv_gots.append(pp(after(dkv_b, y_part), "ctx", 1))
+            dkv_gots.append(pp(dkv_b, "ctx", 1))
             out_own, sums = own_call(
                 after_down_kernel,
                 "after_down",
@@ -1164,13 +1202,13 @@
         d_parts, dkv_img, dkv_txt, qv_sums, end_sums = [], [], [], [], []
         for n in slots:
             send, keep, kvi, kvt, qv, sums = grad_in(
-                core_arr, [out_owns[n], one_all], dqs[n], dkv_own[n], dkv_gots[n], nis[n], nts[n], w_one, nt, txt
+                core_arr, [low_sums[n], one_all], dqs[n], dkv_own[n], dkv_gots[n], nis[n], nts[n], w_one, nt, txt
             )
             dkv_img.append(kvi)
             dkv_txt.append(kvt)
             qv_sums.append(qv)
             end_sums.append(sums)
-            tie = fold(send, keep)
+            tie = fold_after(keep, pp(send, "shard", 1), out_owns[n])
             d_parts.append(swap(tie, "tensor"))
         q_grads = []
         for s, (part, left, right) in enumerate(((slice(0, img), his, dkv_img), (slice(img, T), hts, dkv_txt))):

time: 643 us -> 633 us (0.984)
  waiting for transfers between devices: 219 us -> 191 us
  Pallas kernels: 205 us -> 222 us
    ppermute x30, waiting for transfers between devices: 100 us -> 67.8 us  [pp(): return lax.ppermute(x, axis, [(i, i ^ xor) for i in range(sizes[axis])])]
    pallas_call x2 -> x5, Pallas kernels: 48 us -> 63.6 us  [the longest x2 33.9 us: attn_bwd_half(): pl.pallas_call(functools.partial(attn_bwd_kernel, heads), grid=(T // bk,)...]
  transfers between devices with their start and end apart: 46 -> 46, of which waited for: 29 -> 30; matrix products, arithmetic and copies ran while one was open for 17% -> 18% of each run, Pallas kernels for 27% -> 30%
where the time goes in v4:
time: 633 us; the launch traced here: 627 us
  Pallas kernels  222 us (35%)
  waiting for transfers between devices  191 us (30%)
  starting transfers between devices  62.6 us (10%)
  other arithmetic  47.9 us (8%)
  local copies, waits for them, and re-layouts  46.1 us (7%)
  matrix products  40.3 us (6%)
  between operations  17.3 us (3%)
    all_to_all x8, waiting for transfers between devices, swap(): return lax.all_to_all(x, axis, 0, 0, tiled=True)  90.6 us
    ppermute x30, waiting for transfers between devices, pp(): return lax.ppermute(x, axis, [(i, i ^ xor) for i in range(sizes[axis])])  67.8 us
    pallas_call x3, Pallas kernels, seg_call(): pl.pallas_call(kernel, grid_spec=pltpu.PrefetchScalarGridSpec(num_scalar_...  40.3 us
    dot_general x14, matrix products, dotf(): lax.dot_general(a, b, dims, preferred_element_type=f32, precision=precision)  34.3 us
    pallas_call x2, Pallas kernels, attn_bwd_half(): pl.pallas_call(functools.partial(attn_bwd_kernel, heads), grid=(T // bk,)...  33.9 us
    all_to_all x8, starting transfers between devices, swap(): return lax.all_to_all(x, axis, 0, 0, tiled=True)  32.2 us
    all_gather x3, waiting for transfers between devices, gather(): return lax.all_gather(w, everyone, axis=1, tiled=True)  27.5 us
    ppermute x30, starting transfers between devices, pp(): return lax.ppermute(x, axis, [(i, i ^ xor) for i in range(sizes[axis])])  25.8 us
  transfers between devices with their start and end apart: 46, of which 30 were waited for; matrix products, arithmetic and copies ran while one was open for 18% of the time, Pallas kernels for 30%

profile of v4, /device:TPU:0, one launch (start us, length us, event | category | flops | bytes accessed | tf_op | source)
XLA Modules:
  0.0 626.6 jit_solution(8264413034754231895)
XLA Ops:
  13.6 5.0 mod_partial.1
  29.8 3.7 collective-permute-start.11
  44.0 4.0 select_bitcast_fusion.xi_ref.refs_1_
  50.1 13.6 %all-gather.4.cloned.1.call-done.w_ref = bf16[6,1536,384]{2,1,0:T(8,128)(2,1)} async-done(((bf16[6,192,384]{2,1,0:T(8,128)(2,1)}), bf16[6,1536,384]{2,1,0:T(8,128)(2,1)}) %all-gather.4.cloned.1.call-update) | async-done | bytes 7077904 | tf_op jit(solution)/shard_map/all_gather | solution.py:1024
  63.7 11.1 %qkv.1 = (bf16[1024,1536]{1,0:T(8,128)(2,1)}, bf16[128,1536]{1,0:T(8,128)(2,1)}, bf16[1024,1536]{1,0:T(8,128)(2,1)}, bf16[128,1536]{1,0:T(8,128)(2,1)}, bf16[115...) custom-call(s32[1]{0:T(128)} %bitcast.core_ref, bf16[1024,1536]{1,0:T(8,128)(2,1)} %select_bitcast_fusion.xi_ref.refs_1_, ...), custom_call_target="tpu_custom_call" | custom-call | flops 1024 | bytes 1024 | tf_op jit(solution)/shard_map/qkv/pallas_call | solution.py:182
  76.0 4.8 bitcast_convert_fusion
  84.8 10.2 %attn_first.1 = (f32[1152,256]{1,0:T(8,128)}, f32[1152,128]{1,0:T(8,128)}) custom-call(bf16[1152,256]{1,0:T(8,128)(2,1)} %get-tuple-element.99.q_ref, bf16[1152,384]{1,0:T(8,128)(2,1)} %get-tuple-element.100.kv_ref), custom_call_target="tpu_custom_call" | custom-call | flops 1024 | bytes 1024 | tf_op jit(solution)/shard_map/attn_first/pallas_call | solution.py:780
  95.1 9.3 %collective-permute-done.12.kv_ref = bf16[1152,384]{1,0:T(8,128)(2,1)S(1)} collective-permute-done((bf16[1152,384]{1,0:T(8,128)(2,1)}, bf16[1152,384]{1,0:T(8,128)(2,1)S(1)}, u32[]{:S(2)}, u32[]{:S(2)}) %collective-permute-start.12) | collective-permute-done | bytes 884768 | tf_op jit(solution)/shard_map/ppermute | solution.py:959
  105.3 15.3 %attn_last.1 = (bf16[1152,192]{1,0:T(8,128)(2,1)}, f32[8,1152]{1,0:T(8,128)}) custom-call(bf16[1152,256]{1,0:T(8,128)(2,1)} %get-tuple-element.99.q_ref, bf16[1152,384]{1,0:T(8,128)(2,1)} %copy-done.15, f32[1152,256]{1,0:T(8,128)} %get-tuple-element.101.refs_0_, f32[1152,128]{1,0:T(8,128)} %get-tuple-element.102.refs_1_), custom_call_target="tpu_custom_call" | custom-call | flops 1024 | bytes 1024 | tf_op jit(solution)/shard_map/attn_last/pallas_call | solution.py:780
  120.6 4.8 oproj.1
  125.4 3.9 collective-permute-done.13
  132.4 4.8 all-to-all-start
  138.0 9.6 %zeros.1 = (bf16[24576,384]{1,0:T(8,128)(2,1)}, bf16[12288,384]{1,0:T(8,128)(2,1)}) custom-call(s32[1]{0:T(128)} %bitcast.core_ref), custom_call_target="tpu_custom_call" | custom-call | flops 1024 | bytes 1024 | tf_op jit(solution)/shard_map/zeros/pallas_call | solution.py:408
  147.6 31.1 %all-to-all-done.refs_5_ = bf16[4,144,1536]{2,1,0:T(8,128)(2,1)S(1)} async-done(((bf16[4,144,1536]{2,1,0:T(8,128)(2,1)}), bf16[4,144,1536]{2,1,0:T(8,128)(2,1)S(1)}, u32[]{:S(2)}, u32[]{:S(2)}) %all-to-all-start) | async-done | bytes 1769504 | tf_op jit(solution)/shard_map/all_to_all | solution.py:962
  179.9 3.7 after_attn.1
  183.6 3.7 all-to-all-start.1
  189.7 13.9 %all-gather.8.cloned.1.call-done.w_ref = bf16[16,1536,384]{2,1,0:T(8,128)(2,1)} async-done(((bf16[16,192,384]{2,1,0:T(8,128)(2,1)}), bf16[16,1536,384]{2,1,0:T(8,128)(2,1)}) %all-gather.8.cloned.1.call-update) | async-done | bytes 18874384 | tf_op jit(solution)/shard_map/all_gather | solution.py:1024
  203.6 10.6 %grad_gate.1 = (bf16[1024,1536]{1,0:T(8,128)(2,1)}, bf16[128,1536]{1,0:T(8,128)(2,1)}, f32[2,1024,384]{2,1,0:T(8,128)}, f32[2,128,384]{2,1,0:T(8,128)}) custom-call(s32[1]{0:T(128)} %bitcast.core_ref, bf16[1024,1536]{1,0:T(8,128)(2,1)} %multiply_bitcast_fusion.ci_ref.refs_3_, bf16[128,1536]{1,0:T(8,128)(2,1)} %pad.13.ct_ref.refs_4_, ...), custom_call_target="tpu_custom_call" | custom-call | flops 1024 | bytes 1024 | tf_op jit(solution)/shard_map/grad_gate/pallas_call | solution.py:384
  214.2 13.8 %all-to-all-done.1.mine = bf16[4,144,1536]{2,1,0:T(8,128)(2,1)S(1)} async-done(((bf16[4,144,1536]{2,1,0:T(8,128)(2,1)}), bf16[4,144,1536]{2,1,0:T(8,128)(2,1)S(1)}, u32[]{:S(2)}, u32[]{:S(2)}) %all-to-all-start.1) | async-done | bytes 1769504 | tf_op jit(solution)/shard_map/all_to_all | solution.py:962
  232.9 19.1 %mlp.1 = (bf16[1024,1536]{1,0:T(8,128)(2,1)}, bf16[128,1536]{1,0:T(8,128)(2,1)}, bf16[2,1024,384]{2,1,0:T(8,128)(2,1)}, bf16[2,128,384]{2,1,0:T(8,128)(2,1)}, bf...) custom-call(s32[1]{0:T(128)} %bitcast.core_ref, ...), custom_call_target="tpu_custom_call" | custom-call | flops 1024 | bytes 1024 | tf_op jit(solution)/shard_map/mlp/pallas_call | solution.py:384
  252.2 3.8 collective-permute-done.15
  264.6 5.1 fusion.1
  283.0 21.5 %all-to-all-done.2.refs_7_ = bf16[4,144,1536]{2,1,0:T(8,128)(2,1)S(1)} async-done(((bf16[4,144,1536]{2,1,0:T(8,128)(2,1)}), bf16[4,144,1536]{2,1,0:T(8,128)(2,1)S(1)}, u32[]{:S(2)}, u32[]{:S(2)}) %all-to-all-start.2) | async-done | bytes 1769504 | tf_op jit(solution)/shard_map/all_to_all | solution.py:962
  305.7 4.8 after_mlp.1
  314.2 4.0 all-to-all-start.3
  318.2 10.7 %down.1 = (bf16[4,144,1536]{2,1,0:T(8,128)(2,1)}, bf16[4,144,1536]{2,1,0:T(8,128)(2,1)}) custom-call(s32[1]{0:T(128)} %bitcast.core_ref, bf16[2,1024,384]{2,1,0:T(8,128)(2,1)} %get-tuple-element.130.gi, bf16[2,128,384]{2,1,0:T(8,128)(2,1)} %get-tuple-element.131.gt, bf16[16,1536,384]{2,1,0:T(8,128)(2,1)} %all-gather.8.cloned.1.call-done.w_ref), custom_call_target="tpu_custom_call" | custom-call | flops 1024 | bytes 1024 | tf_op jit(solution)/shard_map/down/pallas_call | solution.py:384
  328.8 4.6 collective-permute-done.16
  336.6 22.5 %all-to-all-done.3.mine = bf16[4,144,1536]{2,1,0:T(8,128)(2,1)S(1)} async-done(((bf16[4,144,1536]{2,1,0:T(8,128)(2,1)}), bf16[4,144,1536]{2,1,0:T(8,128)(2,1)S(1)}, u32[]{:S(2)}, u32[]{:S(2)}) %all-to-all-start.3) | async-done | bytes 1769504 | tf_op jit(solution)/shard_map/all_to_all | solution.py:962
  362.8 3.7 collective-permute-done.17.other
  367.7 5.5 grad_attn.1
  373.2 16.7 %attn_bwd.2 = (f32[1152,192]{1,0:T(8,128)}, bf16[1152,384]{1,0:T(8,128)(2,1)}) custom-call(bf16[1152,256]{1,0:T(8,128)(2,1)} %get-tuple-element.99.q_ref, bf16[1152,384]{1,0:T(8,128)(2,1)} %copy-done.15, bf16[1152,192]{1,0:T(8,128)(2,1)} %get-tuple-element.103.a_ref, bf16[1152,192]{1,0:T(8,128)(2,1)} %get-tuple-element.136.da_ref.dep_ref, ...), custom_call_target="tpu_custom_call" | custom-call | flops 1024 | bytes 1024 | tf_op jit(solution)/shard_map/attn_bwd/pallas_call | solution.py:832
  389.9 17.2 %attn_bwd.3 = (f32[1152,192]{1,0:T(8,128)}, bf16[1152,384]{1,0:T(8,128)(2,1)}) custom-call(bf16[1152,256]{1,0:T(8,128)(2,1)} %get-tuple-element.99.q_ref, bf16[1152,384]{1,0:T(8,128)(2,1)} %get-tuple-element.100.kv_ref, bf16[1152,192]{1,0:T(8,128)(2,1)} %get-tuple-element.103.a_ref, bf16[1152,192]{1,0:T(8,128)(2,1)} %get-tuple-element.136.da_ref.dep_ref, ...), custom_call_target="tpu_custom_call" | custom-call | flops 1024 | bytes 1024 | tf_op jit(solution)/shard_map/attn_bwd/pallas_call | solution.py:832
  411.0 4.8 after_down.1
  415.8 5.1 all-to-all-start.5
  432.0 13.1 %collective-permute-done.19.b_ref = bf16[1152,384]{1,0:T(8,128)(2,1)} collective-permute-done((bf16[1152,384]{1,0:T(8,128)(2,1)}, bf16[1152,384]{1,0:T(8,128)(2,1)}, u32[]{:S(2)}, u32[]{:S(2)}) %collective-permute-start.19) | collective-permute-done | bytes 884768 | tf_op jit(solution)/shard_map/ppermute | solution.py:959
  445.1 8.8 %grad_in.1 = (bf16[4,144,1536]{2,1,0:T(8,128)(2,1)}, bf16[4,144,1536]{2,1,0:T(8,128)(2,1)}, bf16[1024,384]{1,0:T(8,128)(2,1)}, bf16[128,384]{1,0:T(8,128)(2,1)}, f32[8,384]{1,0:T(8,128)}, /*index=5*/f32[8,1536]{1,0:T(8,128)}) custom-call(s32[1]{0:T(128)} %bitcast.core_ref, f32[16,1536]{1,0:T(8,128)} %get-tuple-element.145.dep_ref.low_ref, ...), custom_call_target="tpu_custom_call" | custom-call | flops 1024 | bytes 1024 | tf_op jit(solution)/shard_map/grad_in/pallas_call | solution.py:619
  454.0 5.1 fusion.9
  463.6 4.1 fold_after.1
  488.6 4.5 collective-permute-done.22
  510.5 4.7 collective-permute-start.25
  516.7 4.0 join_tokens.2
  520.7 4.4 collective-permute-done.25
  528.6 4.0 after_back.1
  532.6 3.8 all-to-all-start.7
  538.1 19.4 %adam.1 = (f32[2,18,192,384]{3,2,1,0:T(8,128)}, f32[2,18,192,384]{3,2,1,0:T(8,128)}, f32[2,18,192,384]{3,2,1,0:T(8,128)}, f32[2,18,192,384]{3,2,1,0:T(8,128)}) custom-call(f32[2,8]{1,0:T(2,128)} %min.22.f_ref, bf16[2,8,192,384]{3,2,1,0:T(8,128)(2,1)} %bitcast.181, f32[2,18,192,384]{3,2,1,0:T(8,128)} %bitcast.164, f32[2,18,192,384]{3,2,1,0:T(8,128)} %bitcast.168, ...), custom_call_target="tpu_custom_call" | custom-call | flops 1024 | bytes 1024 | tf_op jit(solution)/shard_map/adam/pallas_call | solution.py:857
  560.0 11.5 %adam_mod.1 = (f32[2,18,192,384]{3,2,1,0:T(8,128)}, f32[2,18,192,384]{3,2,1,0:T(8,128)}, f32[2,18,192,384]{3,2,1,0:T(8,128)}, f32[2,18,192,384]{3,2,1,0:T(8,128)}) custom-call(f32[192,2]{1,0:T(8,128)} %get-tuple-element.236.sc_ref, ...), custom_call_target="tpu_custom_call", output_to_operand_aliasing={{0}: (6, {}), {1}: (7, {}), {2}: (8, {}), {3}: (9, {})} | custom-call | flops 1024 | bytes 1024 | tf_op jit(solution)/shard_map/adam_mod/pallas_call | solution.py:930
  605.6 7.2 %adam_one.1 = (f32[2,18,192,384]{3,2,1,0:T(8,128)}, f32[2,18,192,384]{3,2,1,0:T(8,128)}, f32[2,18,192,384]{3,2,1,0:T(8,128)}, f32[2,18,192,384]{3,2,1,0:T(8,128)}) custom-call(f32[2,4]{1,0:T(2,128)} %min.24.f_ref, ...), custom_call_target="tpu_custom_call", output_to_operand_aliasing={{0}: (5, {}), {1}: (6, {}), {2}: (7, {}), {3}: (8, {})} | custom-call | flops 1024 | bytes 1024 | tf_op jit(solution)/shard_map/adam_one/pallas_call | solution.py:899
  614.1 4.0 join_tokens.3
  (274 shorter events, 184.8 us)
Async XLA Ops:
  7.2 56.5 %all-gather.4.cloned.1.call-start = ((), (), s32[]{:S(2)}) async-start(), calls=%async_computation.10 | async-start | bytes 7962624 | tf_op jit(solution)/shard_map/all_gather | solution.py:1024
  10.2 110.5 %all-gather.6.cloned.1.call-start = ((), (), s32[]{:S(2)}) async-start(), calls=%async_computation.11 | async-start | bytes 2654208 | tf_op jit(solution)/shard_map/all_gather | solution.py:1024
  10.2 33.8 %collective-permute-start = (bf16[1,1024,1536]{2,1,0:T(8,128)(2,1)}, bf16[1,1024,1536]{2,1,0:T(8,128)(2,1)}, u32[]{:S(2)}, u32[]{:S(2)}) collective-permute-start(bf16[1,1024,1536]{2,1,0:T(8,128)(2,1)} %param.12), channel_id=1, source_target_pairs={{0,8},{8,0},{16,24},{24,16},{1,9},{9,1},{17,25},{25,17},{2,10},{10... | collective-permute-start | bytes 9437192 | tf_op jit(solution)/shard_map/ppermute | solution.py:959
  13.6 25.3 %copy-start.26 = (f32[2,14,1536]{2,0,1:T(2,128)S(1)}, f32[2,14,1536]{2,0,1:T(2,128)}, u32[]{:S(2)}) copy-start(f32[2,14,1536]{2,0,1:T(2,128)} %param.19) | copy-start | bytes 516100
  18.7 1.4 collective-permute-start.5
  20.9 6.5 %collective-permute-start.8 = (f32[2,6,2,384]{3,2,1,0:T(2,128)S(1)}, f32[2,6,2,384]{3,2,1,0:T(2,128)S(1)}, u32[]{:S(2)}, u32[]{:S(2)}) collective-permute-start(f32[2,6,2,384]{3,2,1,0:T(2,128)S(1)} %add.189), channel_id=1, source_target_pairs={{0,20},{4,16},{8,28},{12,24},{16,4},{20,0},{24,12},{28,8},{1,21},{... | collective-permute-start | bytes 110600 | tf_op jit(solution)/shard_map/ppermute | solution.py:1048
  24.6 5.0 collective-permute-start.7
  25.1 4.7 collective-permute-start.6
  29.8 6.6 %collective-permute-start.11 = (f32[2,6,2,384]{3,2,1,0:T(2,128)S(1)}, f32[2,6,2,384]{3,2,1,0:T(2,128)S(1)}, u32[]{:S(2)}, u32[]{:S(2)}) collective-permute-start(f32[2,6,2,384]{3,2,1,0:T(2,128)S(1)} %add_add_fusion), channel_id=1, source_target_pairs={{0,3},{1,2},{2,1},{3,0},{4,7},{5,6},{6,5},{7,4},{8,11},{9,10},{10,... | collective-permute-start | bytes 110600 | tf_op jit(solution)/shard_map/ppermute | solution.py:959
  33.6 4.9 collective-permute-start.10
  33.6 4.9 collective-permute-start.9
  34.3 1.2 collective-permute-start.3
  35.5 12.5 %collective-permute-start.2 = (bf16[1,1024,1536]{2,1,0:T(8,128)(2,1)}, bf16[1,1024,1536]{2,1,0:T(8,128)(2,1)S(1)}, u32[]{:S(2)}, u32[]{:S(2)}) collective-permute-start(bf16[1,1024,1536]{2,1,0:T(8,128)(2,1)} %param.22), channel_id=1, source_target_pairs={{0,8},{8,0},{16,24},{24,16},{1,9},{9,1},{17,25},{25,17},{2,10},{10... | collective-permute-start | bytes 9437192 | tf_op jit(solution)/shard_map/ppermute | solution.py:959
  39.8 163.8 %all-gather.8.cloned.1.call-start = ((), (), s32[]{:S(2)}) async-start(), calls=%async_computation.12 | async-start | bytes 21233664 | tf_op jit(solution)/shard_map/all_gather | solution.py:1024
  39.8 2.4 collective-permute-start.1
  74.8 29.6 %collective-permute-start.12 = (bf16[1152,384]{1,0:T(8,128)(2,1)}, bf16[1152,384]{1,0:T(8,128)(2,1)S(1)}, u32[]{:S(2)}, u32[]{:S(2)}) collective-permute-start(bf16[1152,384]{1,0:T(8,128)(2,1)} %get-tuple-element.100.kv_ref), channel_id=1, source_target_pairs={{0,4},{4,0},{1,5},{5,1},{2,6},{6,2},{3,7},{7,3},{8,12},{12,8},{9,1... | collective-permute-start | bytes 2654216 | tf_op jit(solution)/shard_map/ppermute | solution.py:959
  125.4 3.9 collective-permute-start.13
  132.4 46.2 %all-to-all-start = ((bf16[4,144,1536]{2,1,0:T(8,128)(2,1)}), bf16[4,144,1536]{2,1,0:T(8,128)(2,1)S(1)}, u32[]{:S(2)}, u32[]{:S(2)}) async-start(bf16[4,144,1536]{2,1,0:T(8,128)(2,1)} %add_convert_fusion.2), calls=%async_computation | async-start | bytes 3538944 | tf_op jit(solution)/shard_map/all_to_all | solution.py:962
  183.6 44.4 %all-to-all-start.1 = ((bf16[4,144,1536]{2,1,0:T(8,128)(2,1)}), bf16[4,144,1536]{2,1,0:T(8,128)(2,1)S(1)}, u32[]{:S(2)}, u32[]{:S(2)}) async-start(bf16[4,144,1536]{2,1,0:T(8,128)(2,1)} %get-tuple-element.113), calls=%async_computation.1 | async-start | bytes 3538944 | tf_op jit(solution)/shard_map/all_to_all | solution.py:962
  187.3 1.6 collective-permute-start.4
  228.0 3.7 collective-permute-start.14
  252.0 4.0 collective-permute-start.15
  259.1 45.3 %all-to-all-start.2 = ((bf16[4,144,1536]{2,1,0:T(8,128)(2,1)}), bf16[4,144,1536]{2,1,0:T(8,128)(2,1)S(1)}, u32[]{:S(2)}, u32[]{:S(2)}) async-start(bf16[4,144,1536]{2,1,0:T(8,128)(2,1)} %add_convert_fusion.1), calls=%async_computation.2 | async-start | bytes 3538944 | tf_op jit(solution)/shard_map/all_to_all | solution.py:962
  262.7 214.9 %reduce-scatter.3.cloned.1.call-start = ((), (), s32[]{:S(2)}) async-start(), calls=%async_computation.13 | async-start | bytes 21233664 | tf_op jit(solution)/shard_map/reduce_scatter | solution.py:1135
  283.0 30.0 %copy-start.4 = (bf16[1536,384]{1,0:T(8,128)(2,1)S(1)}, bf16[1536,384]{1,0:T(8,128)(2,1)}, u32[]{:S(2)}) copy-start(bf16[1536,384]{1,0:T(8,128)(2,1)} %convolution_convert_fusion.1.refs_9_) | copy-start | bytes 3538948
  314.2 44.9 %all-to-all-start.3 = ((bf16[4,144,1536]{2,1,0:T(8,128)(2,1)}), bf16[4,144,1536]{2,1,0:T(8,128)(2,1)S(1)}, u32[]{:S(2)}, u32[]{:S(2)}) async-start(bf16[4,144,1536]{2,1,0:T(8,128)(2,1)} %get-tuple-element.129), calls=%async_computation.3 | async-start | bytes 3538944 | tf_op jit(solution)/shard_map/all_to_all | solution.py:962
  328.8 4.6 collective-permute-start.16
  359.1 50.7 %all-to-all-start.4 = ((bf16[4,144,1536]{2,1,0:T(8,128)(2,1)}), bf16[4,144,1536]{2,1,0:T(8,128)(2,1)S(1)}, u32[]{:S(2)}, u32[]{:S(2)}) async-start(bf16[4,144,1536]{2,1,0:T(8,128)(2,1)} %add_convert_fusion), calls=%async_computation.4 | async-start | bytes 3538944 | tf_op jit(solution)/shard_map/all_to_all | solution.py:962
  362.7 3.8 collective-permute-start.17
  407.1 38.0 %collective-permute-start.19 = (bf16[1152,384]{1,0:T(8,128)(2,1)}, bf16[1152,384]{1,0:T(8,128)(2,1)}, u32[]{:S(2)}, u32[]{:S(2)}) collective-permute-start(bf16[1152,384]{1,0:T(8,128)(2,1)} %get-tuple-element.137.dep_ref), channel_id=1, source_target_pairs={{0,4},{4,0},{1,5},{5,1},{2,6},{6,2},{3,7},{7,3},{8,12},{12,8},{9,1... | collective-permute-start | bytes 2654216 | tf_op jit(solution)/shard_map/ppermute | solution.py:959
  415.8 46.6 %all-to-all-start.5 = ((bf16[4,144,1536]{2,1,0:T(8,128)(2,1)}), bf16[4,144,1536]{2,1,0:T(8,128)(2,1)S(1)}, u32[]{:S(2)}, u32[]{:S(2)}) async-start(bf16[4,144,1536]{2,1,0:T(8,128)(2,1)} %get-tuple-element.141), calls=%async_computation.5 | async-start | bytes 3538944 | tf_op jit(solution)/shard_map/all_to_all | solution.py:962
  421.0 150.5 %reduce-scatter.5.cloned.1.call-start = ((), (), s32[]{:S(2)}) async-start(), calls=%async_computation.14 | async-start | bytes 10616832 | tf_op jit(solution)/shard_map/reduce_scatter | solution.py:1135
  453.9 6.7 %collective-permute-start.20 = (bf16[4,144,1536]{2,1,0:T(8,128)(2,1)}, bf16[4,144,1536]{2,1,0:T(8,128)(2,1)}, u32[]{:S(2)}, u32[]{:S(2)}) collective-permute-start(bf16[4,144,1536]{2,1,0:T(8,128)(2,1)} %get-tuple-element.155), channel_id=1, source_target_pairs={{0,8},{8,0},{16,24},{24,16},{1,9},{9,1},{17,25},{25,17},{2,10},{10... | collective-permute-start | bytes 5308424 | tf_op jit(solution)/shard_map/ppermute | solution.py:959
  473.5 53.9 %all-to-all-start.6 = ((bf16[4,144,1536]{2,1,0:T(8,128)(2,1)}), bf16[4,144,1536]{2,1,0:T(8,128)(2,1)S(1)}, u32[]{:S(2)}, u32[]{:S(2)}) async-start(bf16[4,144,1536]{2,1,0:T(8,128)(2,1)} %fold_after.1), calls=%async_computation.6 | async-start | bytes 3538944 | tf_op jit(solution)/shard_map/all_to_all | solution.py:962
  477.6 39.0 %collective-permute-start.18 = (bf16[4,144,1536]{2,1,0:T(8,128)(2,1)S(1)}, bf16[4,144,1536]{2,1,0:T(8,128)(2,1)}, u32[]{:S(2)}, u32[]{:S(2)}) collective-permute-start(bf16[4,144,1536]{2,1,0:T(8,128)(2,1)S(1)} %copy-done.2), channel_id=1, source_target_pairs={{0,8},{8,0},{16,24},{24,16},{1,9},{9,1},{17,25},{25,17},{2,10},{10... | collective-permute-start | bytes 5308424 | tf_op jit(solution)/shard_map/ppermute | solution.py:959
  483.9 1.9 collective-permute-start.21
  486.9 6.2 collective-permute-start.22
  493.8 5.6 collective-permute-start.23
  501.1 8.4 %collective-permute-start.24 = (f32[24,1536]{1,0:T(8,128)}, f32[24,1536]{1,0:T(8,128)}, u32[]{:S(2)}, u32[]{:S(2)}) collective-permute-start(f32[24,1536]{1,0:T(8,128)} %add.213), channel_id=1, source_target_pairs={{0,1},{1,0},{2,3},{3,2},{4,5},{5,4},{6,7},{7,6},{8,9},{9,8},{10,11... | collective-permute-start | bytes 442376 | tf_op jit(solution)/shard_map/ppermute | solution.py:959
  510.5 14.6 %collective-permute-start.25 = (f32[24,1536]{1,0:T(8,128)S(1)}, f32[24,1536]{1,0:T(8,128)S(1)}, u32[]{:S(2)}, u32[]{:S(2)}) collective-permute-start(f32[24,1536]{1,0:T(8,128)S(1)} %add.214), channel_id=1, source_target_pairs={{0,2},{1,3},{2,0},{3,1},{4,6},{5,7},{6,4},{7,5},{8,10},{9,11},{10,... | collective-permute-start | bytes 442376 | tf_op jit(solution)/shard_map/ppermute | solution.py:959
  525.7 10.7 %collective-permute-start.26 = (f32[24,1536]{1,0:T(8,128)}, f32[24,1536]{1,0:T(8,128)}, u32[]{:S(2)}, u32[]{:S(2)}) collective-permute-start(f32[24,1536]{1,0:T(8,128)} %add.215), channel_id=1, source_target_pairs={{0,8},{8,0},{16,24},{24,16},{1,9},{9,1},{17,25},{25,17},{2,10},{10... | collective-permute-start | bytes 442376 | tf_op jit(solution)/shard_map/ppermute | solution.py:959
  532.6 50.6 %all-to-all-start.7 = ((bf16[4,144,1536]{2,1,0:T(8,128)(2,1)}), bf16[4,144,1536]{2,1,0:T(8,128)(2,1)S(1)}, u32[]{:S(2)}, u32[]{:S(2)}) async-start(bf16[4,144,1536]{2,1,0:T(8,128)(2,1)} %after_back.1), calls=%async_computation.7 | async-start | bytes 3538944 | tf_op jit(solution)/shard_map/all_to_all | solution.py:962
  582.5 4.7 collective-permute-start.28
  587.2 27.0 %collective-permute-start.27 = (bf16[4,144,1536]{2,1,0:T(8,128)(2,1)}, bf16[4,144,1536]{2,1,0:T(8,128)(2,1)}, u32[]{:S(2)}, u32[]{:S(2)}) collective-permute-start(bf16[4,144,1536]{2,1,0:T(8,128)(2,1)} %copy_after.1), channel_id=1, source_target_pairs={{0,8},{8,0},{16,24},{24,16},{1,9},{9,1},{17,25},{25,17},{2,10},{10... | collective-permute-start | bytes 5308424 | tf_op jit(solution)/shard_map/ppermute | solution.py:959
  587.2 3.8 collective-permute-start.29
  591.0 3.7 collective-permute-start.30
  594.8 3.7 collective-permute-start.31
  598.5 6.4 %collective-permute-start.32 = (f32[3080]{0:T(1024)S(1)}, f32[3080]{0:T(1024)S(1)}, u32[]{:S(2)}, u32[]{:S(2)}) collective-permute-start(f32[3080]{0:T(1024)S(1)} %add.222), channel_id=1, source_target_pairs={{0,2},{1,3},{2,0},{3,1},{4,6},{5,7},{6,4},{7,5},{8,10},{9,11},{10,... | collective-permute-start | bytes 36968 | tf_op jit(solution)/shard_map/ppermute | solution.py:959
  (38 other events, 204.5 us)
Sparse Core Ops, SparseCore 0:
  10.5 53.1 all-gather.3
  65.6 36.6 all-gather.5
  104.8 98.7 all-gather.7
  314.3 141.2 reduce-scatter.2
  473.0 76.8 reduce-scatter.4

commit v5 on v4

--- a/solution.py
+++ b/solution.py
@@ -745,17 +745,16 @@
         s_img = dotf(qm, kv_ref[:img, :256], NT)
         s_txt = jnp.where(keep, dotf(qm, kv_ref[img:, :256], NT), -1e30)
         m = jnp.maximum(jnp.max(s_img, axis=1, keepdims=True), jnp.max(s_txt, axis=1, keepdims=True))
-        if last:
-            m_old = stat[:, h : h + 1]
-            m = jnp.maximum(m, m_old)
         e_img, e_txt = jnp.exp(s_img - m), jnp.exp(s_txt - m)
         l = jnp.sum(e_img, axis=1, keepdims=True) + jnp.sum(e_txt, axis=1, keepdims=True)
         pv = dotf(e_img.astype(bf), kv_ref[:img, 128:384], NN) + dotf(e_txt.astype(bf), kv_ref[img:, 128:384], NN)
         if last:
-            scale = jnp.exp(m_old - m)
-            l = l + stat[:, heads + h : heads + h + 1] * scale
-            pv = (pv + before * scale) / l
-            tile = jnp.where(lane1 == h, m + jnp.log(l), tile)
+            m_old = stat[:, h : h + 1]
+            m_all = jnp.maximum(m, m_old)
+            scale, scale_old = jnp.exp(m - m_all), jnp.exp(m_old - m_all)
+            l = l * scale + stat[:, heads + h : heads + h + 1] * scale_old
+            pv = pv * (scale / l) + before * (scale_old / l)
+            tile = jnp.where(lane1 == h, m_all + jnp.log(l), tile)
         else:
             tile = jnp.where(lane1 == h, m, jnp.where(lane1 == heads + h, l, tile))
         acc = jnp.where((lane >> 6) == h + 1, pv, acc)

time: 633 us -> 634 us (level)
  transfers between devices with their start and end apart: 46 -> 46, of which waited for: 30 -> 30; matrix products, arithmetic and copies ran while one was open for 18% -> 18% of each run, Pallas kernels for 30% -> 31%
where the time goes in v5:
time: 634 us; the launch traced here: 627 us
  Pallas kernels  222 us (35%)
  waiting for transfers between devices  190 us (30%)
  starting transfers between devices  62.9 us (10%)
  other arithmetic  47.9 us (8%)
  local copies, waits for them, and re-layouts  46.1 us (7%)
  matrix products  40.3 us (6%)
  between operations  17.3 us (3%)
    all_to_all x8, waiting for transfers between devices, swap(): return lax.all_to_all(x, axis, 0, 0, tiled=True)  91.2 us
    ppermute x30, waiting for transfers between devices, pp(): return lax.ppermute(x, axis, [(i, i ^ xor) for i in range(sizes[axis])])  67.8 us
    pallas_call x3, Pallas kernels, seg_call(): pl.pallas_call(kernel, grid_spec=pltpu.PrefetchScalarGridSpec(num_scalar_...  40.3 us
    dot_general x14, matrix products, dotf(): lax.dot_general(a, b, dims, preferred_element_type=f32, precision=precision)  34.3 us
    pallas_call x2, Pallas kernels, attn_bwd_half(): pl.pallas_call(functools.partial(attn_bwd_kernel, heads), grid=(T // bk,)...  33.9 us
    all_to_all x8, starting transfers between devices, swap(): return lax.all_to_all(x, axis, 0, 0, tiled=True)  32.2 us
    all_gather x3, waiting for transfers between devices, gather(): return lax.all_gather(w, everyone, axis=1, tiled=True)  26.5 us
    pallas_call x2, Pallas kernels, attn_half(): pl.pallas_call(functools.partial(attn_fwd_kernel, heads, img, live, last)...  26.2 us
  transfers between devices with their start and end apart: 46, of which 30 were waited for; matrix products, arithmetic and copies ran while one was open for 18% of the time, Pallas kernels for 31%

profile of v5, /device:TPU:0, one launch (start us, length us, event | category | flops | bytes accessed | tf_op | source)
XLA Modules:
  0.0 627.2 jit_solution(10703248760409021994)
XLA Ops:
  13.6 5.0 mod_partial.1
  29.8 3.7 collective-permute-start.11
  44.0 4.0 select_bitcast_fusion.xi_ref.refs_1_
  50.1 13.6 %all-gather.4.cloned.1.call-done.w_ref = bf16[6,1536,384]{2,1,0:T(8,128)(2,1)} async-done(((bf16[6,192,384]{2,1,0:T(8,128)(2,1)}), bf16[6,1536,384]{2,1,0:T(8,128)(2,1)}) %all-gather.4.cloned.1.call-update) | async-done | bytes 7077904 | tf_op jit(solution)/shard_map/all_gather | solution.py:1023
  63.7 11.1 %qkv.1 = (bf16[1024,1536]{1,0:T(8,128)(2,1)}, bf16[128,1536]{1,0:T(8,128)(2,1)}, bf16[1024,1536]{1,0:T(8,128)(2,1)}, bf16[128,1536]{1,0:T(8,128)(2,1)}, bf16[115...) custom-call(s32[1]{0:T(128)} %bitcast.core_ref, bf16[1024,1536]{1,0:T(8,128)(2,1)} %select_bitcast_fusion.xi_ref.refs_1_, ...), custom_call_target="tpu_custom_call" | custom-call | flops 1024 | bytes 1024 | tf_op jit(solution)/shard_map/qkv/pallas_call | solution.py:182
  76.0 4.8 bitcast_convert_fusion
  84.8 10.2 %attn_first.1 = (f32[1152,256]{1,0:T(8,128)}, f32[1152,128]{1,0:T(8,128)}) custom-call(bf16[1152,256]{1,0:T(8,128)(2,1)} %get-tuple-element.99.q_ref, bf16[1152,384]{1,0:T(8,128)(2,1)} %get-tuple-element.100.kv_ref), custom_call_target="tpu_custom_call" | custom-call | flops 1024 | bytes 1024 | tf_op jit(solution)/shard_map/attn_first/pallas_call | solution.py:779
  95.1 9.3 %collective-permute-done.12.kv_ref = bf16[1152,384]{1,0:T(8,128)(2,1)S(1)} collective-permute-done((bf16[1152,384]{1,0:T(8,128)(2,1)}, bf16[1152,384]{1,0:T(8,128)(2,1)S(1)}, u32[]{:S(2)}, u32[]{:S(2)}) %collective-permute-start.12) | collective-permute-done | bytes 884768 | tf_op jit(solution)/shard_map/ppermute | solution.py:958
  105.3 15.9 %attn_last.1 = (bf16[1152,192]{1,0:T(8,128)(2,1)}, f32[8,1152]{1,0:T(8,128)}) custom-call(bf16[1152,256]{1,0:T(8,128)(2,1)} %get-tuple-element.99.q_ref, bf16[1152,384]{1,0:T(8,128)(2,1)} %copy-done.15, f32[1152,256]{1,0:T(8,128)} %get-tuple-element.101.refs_0_, f32[1152,128]{1,0:T(8,128)} %get-tuple-element.102.refs_1_), custom_call_target="tpu_custom_call" | custom-call | flops 1024 | bytes 1024 | tf_op jit(solution)/shard_map/attn_last/pallas_call | solution.py:779
  121.2 4.8 oproj.1
  126.0 3.9 collective-permute-done.13
  133.0 4.8 all-to-all-start
  138.6 9.6 %zeros.1 = (bf16[24576,384]{1,0:T(8,128)(2,1)}, bf16[12288,384]{1,0:T(8,128)(2,1)}) custom-call(s32[1]{0:T(128)} %bitcast.core_ref), custom_call_target="tpu_custom_call" | custom-call | flops 1024 | bytes 1024 | tf_op jit(solution)/shard_map/zeros/pallas_call | solution.py:408
  148.2 31.1 %all-to-all-done.refs_5_ = bf16[4,144,1536]{2,1,0:T(8,128)(2,1)S(1)} async-done(((bf16[4,144,1536]{2,1,0:T(8,128)(2,1)}), bf16[4,144,1536]{2,1,0:T(8,128)(2,1)S(1)}, u32[]{:S(2)}, u32[]{:S(2)}) %all-to-all-start) | async-done | bytes 1769504 | tf_op jit(solution)/shard_map/all_to_all | solution.py:961
  180.5 3.7 after_attn.1
  184.2 3.7 all-to-all-start.1
  190.6 12.9 %all-gather.8.cloned.1.call-done.w_ref = bf16[16,1536,384]{2,1,0:T(8,128)(2,1)} async-done(((bf16[16,192,384]{2,1,0:T(8,128)(2,1)}), bf16[16,1536,384]{2,1,0:T(8,128)(2,1)}) %all-gather.8.cloned.1.call-update) | async-done | bytes 18874384 | tf_op jit(solution)/shard_map/all_gather | solution.py:1023
  203.6 10.6 %grad_gate.1 = (bf16[1024,1536]{1,0:T(8,128)(2,1)}, bf16[128,1536]{1,0:T(8,128)(2,1)}, f32[2,1024,384]{2,1,0:T(8,128)}, f32[2,128,384]{2,1,0:T(8,128)}) custom-call(s32[1]{0:T(128)} %bitcast.core_ref, bf16[1024,1536]{1,0:T(8,128)(2,1)} %multiply_bitcast_fusion.ci_ref.refs_3_, bf16[128,1536]{1,0:T(8,128)(2,1)} %pad.13.ct_ref.refs_4_, ...), custom_call_target="tpu_custom_call" | custom-call | flops 1024 | bytes 1024 | tf_op jit(solution)/shard_map/grad_gate/pallas_call | solution.py:384
  214.2 14.4 %all-to-all-done.1.mine = bf16[4,144,1536]{2,1,0:T(8,128)(2,1)S(1)} async-done(((bf16[4,144,1536]{2,1,0:T(8,128)(2,1)}), bf16[4,144,1536]{2,1,0:T(8,128)(2,1)S(1)}, u32[]{:S(2)}, u32[]{:S(2)}) %all-to-all-start.1) | async-done | bytes 1769504 | tf_op jit(solution)/shard_map/all_to_all | solution.py:961
  233.5 19.1 %mlp.1 = (bf16[1024,1536]{1,0:T(8,128)(2,1)}, bf16[128,1536]{1,0:T(8,128)(2,1)}, bf16[2,1024,384]{2,1,0:T(8,128)(2,1)}, bf16[2,128,384]{2,1,0:T(8,128)(2,1)}, bf...) custom-call(s32[1]{0:T(128)} %bitcast.core_ref, ...), custom_call_target="tpu_custom_call" | custom-call | flops 1024 | bytes 1024 | tf_op jit(solution)/shard_map/mlp/pallas_call | solution.py:384
  252.8 3.8 collective-permute-done.15
  265.2 5.1 fusion.1
  283.6 21.5 %all-to-all-done.2.refs_7_ = bf16[4,144,1536]{2,1,0:T(8,128)(2,1)S(1)} async-done(((bf16[4,144,1536]{2,1,0:T(8,128)(2,1)}), bf16[4,144,1536]{2,1,0:T(8,128)(2,1)S(1)}, u32[]{:S(2)}, u32[]{:S(2)}) %all-to-all-start.2) | async-done | bytes 1769504 | tf_op jit(solution)/shard_map/all_to_all | solution.py:961
  306.3 4.8 after_mlp.1
  314.8 4.0 all-to-all-start.3
  318.8 10.7 %down.1 = (bf16[4,144,1536]{2,1,0:T(8,128)(2,1)}, bf16[4,144,1536]{2,1,0:T(8,128)(2,1)}) custom-call(s32[1]{0:T(128)} %bitcast.core_ref, bf16[2,1024,384]{2,1,0:T(8,128)(2,1)} %get-tuple-element.130.gi, bf16[2,128,384]{2,1,0:T(8,128)(2,1)} %get-tuple-element.131.gt, bf16[16,1536,384]{2,1,0:T(8,128)(2,1)} %all-gather.8.cloned.1.call-done.w_ref), custom_call_target="tpu_custom_call" | custom-call | flops 1024 | bytes 1024 | tf_op jit(solution)/shard_map/down/pallas_call | solution.py:384
  329.4 4.6 collective-permute-done.16
  337.2 22.5 %all-to-all-done.3.mine = bf16[4,144,1536]{2,1,0:T(8,128)(2,1)S(1)} async-done(((bf16[4,144,1536]{2,1,0:T(8,128)(2,1)}), bf16[4,144,1536]{2,1,0:T(8,128)(2,1)S(1)}, u32[]{:S(2)}, u32[]{:S(2)}) %all-to-all-start.3) | async-done | bytes 1769504 | tf_op jit(solution)/shard_map/all_to_all | solution.py:961
  363.4 3.7 collective-permute-done.17.other
  368.3 5.5 grad_attn.1
  373.8 16.7 %attn_bwd.2 = (f32[1152,192]{1,0:T(8,128)}, bf16[1152,384]{1,0:T(8,128)(2,1)}) custom-call(bf16[1152,256]{1,0:T(8,128)(2,1)} %get-tuple-element.99.q_ref, bf16[1152,384]{1,0:T(8,128)(2,1)} %copy-done.15, bf16[1152,192]{1,0:T(8,128)(2,1)} %get-tuple-element.103.a_ref, bf16[1152,192]{1,0:T(8,128)(2,1)} %get-tuple-element.136.da_ref.dep_ref, ...), custom_call_target="tpu_custom_call" | custom-call | flops 1024 | bytes 1024 | tf_op jit(solution)/shard_map/attn_bwd/pallas_call | solution.py:831
  390.5 17.2 %attn_bwd.3 = (f32[1152,192]{1,0:T(8,128)}, bf16[1152,384]{1,0:T(8,128)(2,1)}) custom-call(bf16[1152,256]{1,0:T(8,128)(2,1)} %get-tuple-element.99.q_ref, bf16[1152,384]{1,0:T(8,128)(2,1)} %get-tuple-element.100.kv_ref, bf16[1152,192]{1,0:T(8,128)(2,1)} %get-tuple-element.103.a_ref, bf16[1152,192]{1,0:T(8,128)(2,1)} %get-tuple-element.136.da_ref.dep_ref, ...), custom_call_target="tpu_custom_call" | custom-call | flops 1024 | bytes 1024 | tf_op jit(solution)/shard_map/attn_bwd/pallas_call | solution.py:831
  411.6 4.9 after_down.1
  416.5 5.1 all-to-all-start.5
  432.7 13.0 %collective-permute-done.19.b_ref = bf16[1152,384]{1,0:T(8,128)(2,1)} collective-permute-done((bf16[1152,384]{1,0:T(8,128)(2,1)}, bf16[1152,384]{1,0:T(8,128)(2,1)}, u32[]{:S(2)}, u32[]{:S(2)}) %collective-permute-start.19) | collective-permute-done | bytes 884768 | tf_op jit(solution)/shard_map/ppermute | solution.py:958
  445.7 8.8 %grad_in.1 = (bf16[4,144,1536]{2,1,0:T(8,128)(2,1)}, bf16[4,144,1536]{2,1,0:T(8,128)(2,1)}, bf16[1024,384]{1,0:T(8,128)(2,1)}, bf16[128,384]{1,0:T(8,128)(2,1)}, f32[8,384]{1,0:T(8,128)}, /*index=5*/f32[8,1536]{1,0:T(8,128)}) custom-call(s32[1]{0:T(128)} %bitcast.core_ref, f32[16,1536]{1,0:T(8,128)} %get-tuple-element.145.dep_ref.low_ref, ...), custom_call_target="tpu_custom_call" | custom-call | flops 1024 | bytes 1024 | tf_op jit(solution)/shard_map/grad_in/pallas_call | solution.py:619
  454.6 5.1 fusion.9
  464.2 4.1 fold_after.1
  489.2 4.5 collective-permute-done.22
  511.1 4.7 collective-permute-start.25
  517.3 4.0 join_tokens.2
  521.3 4.4 collective-permute-done.25
  529.2 4.0 after_back.1
  533.2 3.8 all-to-all-start.7
  538.7 19.4 %adam.1 = (f32[2,18,192,384]{3,2,1,0:T(8,128)}, f32[2,18,192,384]{3,2,1,0:T(8,128)}, f32[2,18,192,384]{3,2,1,0:T(8,128)}, f32[2,18,192,384]{3,2,1,0:T(8,128)}) custom-call(f32[2,8]{1,0:T(2,128)} %min.22.f_ref, bf16[2,8,192,384]{3,2,1,0:T(8,128)(2,1)} %bitcast.181, f32[2,18,192,384]{3,2,1,0:T(8,128)} %bitcast.164, f32[2,18,192,384]{3,2,1,0:T(8,128)} %bitcast.168, ...), custom_call_target="tpu_custom_call" | custom-call | flops 1024 | bytes 1024 | tf_op jit(solution)/shard_map/adam/pallas_call | solution.py:856
  560.6 11.5 %adam_mod.1 = (f32[2,18,192,384]{3,2,1,0:T(8,128)}, f32[2,18,192,384]{3,2,1,0:T(8,128)}, f32[2,18,192,384]{3,2,1,0:T(8,128)}, f32[2,18,192,384]{3,2,1,0:T(8,128)}) custom-call(f32[192,2]{1,0:T(8,128)} %get-tuple-element.236.sc_ref, ...), custom_call_target="tpu_custom_call", output_to_operand_aliasing={{0}: (6, {}), {1}: (7, {}), {2}: (8, {}), {3}: (9, {})} | custom-call | flops 1024 | bytes 1024 | tf_op jit(solution)/shard_map/adam_mod/pallas_call | solution.py:929
  606.1 7.2 %adam_one.1 = (f32[2,18,192,384]{3,2,1,0:T(8,128)}, f32[2,18,192,384]{3,2,1,0:T(8,128)}, f32[2,18,192,384]{3,2,1,0:T(8,128)}, f32[2,18,192,384]{3,2,1,0:T(8,128)}) custom-call(f32[2,4]{1,0:T(2,128)} %min.24.f_ref, ...), custom_call_target="tpu_custom_call", output_to_operand_aliasing={{0}: (5, {}), {1}: (6, {}), {2}: (7, {}), {3}: (8, {})} | custom-call | flops 1024 | bytes 1024 | tf_op jit(solution)/shard_map/adam_one/pallas_call | solution.py:898
  614.7 4.0 join_tokens.3
  (274 shorter events, 185.1 us)
Async XLA Ops:
  7.2 56.5 %all-gather.4.cloned.1.call-start = ((), (), s32[]{:S(2)}) async-start(), calls=%async_computation.10 | async-start | bytes 7962624 | tf_op jit(solution)/shard_map/all_gather | solution.py:1023
  10.2 111.1 %all-gather.6.cloned.1.call-start = ((), (), s32[]{:S(2)}) async-start(), calls=%async_computation.11 | async-start | bytes 2654208 | tf_op jit(solution)/shard_map/all_gather | solution.py:1023
  10.2 33.8 %collective-permute-start = (bf16[1,1024,1536]{2,1,0:T(8,128)(2,1)}, bf16[1,1024,1536]{2,1,0:T(8,128)(2,1)}, u32[]{:S(2)}, u32[]{:S(2)}) collective-permute-start(bf16[1,1024,1536]{2,1,0:T(8,128)(2,1)} %param.12), channel_id=1, source_target_pairs={{0,8},{8,0},{16,24},{24,16},{1,9},{9,1},{17,25},{25,17},{2,10},{10... | collective-permute-start | bytes 9437192 | tf_op jit(solution)/shard_map/ppermute | solution.py:958
  13.6 25.3 %copy-start.26 = (f32[2,14,1536]{2,0,1:T(2,128)S(1)}, f32[2,14,1536]{2,0,1:T(2,128)}, u32[]{:S(2)}) copy-start(f32[2,14,1536]{2,0,1:T(2,128)} %param.19) | copy-start | bytes 516100
  18.7 1.4 collective-permute-start.5
  20.9 6.5 %collective-permute-start.8 = (f32[2,6,2,384]{3,2,1,0:T(2,128)S(1)}, f32[2,6,2,384]{3,2,1,0:T(2,128)S(1)}, u32[]{:S(2)}, u32[]{:S(2)}) collective-permute-start(f32[2,6,2,384]{3,2,1,0:T(2,128)S(1)} %add.189), channel_id=1, source_target_pairs={{0,20},{4,16},{8,28},{12,24},{16,4},{20,0},{24,12},{28,8},{1,21},{... | collective-permute-start | bytes 110600 | tf_op jit(solution)/shard_map/ppermute | solution.py:1047
  24.6 5.0 collective-permute-start.7
  25.1 4.7 collective-permute-start.6
  29.8 6.6 %collective-permute-start.11 = (f32[2,6,2,384]{3,2,1,0:T(2,128)S(1)}, f32[2,6,2,384]{3,2,1,0:T(2,128)S(1)}, u32[]{:S(2)}, u32[]{:S(2)}) collective-permute-start(f32[2,6,2,384]{3,2,1,0:T(2,128)S(1)} %add_add_fusion), channel_id=1, source_target_pairs={{0,3},{1,2},{2,1},{3,0},{4,7},{5,6},{6,5},{7,4},{8,11},{9,10},{10,... | collective-permute-start | bytes 110600 | tf_op jit(solution)/shard_map/ppermute | solution.py:958
  33.6 4.9 collective-permute-start.10
  33.6 4.9 collective-permute-start.9
  34.3 1.2 collective-permute-start.3
  35.5 12.5 %collective-permute-start.2 = (bf16[1,1024,1536]{2,1,0:T(8,128)(2,1)}, bf16[1,1024,1536]{2,1,0:T(8,128)(2,1)S(1)}, u32[]{:S(2)}, u32[]{:S(2)}) collective-permute-start(bf16[1,1024,1536]{2,1,0:T(8,128)(2,1)} %param.22), channel_id=1, source_target_pairs={{0,8},{8,0},{16,24},{24,16},{1,9},{9,1},{17,25},{25,17},{2,10},{10... | collective-permute-start | bytes 9437192 | tf_op jit(solution)/shard_map/ppermute | solution.py:958
  39.8 163.8 %all-gather.8.cloned.1.call-start = ((), (), s32[]{:S(2)}) async-start(), calls=%async_computation.12 | async-start | bytes 21233664 | tf_op jit(solution)/shard_map/all_gather | solution.py:1023
  39.8 2.4 collective-permute-start.1
  74.8 29.6 %collective-permute-start.12 = (bf16[1152,384]{1,0:T(8,128)(2,1)}, bf16[1152,384]{1,0:T(8,128)(2,1)S(1)}, u32[]{:S(2)}, u32[]{:S(2)}) collective-permute-start(bf16[1152,384]{1,0:T(8,128)(2,1)} %get-tuple-element.100.kv_ref), channel_id=1, source_target_pairs={{0,4},{4,0},{1,5},{5,1},{2,6},{6,2},{3,7},{7,3},{8,12},{12,8},{9,1... | collective-permute-start | bytes 2654216 | tf_op jit(solution)/shard_map/ppermute | solution.py:958
  126.0 3.9 collective-permute-start.13
  133.0 46.2 %all-to-all-start = ((bf16[4,144,1536]{2,1,0:T(8,128)(2,1)}), bf16[4,144,1536]{2,1,0:T(8,128)(2,1)S(1)}, u32[]{:S(2)}, u32[]{:S(2)}) async-start(bf16[4,144,1536]{2,1,0:T(8,128)(2,1)} %add_convert_fusion.2), calls=%async_computation | async-start | bytes 3538944 | tf_op jit(solution)/shard_map/all_to_all | solution.py:961
  184.2 44.4 %all-to-all-start.1 = ((bf16[4,144,1536]{2,1,0:T(8,128)(2,1)}), bf16[4,144,1536]{2,1,0:T(8,128)(2,1)S(1)}, u32[]{:S(2)}, u32[]{:S(2)}) async-start(bf16[4,144,1536]{2,1,0:T(8,128)(2,1)} %get-tuple-element.113), calls=%async_computation.1 | async-start | bytes 3538944 | tf_op jit(solution)/shard_map/all_to_all | solution.py:961
  187.9 1.9 collective-permute-start.4
  228.6 3.7 collective-permute-start.14
  252.6 4.0 collective-permute-start.15
  259.7 45.3 %all-to-all-start.2 = ((bf16[4,144,1536]{2,1,0:T(8,128)(2,1)}), bf16[4,144,1536]{2,1,0:T(8,128)(2,1)S(1)}, u32[]{:S(2)}, u32[]{:S(2)}) async-start(bf16[4,144,1536]{2,1,0:T(8,128)(2,1)} %add_convert_fusion.1), calls=%async_computation.2 | async-start | bytes 3538944 | tf_op jit(solution)/shard_map/all_to_all | solution.py:961
  263.3 214.9 %reduce-scatter.3.cloned.1.call-start = ((), (), s32[]{:S(2)}) async-start(), calls=%async_computation.13 | async-start | bytes 21233664 | tf_op jit(solution)/shard_map/reduce_scatter | solution.py:1134
  283.6 30.0 %copy-start.4 = (bf16[1536,384]{1,0:T(8,128)(2,1)S(1)}, bf16[1536,384]{1,0:T(8,128)(2,1)}, u32[]{:S(2)}) copy-start(bf16[1536,384]{1,0:T(8,128)(2,1)} %convolution_convert_fusion.1.refs_9_) | copy-start | bytes 3538948
  314.8 44.9 %all-to-all-start.3 = ((bf16[4,144,1536]{2,1,0:T(8,128)(2,1)}), bf16[4,144,1536]{2,1,0:T(8,128)(2,1)S(1)}, u32[]{:S(2)}, u32[]{:S(2)}) async-start(bf16[4,144,1536]{2,1,0:T(8,128)(2,1)} %get-tuple-element.129), calls=%async_computation.3 | async-start | bytes 3538944 | tf_op jit(solution)/shard_map/all_to_all | solution.py:961
  329.4 4.6 collective-permute-start.16
  359.7 50.7 %all-to-all-start.4 = ((bf16[4,144,1536]{2,1,0:T(8,128)(2,1)}), bf16[4,144,1536]{2,1,0:T(8,128)(2,1)S(1)}, u32[]{:S(2)}, u32[]{:S(2)}) async-start(bf16[4,144,1536]{2,1,0:T(8,128)(2,1)} %add_convert_fusion), calls=%async_computation.4 | async-start | bytes 3538944 | tf_op jit(solution)/shard_map/all_to_all | solution.py:961
  363.3 3.8 collective-permute-start.17
  407.7 38.0 %collective-permute-start.19 = (bf16[1152,384]{1,0:T(8,128)(2,1)}, bf16[1152,384]{1,0:T(8,128)(2,1)}, u32[]{:S(2)}, u32[]{:S(2)}) collective-permute-start(bf16[1152,384]{1,0:T(8,128)(2,1)} %get-tuple-element.137.dep_ref), channel_id=1, source_target_pairs={{0,4},{4,0},{1,5},{5,1},{2,6},{6,2},{3,7},{7,3},{8,12},{12,8},{9,1... | collective-permute-start | bytes 2654216 | tf_op jit(solution)/shard_map/ppermute | solution.py:958
  416.5 46.5 %all-to-all-start.5 = ((bf16[4,144,1536]{2,1,0:T(8,128)(2,1)}), bf16[4,144,1536]{2,1,0:T(8,128)(2,1)S(1)}, u32[]{:S(2)}, u32[]{:S(2)}) async-start(bf16[4,144,1536]{2,1,0:T(8,128)(2,1)} %get-tuple-element.141), calls=%async_computation.5 | async-start | bytes 3538944 | tf_op jit(solution)/shard_map/all_to_all | solution.py:961
  421.6 150.5 %reduce-scatter.5.cloned.1.call-start = ((), (), s32[]{:S(2)}) async-start(), calls=%async_computation.14 | async-start | bytes 10616832 | tf_op jit(solution)/shard_map/reduce_scatter | solution.py:1134
  454.5 6.7 %collective-permute-start.20 = (bf16[4,144,1536]{2,1,0:T(8,128)(2,1)}, bf16[4,144,1536]{2,1,0:T(8,128)(2,1)}, u32[]{:S(2)}, u32[]{:S(2)}) collective-permute-start(bf16[4,144,1536]{2,1,0:T(8,128)(2,1)} %get-tuple-element.155), channel_id=1, source_target_pairs={{0,8},{8,0},{16,24},{24,16},{1,9},{9,1},{17,25},{25,17},{2,10},{10... | collective-permute-start | bytes 5308424 | tf_op jit(solution)/shard_map/ppermute | solution.py:958
  474.1 53.8 %all-to-all-start.6 = ((bf16[4,144,1536]{2,1,0:T(8,128)(2,1)}), bf16[4,144,1536]{2,1,0:T(8,128)(2,1)S(1)}, u32[]{:S(2)}, u32[]{:S(2)}) async-start(bf16[4,144,1536]{2,1,0:T(8,128)(2,1)} %fold_after.1), calls=%async_computation.6 | async-start | bytes 3538944 | tf_op jit(solution)/shard_map/all_to_all | solution.py:961
  478.3 39.0 %collective-permute-start.18 = (bf16[4,144,1536]{2,1,0:T(8,128)(2,1)S(1)}, bf16[4,144,1536]{2,1,0:T(8,128)(2,1)}, u32[]{:S(2)}, u32[]{:S(2)}) collective-permute-start(bf16[4,144,1536]{2,1,0:T(8,128)(2,1)S(1)} %copy-done.2), channel_id=1, source_target_pairs={{0,8},{8,0},{16,24},{24,16},{1,9},{9,1},{17,25},{25,17},{2,10},{10... | collective-permute-start | bytes 5308424 | tf_op jit(solution)/shard_map/ppermute | solution.py:958
  484.6 1.9 collective-permute-start.21
  487.5 6.1 collective-permute-start.22
  494.3 5.7 collective-permute-start.23
  501.7 8.4 %collective-permute-start.24 = (f32[24,1536]{1,0:T(8,128)}, f32[24,1536]{1,0:T(8,128)}, u32[]{:S(2)}, u32[]{:S(2)}) collective-permute-start(f32[24,1536]{1,0:T(8,128)} %add.213), channel_id=1, source_target_pairs={{0,1},{1,0},{2,3},{3,2},{4,5},{5,4},{6,7},{7,6},{8,9},{9,8},{10,11... | collective-permute-start | bytes 442376 | tf_op jit(solution)/shard_map/ppermute | solution.py:958
  511.1 14.6 %collective-permute-start.25 = (f32[24,1536]{1,0:T(8,128)S(1)}, f32[24,1536]{1,0:T(8,128)S(1)}, u32[]{:S(2)}, u32[]{:S(2)}) collective-permute-start(f32[24,1536]{1,0:T(8,128)S(1)} %add.214), channel_id=1, source_target_pairs={{0,2},{1,3},{2,0},{3,1},{4,6},{5,7},{6,4},{7,5},{8,10},{9,11},{10,... | collective-permute-start | bytes 442376 | tf_op jit(solution)/shard_map/ppermute | solution.py:958
  526.3 10.7 %collective-permute-start.26 = (f32[24,1536]{1,0:T(8,128)}, f32[24,1536]{1,0:T(8,128)}, u32[]{:S(2)}, u32[]{:S(2)}) collective-permute-start(f32[24,1536]{1,0:T(8,128)} %add.215), channel_id=1, source_target_pairs={{0,8},{8,0},{16,24},{24,16},{1,9},{9,1},{17,25},{25,17},{2,10},{10... | collective-permute-start | bytes 442376 | tf_op jit(solution)/shard_map/ppermute | solution.py:958
  533.2 50.6 %all-to-all-start.7 = ((bf16[4,144,1536]{2,1,0:T(8,128)(2,1)}), bf16[4,144,1536]{2,1,0:T(8,128)(2,1)S(1)}, u32[]{:S(2)}, u32[]{:S(2)}) async-start(bf16[4,144,1536]{2,1,0:T(8,128)(2,1)} %after_back.1), calls=%async_computation.7 | async-start | bytes 3538944 | tf_op jit(solution)/shard_map/all_to_all | solution.py:961
  583.1 4.7 collective-permute-start.28
  587.7 27.0 %collective-permute-start.27 = (bf16[4,144,1536]{2,1,0:T(8,128)(2,1)}, bf16[4,144,1536]{2,1,0:T(8,128)(2,1)}, u32[]{:S(2)}, u32[]{:S(2)}) collective-permute-start(bf16[4,144,1536]{2,1,0:T(8,128)(2,1)} %copy_after.1), channel_id=1, source_target_pairs={{0,8},{8,0},{16,24},{24,16},{1,9},{9,1},{17,25},{25,17},{2,10},{10... | collective-permute-start | bytes 5308424 | tf_op jit(solution)/shard_map/ppermute | solution.py:958
  587.8 3.8 collective-permute-start.29
  591.6 3.7 collective-permute-start.30
  595.4 3.7 collective-permute-start.31
  599.1 6.3 %collective-permute-start.32 = (f32[3080]{0:T(1024)S(1)}, f32[3080]{0:T(1024)S(1)}, u32[]{:S(2)}, u32[]{:S(2)}) collective-permute-start(f32[3080]{0:T(1024)S(1)} %add.222), channel_id=1, source_target_pairs={{0,2},{1,3},{2,0},{3,1},{4,6},{5,7},{6,4},{7,5},{8,10},{9,11},{10,... | collective-permute-start | bytes 36968 | tf_op jit(solution)/shard_map/ppermute | solution.py:958
  (38 other events, 204.5 us)
Sparse Core Ops, SparseCore 0:
  10.5 53.1 all-gather.3
  65.6 36.6 all-gather.5
  104.8 98.7 all-gather.7
  314.9 141.2 reduce-scatter.2
  473.7 76.7 reduce-scatter.4
